TPU v7x, 32 devices: a whole 2x2x4 slice. The times are simulated.
32 devices in a mesh: fsdp: 8 (over y, x, core), tensor: 4 (over z).
Axes of the slice: x: 2, y: 2, z: 4, core: 2. Of those that a mesh axis runs over, the one named last changes fastest.
Arguments:
- enc_in: bfloat16 [4096, 1024], P(('fsdp', 'tensor')), may hold values from -6 to 6
- dec_in: bfloat16 [4096, 1024], P(('fsdp', 'tensor')), may hold values from -6 to 6
- enc_cot: bfloat16 [4096, 1024], P(('fsdp', 'tensor')), may hold values from -6 to 6
- dec_cot: bfloat16 [4096, 1024], P(('fsdp', 'tensor')), may hold values from -6 to 6
- seq_lens: int32 [12], replicated, may hold values from 1 to 512, 4096 in all
- pic_start: int32 [12, 2], replicated, may hold values from 0 to 255
- pic_len: int32 [12, 2], replicated, may hold values from 1 to 256, as said below
- enc_attn_w: bfloat16 [4, 1024, 1024], P(None, 'fsdp', 'tensor')
- enc_attn_bias: bfloat16 [3, 1024], P(None, 'fsdp'), may hold values from -1.1953125 to 1.1953125
- enc_attn_norm: bfloat16 [2, 1024], P(None, 'fsdp')
- enc_ffn_w: bfloat16 [2, 1024, 4096], P(None, 'fsdp', 'tensor')
- enc_ffn_b1: bfloat16 [1, 4096], P(None, 'fsdp'), may hold values from -1.1953125 to 1.1953125
- enc_ffn_vec: bfloat16 [3, 1024], P(None, 'fsdp')
- self_attn_w: bfloat16 [4, 1024, 1024], P(None, 'fsdp', 'tensor')
- self_attn_bias: bfloat16 [3, 1024], P(None, 'fsdp'), may hold values from -1.1953125 to 1.1953125
- self_attn_norm: bfloat16 [2, 1024], P(None, 'fsdp')
- cross_attn_w: bfloat16 [4, 1024, 1024], P(None, 'fsdp', 'tensor')
- cross_attn_bias: bfloat16 [3, 1024], P(None, 'fsdp'), may hold values from -1.1953125 to 1.1953125
- cross_attn_norm: bfloat16 [2, 1024], P(None, 'fsdp')
- dec_ffn_w: bfloat16 [2, 1024, 4096], P(None, 'fsdp', 'tensor')
- dec_ffn_b1: bfloat16 [1, 4096], P(None, 'fsdp'), may hold values from -1.1953125 to 1.1953125
- dec_ffn_vec: bfloat16 [3, 1024], P(None, 'fsdp')
Outputs:
- enc_out: bfloat16 [4096, 1024], P(('fsdp', 'tensor'))
- dec_out: bfloat16 [4096, 1024], P(('fsdp', 'tensor'))
- enc_in_grad: float32 [4096, 1024], P(('fsdp', 'tensor'))
- dec_in_grad: float32 [4096, 1024], P(('fsdp', 'tensor'))
- enc_attn_w_grad: float32 [4, 1024, 1024], P(None, 'fsdp', 'tensor')
- enc_attn_bias_grad: float32 [3, 1024], P(None, 'fsdp')
- enc_attn_norm_grad: float32 [2, 1024], P(None, 'fsdp')
- enc_ffn_w_grad: float32 [2, 1024, 4096], P(None, 'fsdp', 'tensor')
- enc_ffn_b1_grad: float32 [1, 4096], P(None, 'fsdp')
- enc_ffn_vec_grad: float32 [3, 1024], P(None, 'fsdp')
- self_attn_w_grad: float32 [4, 1024, 1024], P(None, 'fsdp', 'tensor')
- self_attn_bias_grad: float32 [3, 1024], P(None, 'fsdp')
- self_attn_norm_grad: float32 [2, 1024], P(None, 'fsdp')
- cross_attn_w_grad: float32 [4, 1024, 1024], P(None, 'fsdp', 'tensor')
- cross_attn_bias_grad: float32 [3, 1024], P(None, 'fsdp')
- cross_attn_norm_grad: float32 [2, 1024], P(None, 'fsdp')
- dec_ffn_w_grad: float32 [2, 1024, 4096], P(None, 'fsdp', 'tensor')
- dec_ffn_b1_grad: float32 [1, 4096], P(None, 'fsdp')
- dec_ffn_vec_grad: float32 [3, 1024], P(None, 'fsdp')
Inputs may be any that keep to these rules, and one draw needn't show every extreme that they name: `seq_lens`: the sequences fill the stream; the longest has exactly 512 tokens. `pic_len`: some piece has exactly 256 tokens; a piece reaching past its sequence's end covers only the tokens inside it.
All inputs are finite; a program needn't handle non-finite values.
Results may differ from a plain program's by a relative error of at most 0.03.
Values may be sent and summed in bfloat16 or wider, within the bound.
No kernel may reach another device: no remote copies, remote signals or barrier semaphores. Data moves between devices by JAX's collectives and lax.ppermute only.
A program may use at most 192 MiB of HBM per device.

v0:
```python
import jax
import jax.numpy as jnp
from jax import lax
from jax.sharding import PartitionSpec as P

HD = 64


def extended(shard, sides, width):
    for axis, dim in sides:
        peers, length = (lax.axis_size(axis), shard.shape[dim])
        up = [(i, (i + 1) % peers) for i in range(peers - 1)]
        down = [(j, i) for i, j in up]
        last = lax.slice_in_dim(shard, length - width, length, axis=dim)
        first = lax.slice_in_dim(shard, 0, width, axis=dim)
        before = lax.ppermute(last, axis, up)
        after = lax.ppermute(first, axis, down)
        shard = jnp.concatenate([before, shard, after], axis=dim)
    return shard


def passed_along(shard, axis, by):
    peers = lax.axis_size(axis)
    pairs = [(i, i + by) for i in range(peers) if 0 <= i + by < peers]
    return lax.ppermute(shard, axis, pairs)


def norm_rows(residual, gain_row, shift_row):
    center = residual - jnp.mean(residual, -1, keepdims=True)
    spread = jnp.mean(center * center, -1, keepdims=True)
    return center * lax.rsqrt(spread + 1e-05) * gain_row + shift_row


def exact_gelu(before):
    return jax.nn.gelu(before, approximate=False)


def token_info(places, seq_lens, pic_start, pic_len, limit):
    starts = jnp.cumsum(seq_lens) - seq_lens
    inside = (starts[None, :] <= places[:, None]).astype(jnp.int32)
    seq_ids = jnp.sum(inside, 1) - 1
    seq_ids = jnp.where(places < limit, seq_ids, -2)
    picked = (seq_ids[:, None] == jnp.arange(seq_lens.shape[0], dtype=jnp.int32)[None, :]).astype(
        jnp.int32
    )
    offset = places - jnp.sum(picked * starts[None, :], 1)
    first_pos = jnp.sum(picked[:, :, None] * pic_start[None, :, :], 1)
    extent = jnp.sum(picked[:, :, None] * pic_len[None, :, :], 1)
    member = (offset[:, None] >= first_pos) & (offset[:, None] < first_pos + extent)
    return (places, seq_ids, member)


def visible(query_meta, key_meta, text_mask):
    allowed = query_meta[1][:, None] == key_meta[1][None, :]
    if text_mask:
        shared = key_meta[0][None, :] <= query_meta[0][:, None]
        for picture in range(query_meta[2].shape[1]):
            shared = shared | query_meta[2][:, picture][:, None] & key_meta[2][:, picture][None, :]
        allowed = allowed & shared
    return allowed


def product(left, right):
    return jnp.dot(left, right, preferred_element_type=jnp.float32)


def contract_last(left, right):
    return lax.dot_general(
        left, right, (((1,), (1,)), ((), ())), preferred_element_type=jnp.float32
    )


def contract_first(left, right):
    return lax.dot_general(
        left, right, (((0,), (0,)), ((), ())), preferred_element_type=jnp.float32
    )


def gather_rows(values):
    return lax.all_gather(values, "tensor", axis=0, tiled=True)


def sum_rows(term, row_count):
    return lax.psum_scatter(
        term(jnp.int32(0), row_count * lax.axis_size("tensor")).astype(jnp.bfloat16),
        "tensor",
        scatter_dimension=0,
        tiled=True,
    ).astype(jnp.float32)


def sum_back(term, row_count):
    return lax.psum_scatter(
        term(jnp.int32(0), row_count * lax.axis_size("tensor")).astype(jnp.bfloat16),
        "tensor",
        scatter_dimension=0,
        tiled=True,
    ).astype(jnp.float32)


def fetch(first_part, second_part, third_part):
    return (
        lax.all_gather(first_part, "fsdp", axis=1, tiled=True),
        lax.all_gather(second_part, "fsdp", axis=1, tiled=True),
        lax.all_gather(third_part, "fsdp", axis=1, tiled=True),
    )


def fetch_again(first_part, second_part, third_part):
    return (
        lax.all_gather(first_part, "fsdp", axis=1, tiled=True),
        lax.all_gather(second_part, "fsdp", axis=1, tiled=True),
        lax.all_gather(third_part, "fsdp", axis=1, tiled=True),
    )


def reduce_weights(grads):
    return lax.psum_scatter(
        grads.astype(jnp.bfloat16), "fsdp", scatter_dimension=1, tiled=True
    ).astype(jnp.float32)


def key_window(pairs, meta_for):
    token_count = pairs.shape[1]
    window = extended(pairs, (("fsdp", 1),), token_count)
    return (window, meta_for(3 * token_count))


def return_keys(grads, token_count):
    below = grads[:, :token_count]
    owned = grads[:, token_count : 2 * token_count]
    above = grads[:, 2 * token_count :]
    owned = owned + passed_along(below.astype(jnp.bfloat16), "fsdp", -1).astype(below.dtype)
    return owned + passed_along(above.astype(jnp.bfloat16), "fsdp", 1).astype(above.dtype)


def attend_forward(queries, window, query_meta, key_meta, text_mask):
    token_count, feature_count = queries.shape
    head_count = feature_count // HD
    scaling = HD ** (-0.5)
    block_rows = min(512, token_count)
    key_length = window.shape[1]
    key_heads = window[0].reshape(key_length, head_count, HD)
    value_heads = window[1].reshape(key_length, head_count, HD)
    query_heads = queries.reshape(block_rows, head_count, HD)
    allowed = visible(tuple((member for member in query_meta)), key_meta, text_mask)
    scores = (
        jnp.einsum("qhd,khd->hqk", query_heads, key_heads, preferred_element_type=jnp.float32)
        * scaling
    )
    scores = jnp.where(allowed[None], scores, -1e30)
    height = jnp.max(scores, -1, keepdims=True)
    block_total = height + jnp.log(jnp.sum(jnp.exp(scores - height), -1, keepdims=True))
    weights = jnp.exp(scores - block_total).astype(jnp.bfloat16)
    mixture = jnp.einsum("hqk,khd->qhd", weights, value_heads, preferred_element_type=jnp.float32)
    outputs = mixture.reshape(block_rows, feature_count)
    return (outputs.astype(jnp.bfloat16), block_total)


def attend_backward(queries, window, grad_mix, totals, query_meta, key_meta, text_mask):
    token_count, feature_count = queries.shape
    head_count = feature_count // HD
    scaling = HD ** (-0.5)
    block_rows = min(512, token_count)
    key_length = window.shape[1]
    key_heads = window[0].reshape(key_length, head_count, HD)
    value_heads = window[1].reshape(key_length, head_count, HD)
    query_heads = queries.reshape(block_rows, head_count, HD)
    grad_heads = grad_mix.reshape(block_rows, head_count, HD)
    allowed = visible(tuple((member for member in query_meta)), key_meta, text_mask)
    scores = (
        jnp.einsum("qhd,khd->hqk", query_heads, key_heads, preferred_element_type=jnp.float32)
        * scaling
    )
    scores = jnp.where(allowed[None], scores, -1e30)
    weights = jnp.exp(scores - totals)
    incoming = jnp.einsum(
        "qhd,khd->hqk", grad_heads, value_heads, preferred_element_type=jnp.float32
    )
    inner = jnp.sum(incoming * weights, -1, keepdims=True)
    grad_scores = (weights * (incoming - inner)).astype(jnp.bfloat16)
    block_grad = (
        jnp.einsum("hqk,khd->qhd", grad_scores, key_heads, preferred_element_type=jnp.float32)
        * scaling
    )
    query_grads = block_grad.reshape(block_rows, feature_count)
    key_grads = (
        jnp.einsum("hqk,qhd->khd", grad_scores, query_heads, preferred_element_type=jnp.float32)
        * scaling
    )
    value_grads = jnp.einsum(
        "hqk,qhd->khd", weights.astype(jnp.bfloat16), grad_heads, preferred_element_type=jnp.float32
    )
    window_grads = jnp.stack(
        [
            key_grads.reshape(key_length, feature_count),
            value_grads.reshape(key_length, feature_count),
        ]
    )
    return (query_grads.astype(jnp.bfloat16), window_grads)


def attention_forward(residual, source, parts, query_meta, meta_for, text_mask):
    projection, biases, norms = parts
    biases = biases.astype(jnp.float32)
    norms = norms.astype(jnp.float32)
    feature_count = projection.shape[2]
    column = lax.axis_index("tensor") * feature_count
    local_bias = lax.dynamic_slice_in_dim(biases, column, feature_count, 1)
    flat_in = gather_rows(residual.astype(jnp.bfloat16))
    if source is None:
        key_in = flat_in
    else:
        key_in = gather_rows(source.astype(jnp.bfloat16))
    queries = (product(flat_in, projection[0]) + local_bias[0]).astype(jnp.bfloat16)
    key_rows = product(key_in, projection[1]).astype(jnp.bfloat16)
    value_rows = (product(key_in, projection[2]) + local_bias[1]).astype(jnp.bfloat16)
    window, key_meta = key_window(jnp.stack([key_rows, value_rows]), meta_for)
    mixture, totals = attend_forward(queries, window, query_meta, key_meta, text_mask)

    def attention_branch_term(begin_row, row_count):
        return contract_last(mixture, projection[3])

    summed = residual + sum_rows(attention_branch_term, residual.shape[0]) + biases[2]
    output = norm_rows(summed, norms[0], norms[1])
    return (output, (flat_in, key_in, queries, window, key_meta, mixture, totals, summed, None))


def attention_backward(grad_out, kept, parts, query_meta, text_mask, cross):
    flat_in, key_in, queries, window, key_meta, mixture, totals, summed, extra = kept
    projection, biases, norms = parts
    norms = norms.astype(jnp.float32)
    feature_count = projection.shape[2]
    token_count = queries.shape[0]
    column = lax.axis_index("tensor") * feature_count
    unused, pull_norm = jax.vjp(norm_rows, summed, norms[0], norms[1])
    grad_sum, grad_gain, grad_shift = pull_norm(grad_out)
    grad_branch = grad_sum.astype(jnp.bfloat16)
    grad_flat = gather_rows(grad_branch)
    grad_out_proj = contract_first(grad_flat, mixture)
    grad_mix = product(grad_flat, projection[3]).astype(jnp.bfloat16)
    grad_queries, grad_window = attend_backward(
        queries, window, grad_mix, totals, query_meta, key_meta, text_mask
    )
    returned = return_keys(grad_window, token_count)
    grad_keys = returned[0].astype(jnp.bfloat16)
    grad_values = returned[1].astype(jnp.bfloat16)
    grad_proj = jnp.stack(
        [
            contract_first(flat_in, grad_queries),
            contract_first(key_in, grad_keys),
            contract_first(key_in, grad_values),
            grad_out_proj,
        ]
    )
    zeros_row = jnp.zeros((biases.shape[1],), jnp.float32)
    grad_bias = jnp.stack(
        [
            lax.dynamic_update_slice_in_dim(
                zeros_row, jnp.sum(grad_queries.astype(jnp.float32), 0), column, 0
            ),
            lax.dynamic_update_slice_in_dim(
                zeros_row, jnp.sum(grad_values.astype(jnp.float32), 0), column, 0
            ),
            jnp.sum(grad_branch.astype(jnp.float32), 0),
        ]
    )
    grad_norm = jnp.stack([grad_gain, grad_shift])
    row_total = grad_out.shape[0]
    if cross:

        def query_term(begin_row, row_count):
            return contract_last(grad_queries, projection[0])

        def source_term(begin_row, row_count):
            from_keys = contract_last(grad_keys, projection[1])
            from_values = contract_last(grad_values, projection[2])
            return from_keys + from_values

        grad_input = grad_sum + sum_back(query_term, row_total)
        grad_source = sum_back(source_term, row_total)
    else:

        def attention_input_term(begin_row, row_count):
            from_queries = contract_last(grad_queries, projection[0])
            from_keys = contract_last(grad_keys, projection[1])
            from_values = contract_last(grad_values, projection[2])
            return from_queries + from_keys + from_values

        grad_input = grad_sum + sum_back(attention_input_term, row_total)
        grad_source = None
    return (grad_input, grad_source, reduce_weights(grad_proj), grad_bias, grad_norm)


def ffn_forward(residual, parts):
    projection, first_bias, vectors = parts
    vectors = vectors.astype(jnp.float32)
    hidden_count = projection.shape[2]
    column = lax.axis_index("tensor") * hidden_count
    local_bias = lax.dynamic_slice_in_dim(
        first_bias[0].astype(jnp.float32), column, hidden_count, 0
    )
    flat_in = gather_rows(residual.astype(jnp.bfloat16))
    before = product(flat_in, projection[0]) + local_bias
    active = exact_gelu(before).astype(jnp.bfloat16)

    def ffn_branch_term(begin_row, row_count):
        return contract_last(active, projection[1])

    summed = residual + sum_rows(ffn_branch_term, residual.shape[0]) + vectors[0]
    return (norm_rows(summed, vectors[1], vectors[2]), (flat_in, before, active, summed))


def ffn_backward(grad_out, kept, parts):
    flat_in, before, active, summed = kept
    projection, first_bias, vectors = parts
    vectors = vectors.astype(jnp.float32)
    hidden_count = projection.shape[2]
    column = lax.axis_index("tensor") * hidden_count
    unused, pull_norm = jax.vjp(norm_rows, summed, vectors[1], vectors[2])
    grad_sum, grad_gain, grad_shift = pull_norm(grad_out)
    grad_branch = grad_sum.astype(jnp.bfloat16)
    grad_flat = gather_rows(grad_branch)
    grad_down = contract_first(grad_flat, active)
    grad_active = product(grad_flat, projection[1])
    unused_gelu, pull_gelu = jax.vjp(exact_gelu, before)
    grad_before = pull_gelu(grad_active)[0].astype(jnp.bfloat16)
    grad_up = contract_first(flat_in, grad_before)
    zeros_row = jnp.zeros((first_bias.shape[1],), jnp.float32)
    grad_first = lax.dynamic_update_slice_in_dim(
        zeros_row, jnp.sum(grad_before.astype(jnp.float32), 0), column, 0
    )[None]
    grad_vector = jnp.stack([jnp.sum(grad_branch.astype(jnp.float32), 0), grad_gain, grad_shift])

    def ffn_input_term(begin_row, row_count):
        return contract_last(grad_before, projection[0])

    grad_input = grad_sum + sum_back(ffn_input_term, grad_out.shape[0])
    return (grad_input, reduce_weights(jnp.stack([grad_up, grad_down])), grad_first, grad_vector)


def per_device(
    enc_in,
    dec_in,
    enc_cot,
    dec_cot,
    seq_lens,
    pic_start,
    pic_len,
    enc_attn_w,
    enc_attn_bias,
    enc_attn_norm,
    enc_ffn_w,
    enc_ffn_b1,
    enc_ffn_vec,
    self_attn_w,
    self_attn_bias,
    self_attn_norm,
    cross_attn_w,
    cross_attn_bias,
    cross_attn_norm,
    dec_ffn_w,
    dec_ffn_b1,
    dec_ffn_vec,
):
    row_total = enc_in.shape[0]
    token_count = row_total * lax.axis_size("tensor")
    offset_base = lax.axis_index("fsdp") * token_count
    stream_end = lax.axis_size("fsdp") * token_count

    def meta_for(length):
        places = offset_base - token_count + jnp.arange(length, dtype=jnp.int32)
        return token_info(places, seq_lens, pic_start, pic_len, stream_end)

    query_meta = token_info(
        offset_base + jnp.arange(token_count, dtype=jnp.int32),
        seq_lens,
        pic_start,
        pic_len,
        stream_end,
    )
    enc_attn = fetch(enc_attn_w, enc_attn_bias, enc_attn_norm)
    hidden, kept_first = attention_forward(
        enc_in.astype(jnp.float32), None, enc_attn, query_meta, meta_for, False
    )
    enc_ffn = fetch(enc_ffn_w, enc_ffn_b1, enc_ffn_vec)
    encoded, kept_second = ffn_forward(hidden, enc_ffn)
    self_attn = fetch(self_attn_w, self_attn_bias, self_attn_norm)
    decoded, kept_third = attention_forward(
        dec_in.astype(jnp.float32), None, self_attn, query_meta, meta_for, True
    )
    cross_attn = fetch(cross_attn_w, cross_attn_bias, cross_attn_norm)
    crossed, kept_fourth = attention_forward(
        decoded, encoded, cross_attn, query_meta, meta_for, False
    )
    dec_ffn = fetch(dec_ffn_w, dec_ffn_b1, dec_ffn_vec)
    final, kept_fifth = ffn_forward(crossed, dec_ffn)
    dec_ffn_back = fetch_again(dec_ffn_w, dec_ffn_b1, dec_ffn_vec)
    cross_back = fetch_again(cross_attn_w, cross_attn_bias, cross_attn_norm)
    self_back = fetch_again(self_attn_w, self_attn_bias, self_attn_norm)
    enc_ffn_back = fetch_again(enc_ffn_w, enc_ffn_b1, enc_ffn_vec)
    enc_attn_back = fetch_again(enc_attn_w, enc_attn_bias, enc_attn_norm)
    grad_crossed, dec_ffn_w_grad, dec_first_grad, dec_vector_grad = ffn_backward(
        dec_cot.astype(jnp.float32), kept_fifth, dec_ffn_back
    )
    grad_decoded, grad_encoded, cross_w_grad, cross_bias_grad, cross_norm_grad = attention_backward(
        grad_crossed, kept_fourth, cross_back, query_meta, False, True
    )
    grad_target, unused_target, self_w_grad, self_bias_grad, self_norm_grad = attention_backward(
        grad_decoded, kept_third, self_back, query_meta, True, False
    )
    grad_hidden, enc_ffn_w_grad, enc_first_grad, enc_vector_grad = ffn_backward(
        enc_cot.astype(jnp.float32) + grad_encoded, kept_second, enc_ffn_back
    )
    grad_source, unused_source, enc_w_grad, enc_bias_grad, enc_norm_grad = attention_backward(
        grad_hidden, kept_first, enc_attn_back, query_meta, False, False
    )
    summed_small = lax.psum(
        (
            enc_bias_grad,
            enc_norm_grad,
            enc_first_grad,
            enc_vector_grad,
            self_bias_grad,
            self_norm_grad,
            cross_bias_grad,
            cross_norm_grad,
            dec_first_grad,
            dec_vector_grad,
        ),
        ("fsdp", "tensor"),
    )
    piece_index = lax.axis_index("fsdp")
    piece_total = lax.axis_size("fsdp")

    def own_part(values):
        group_width = values.shape[1] // piece_total
        return lax.dynamic_slice_in_dim(values, piece_index * group_width, group_width, 1)

    return (
        encoded.astype(jnp.bfloat16),
        final.astype(jnp.bfloat16),
        grad_source,
        grad_target,
        enc_w_grad,
        own_part(summed_small[0]),
        own_part(summed_small[1]),
        enc_ffn_w_grad,
        own_part(summed_small[2]),
        own_part(summed_small[3]),
        self_w_grad,
        own_part(summed_small[4]),
        own_part(summed_small[5]),
        cross_w_grad,
        own_part(summed_small[6]),
        own_part(summed_small[7]),
        dec_ffn_w_grad,
        own_part(summed_small[8]),
        own_part(summed_small[9]),
    )


def solution(mesh):
    in_specs = (
        P(("fsdp", "tensor"), None),
        P(("fsdp", "tensor"), None),
        P(("fsdp", "tensor"), None),
        P(("fsdp", "tensor"), None),
        P(),
        P(),
        P(),
        P(None, "fsdp", "tensor"),
        P(None, "fsdp"),
        P(None, "fsdp"),
        P(None, "fsdp", "tensor"),
        P(None, "fsdp"),
        P(None, "fsdp"),
        P(None, "fsdp", "tensor"),
        P(None, "fsdp"),
        P(None, "fsdp"),
        P(None, "fsdp", "tensor"),
        P(None, "fsdp"),
        P(None, "fsdp"),
        P(None, "fsdp", "tensor"),
        P(None, "fsdp"),
        P(None, "fsdp"),
    )
    out_specs = (
        P(("fsdp", "tensor"), None),
        P(("fsdp", "tensor"), None),
        P(("fsdp", "tensor"), None),
        P(("fsdp", "tensor"), None),
        P(None, "fsdp", "tensor"),
        P(None, "fsdp"),
        P(None, "fsdp"),
        P(None, "fsdp", "tensor"),
        P(None, "fsdp"),
        P(None, "fsdp"),
        P(None, "fsdp", "tensor"),
        P(None, "fsdp"),
        P(None, "fsdp"),
        P(None, "fsdp", "tensor"),
        P(None, "fsdp"),
        P(None, "fsdp"),
        P(None, "fsdp", "tensor"),
        P(None, "fsdp"),
        P(None, "fsdp"),
    )
    return jax.shard_map(
        per_device, mesh=mesh, in_specs=in_specs, out_specs=out_specs, check_vma=False
    )
```

profile of v0, /device:TPU:0, one launch (start us, length us, event | category | flops | bytes accessed | tf_op | source)
XLA Modules:
  0.0 1303.5 jit_solution(103561756638794761)
XLA Ops:
  40.3 29.3 %all-gather.19.cloned.1.call-done = bf16[4,1024,256]{2,1,0:T(8,128)(2,1)} async-done(((bf16[4,128,256]{2,1,0:T(8,128)(2,1)}), bf16[4,1024,256]{2,1,0:T(8,128)(2,1)}) %all-gather.19.cloned.1.call-update) | async-done | bytes 2097168 | tf_op jit(solution)/shard_map/all_gather | solution.py:103
  177.7 17.8 %all-gather.23.cloned.1.call-done = bf16[2,1024,1024]{2,1,0:T(8,128)(2,1)} async-done(((bf16[2,128,1024]{2,1,0:T(8,128)(2,1)}), bf16[2,1024,1024]{2,1,0:T(8,128)(2,1)}) %all-gather.23.cloned.1.call-update) | async-done | bytes 4194320 | tf_op jit(solution)/shard_map/all_gather | solution.py:103
  195.6 30.2 %all-gather.21.cloned.1.call-done = bf16[512,1024]{1,0:T(8,128)(2,1)} async-done(((bf16[128,1024]{1,0:T(8,128)(2,1)}), bf16[512,1024]{1,0:T(8,128)(2,1)}) %all-gather.21.cloned.1.call-update) | async-done | bytes 1048592 | tf_op jit(solution)/shard_map/all_gather | solution.py:80
  274.7 17.5 %reduce-scatter.25.cloned.1.call-done = bf16[128,1024]{1,0:T(8,128)(2,1)} async-done(((bf16[512,1024]{1,0:T(8,128)(2,1)}), bf16[128,1024]{1,0:T(8,128)(2,1)}) %reduce-scatter.25.cloned.1.call-update) | async-done | bytes 262160 | tf_op jit(solution)/shard_map/reduce_scatter | solution.py:84
  320.7 30.2 %all-gather.29.cloned.1.call-done = bf16[512,1024]{1,0:T(8,128)(2,1)} async-done(((bf16[128,1024]{1,0:T(8,128)(2,1)}), bf16[512,1024]{1,0:T(8,128)(2,1)}) %all-gather.29.cloned.1.call-update) | async-done | bytes 1048592 | tf_op jit(solution)/shard_map/all_gather | solution.py:80
  358.9 21.6 %all-gather.33.cloned.1.call-done = bf16[512,1024]{1,0:T(8,128)(2,1)} async-done(((bf16[128,1024]{1,0:T(8,128)(2,1)}), bf16[512,1024]{1,0:T(8,128)(2,1)}) %all-gather.33.cloned.1.call-update) | async-done | bytes 1048592 | tf_op jit(solution)/shard_map/all_gather | solution.py:80
  418.1 17.3 %reduce-scatter.27.cloned.1.call-done = bf16[128,1024]{1,0:T(8,128)(2,1)} async-done(((bf16[512,1024]{1,0:T(8,128)(2,1)}), bf16[128,1024]{1,0:T(8,128)(2,1)}) %reduce-scatter.27.cloned.1.call-update) | async-done | bytes 262160 | tf_op jit(solution)/shard_map/reduce_scatter | solution.py:84
  446.6 25.8 %all-gather.37.cloned.1.call-done = bf16[2,1024,1024]{2,1,0:T(8,128)(2,1)} async-done(((bf16[2,128,1024]{2,1,0:T(8,128)(2,1)}), bf16[2,1024,1024]{2,1,0:T(8,128)(2,1)}) %all-gather.37.cloned.1.call-update) | async-done | bytes 4194320 | tf_op jit(solution)/shard_map/all_gather | solution.py:103
  472.5 30.0 %all-gather.35.cloned.1.call-done = bf16[512,1024]{1,0:T(8,128)(2,1)} async-done(((bf16[128,1024]{1,0:T(8,128)(2,1)}), bf16[512,1024]{1,0:T(8,128)(2,1)}) %all-gather.35.cloned.1.call-update) | async-done | bytes 1048592 | tf_op jit(solution)/shard_map/all_gather | solution.py:80
  523.3 17.9 %reduce-scatter.29.cloned.1.call-done = bf16[128,1024]{1,0:T(8,128)(2,1)} async-done(((bf16[512,1024]{1,0:T(8,128)(2,1)}), bf16[128,1024]{1,0:T(8,128)(2,1)}) %reduce-scatter.29.cloned.1.call-update) | async-done | bytes 262160 | tf_op jit(solution)/shard_map/reduce_scatter | solution.py:84
  544.9 26.7 %all-gather.39.cloned.1.call-done = bf16[512,1024]{1,0:T(8,128)(2,1)} async-done(((bf16[128,1024]{1,0:T(8,128)(2,1)}), bf16[512,1024]{1,0:T(8,128)(2,1)}) %all-gather.39.cloned.1.call-update) | async-done | bytes 1048592 | tf_op jit(solution)/shard_map/all_gather | solution.py:80
  580.7 26.7 %reduce-scatter.31.cloned.1.call-done = bf16[128,1024]{1,0:T(8,128)(2,1)} async-done(((bf16[512,1024]{1,0:T(8,128)(2,1)}), bf16[128,1024]{1,0:T(8,128)(2,1)}) %reduce-scatter.31.cloned.1.call-update) | async-done | bytes 262160 | tf_op jit(solution)/shard_map/reduce_scatter | solution.py:93
  611.4 26.5 %all-gather.41.cloned.1.call-done = bf16[512,1024]{1,0:T(8,128)(2,1)} async-done(((bf16[128,1024]{1,0:T(8,128)(2,1)}), bf16[512,1024]{1,0:T(8,128)(2,1)}) %all-gather.41.cloned.1.call-update) | async-done | bytes 1048592 | tf_op jit(solution)/shard_map/all_gather | solution.py:80
  667.9 37.0 %reduce-scatter.33.cloned.1.call-done = bf16[128,1024]{1,0:T(8,128)(2,1)} async-done(((bf16[512,1024]{1,0:T(8,128)(2,1)}), bf16[128,1024]{1,0:T(8,128)(2,1)}) %reduce-scatter.33.cloned.1.call-update) | async-done | bytes 262160 | tf_op jit(solution)/shard_map/reduce_scatter | solution.py:93
  717.0 18.8 %all-gather.43.cloned.1.call-done = bf16[512,1024]{1,0:T(8,128)(2,1)} async-done(((bf16[128,1024]{1,0:T(8,128)(2,1)}), bf16[512,1024]{1,0:T(8,128)(2,1)}) %all-gather.43.cloned.1.call-update) | async-done | bytes 1048592 | tf_op jit(solution)/shard_map/all_gather | solution.py:80
  744.3 21.1 %reduce-scatter.39.cloned.1.call-done = bf16[128,1024]{1,0:T(8,128)(2,1)} async-done(((bf16[512,1024]{1,0:T(8,128)(2,1)}), bf16[128,1024]{1,0:T(8,128)(2,1)}) %reduce-scatter.39.cloned.1.call-update) | async-done | bytes 262160 | tf_op jit(solution)/shard_map/reduce_scatter | solution.py:93
  765.4 28.7 %reduce-scatter.35.cloned.1.call-done = bf16[128,1024]{1,0:T(8,128)(2,1)} async-done(((bf16[512,1024]{1,0:T(8,128)(2,1)}), bf16[128,1024]{1,0:T(8,128)(2,1)}) %reduce-scatter.35.cloned.1.call-update) | async-done | bytes 262160 | tf_op jit(solution)/shard_map/reduce_scatter | solution.py:93
  935.5 20.2 %reduce-scatter.45.cloned.1.call-done = bf16[4,128,256]{2,1,0:T(8,128)(2,1)} async-done(((bf16[4,1024,256]{2,1,0:T(8,128)(2,1)}), bf16[4,128,256]{2,1,0:T(8,128)(2,1)}) %reduce-scatter.45.cloned.1.call-update) | async-done | bytes 262160 | tf_op jit(solution)/shard_map/reduce_scatter | solution.py:118
  957.5 133.3 %all-reduce.3.cloned.1.call-done = (f32[3,1024]{1,0:T(4,128)}, f32[2,1024]{1,0:T(2,128)}, f32[1,4096]{1,0:T(1,128)}, f32[3,1024]{1,0:T(4,128)}, f32[3,1024]{1,0:...) async-done(((f32[3,1024]{1,0:T(4,128)}, f32[2,1024]{1,0:T(2,128)}, f32[1,4096]{1,0:T(1,128)}, ...) | async-done | bytes 118800 | tf_op jit(solution)/shard_map/psum | solution.py:418
  1103.2 45.2 %reduce-scatter.43.cloned.1.call-done = bf16[2,128,1024]{2,1,0:T(8,128)(2,1)} async-done(((bf16[2,1024,1024]{2,1,0:T(8,128)(2,1)}), bf16[2,128,1024]{2,1,0:T(8,128)(2,1)}) %reduce-scatter.43.cloned.1.call-update) | async-done | bytes 524304 | tf_op jit(solution)/shard_map/reduce_scatter | solution.py:118
  1150.5 27.3 %reduce-scatter.41.cloned.1.call-done = bf16[128,1024]{1,0:T(8,128)(2,1)} async-done(((bf16[512,1024]{1,0:T(8,128)(2,1)}), bf16[128,1024]{1,0:T(8,128)(2,1)}) %reduce-scatter.41.cloned.1.call-update) | async-done | bytes 262160 | tf_op jit(solution)/shard_map/reduce_scatter | solution.py:93
  1179.7 26.3 %reduce-scatter.37.cloned.1.call-done = bf16[128,1024]{1,0:T(8,128)(2,1)} async-done(((bf16[512,1024]{1,0:T(8,128)(2,1)}), bf16[128,1024]{1,0:T(8,128)(2,1)}) %reduce-scatter.37.cloned.1.call-update) | async-done | bytes 262160 | tf_op jit(solution)/shard_map/reduce_scatter | solution.py:93
  1207.8 41.7 %reduce-scatter.51.cloned.1.call-done = bf16[128,1024]{1,0:T(8,128)(2,1)} async-done(((bf16[1024,1024]{1,0:T(8,128)(2,1)}), bf16[128,1024]{1,0:T(8,128)(2,1)}) %reduce-scatter.51.cloned.1.call-update) | async-done | bytes 262160
  1251.8 42.1 %reduce-scatter.49.cloned.1.call-done = bf16[128,1024]{1,0:T(8,128)(2,1)} async-done(((bf16[1024,1024]{1,0:T(8,128)(2,1)}), bf16[128,1024]{1,0:T(8,128)(2,1)}) %reduce-scatter.49.cloned.1.call-update) | async-done | bytes 262160
  (570 shorter events, 527.6 us)
Async XLA Ops:
  8.7 125.2 %all-gather.25.cloned.1.call-start = ((), (), s32[]{:S(2)}) async-start(), calls=%async_computation.22 | async-start | bytes 1310720 | tf_op jit(solution)/shard_map/all_gather | solution.py:80
  9.4 124.5 %all-gather.27.cloned.1.call-start = ((), (), s32[]{:S(2)}) async-start(), calls=%async_computation.23 | async-start | bytes 2359296 | tf_op jit(solution)/shard_map/all_gather | solution.py:103
  10.0 148.3 %reduce-scatter.21.cloned.1.call-start = ((), (), s32[]{:S(2)}) async-start(), calls=%async_computation.18 | async-start | bytes 1310720 | tf_op jit(solution)/shard_map/reduce_scatter | solution.py:84
  98.7 96.9 %all-gather.23.cloned.1.call-start = ((), (), s32[]{:S(2)}) async-start(), calls=%async_computation.20 | async-start | bytes 4718592 | tf_op jit(solution)/shard_map/all_gather | solution.py:103
  99.3 126.5 %all-gather.21.cloned.1.call-start = ((), (), s32[]{:S(2)}) async-start(), calls=%async_computation.19 | async-start | bytes 1310720 | tf_op jit(solution)/shard_map/all_gather | solution.py:80
  162.4 101.1 %reduce-scatter.23.cloned.1.call-start = ((), (), s32[]{:S(2)}) async-start(), calls=%async_computation.21 | async-start | bytes 1310720 | tf_op jit(solution)/shard_map/reduce_scatter | solution.py:84
  252.9 67.8 %all-gather.31.cloned.1.call-start = ((), (), s32[]{:S(2)}) async-start(), calls=%async_computation.26 | async-start | bytes 2359296 | tf_op jit(solution)/shard_map/all_gather | solution.py:103
  253.5 97.4 %all-gather.29.cloned.1.call-start = ((), (), s32[]{:S(2)}) async-start(), calls=%async_computation.25 | async-start | bytes 1310720 | tf_op jit(solution)/shard_map/all_gather | solution.py:80
  265.9 114.5 %all-gather.33.cloned.1.call-start = ((), (), s32[]{:S(2)}) async-start(), calls=%async_computation.27 | async-start | bytes 1310720 | tf_op jit(solution)/shard_map/all_gather | solution.py:80
  296.4 139.0 %reduce-scatter.27.cloned.1.call-start = ((), (), s32[]{:S(2)}) async-start(), calls=%async_computation.28 | async-start | bytes 1310720 | tf_op jit(solution)/shard_map/reduce_scatter | solution.py:84
  409.1 93.3 %all-gather.35.cloned.1.call-start = ((), (), s32[]{:S(2)}) async-start(), calls=%async_computation.29 | async-start | bytes 1310720 | tf_op jit(solution)/shard_map/all_gather | solution.py:80
  437.7 103.5 %reduce-scatter.29.cloned.1.call-start = ((), (), s32[]{:S(2)}) async-start(), calls=%async_computation.31 | async-start | bytes 1310720 | tf_op jit(solution)/shard_map/reduce_scatter | solution.py:84
  611.1 93.8 %reduce-scatter.33.cloned.1.call-start = ((), (), s32[]{:S(2)}) async-start(), calls=%async_computation.35 | async-start | bytes 1310720 | tf_op jit(solution)/shard_map/reduce_scatter | solution.py:93
  667.8 67.9 %all-gather.43.cloned.1.call-start = ((), (), s32[]{:S(2)}) async-start(), calls=%async_computation.36 | async-start | bytes 1310720 | tf_op jit(solution)/shard_map/all_gather | solution.py:80
  716.5 77.6 %reduce-scatter.35.cloned.1.call-start = ((), (), s32[]{:S(2)}) async-start(), calls=%async_computation.37 | async-start | bytes 1310720 | tf_op jit(solution)/shard_map/reduce_scatter | solution.py:93
  744.3 80.6 %all-gather.47.cloned.1.call-start = ((), (), s32[]{:S(2)}) async-start(), calls=%async_computation.41 | async-start | bytes 1310720 | tf_op jit(solution)/shard_map/all_gather | solution.py:80
  800.6 132.8 %reduce-scatter.47.cloned.1.call-start = ((), (), s32[]{:S(2)}) async-start(), calls=%async_computation.45 | async-start | bytes 4718592 | tf_op jit(solution)/shard_map/reduce_scatter | solution.py:118
  807.3 148.4 %reduce-scatter.45.cloned.1.call-start = ((), (), s32[]{:S(2)}) async-start(), calls=%async_computation.44 | async-start | bytes 2359296 | tf_op jit(solution)/shard_map/reduce_scatter | solution.py:118
  815.0 275.7 %all-reduce.3.cloned.1.call-start = ((), (), s32[]{:S(2)}) async-start(), calls=%async_computation.48 | async-start | bytes 278528 | tf_op jit(solution)/shard_map/psum | solution.py:418
  899.6 248.8 %reduce-scatter.43.cloned.1.call-start = ((), (), s32[]{:S(2)}) async-start(), calls=%async_computation.43 | async-start | bytes 4718592 | tf_op jit(solution)/shard_map/reduce_scatter | solution.py:118
  904.5 273.3 %reduce-scatter.41.cloned.1.call-start = ((), (), s32[]{:S(2)}) async-start(), calls=%async_computation.42 | async-start | bytes 1310720 | tf_op jit(solution)/shard_map/reduce_scatter | solution.py:93
  909.0 296.9 %reduce-scatter.37.cloned.1.call-start = ((), (), s32[]{:S(2)}) async-start(), calls=%async_computation.39 | async-start | bytes 1310720 | tf_op jit(solution)/shard_map/reduce_scatter | solution.py:93
  913.1 336.3 %reduce-scatter.51.cloned.1.call-start = ((), (), s32[]{:S(2)}) async-start(), calls=%async_computation.47 | async-start | bytes 2359296
  922.8 371.1 %reduce-scatter.49.cloned.1.call-start = ((), (), s32[]{:S(2)}) async-start(), calls=%async_computation.46 | async-start | bytes 2359296
  (126 other events, 2360.6 us)
Sparse Core Ops, SparseCore 0:
  9.6 30.6 all-gather.16
  42.2 27.3 all-gather.18
  71.2 27.9 all-gather.24
  100.9 27.4 all-gather.26
  131.1 27.1 reduce-scatter.20
  160.2 35.3 all-gather.22
  197.8 27.9 all-gather.20
  236.8 26.6 reduce-scatter.22
  322.9 27.9 all-gather.28
  353.0 27.4 all-gather.32
  408.7 26.6 reduce-scatter.26
  437.1 35.3 all-gather.36
  474.5 27.9 all-gather.34
  514.5 26.6 reduce-scatter.28
  667.9 36.9 reduce-scatter.32
  738.7 26.6 reduce-scatter.38
  827.1 27.5 all-gather.44
  858.2 53.0 reduce-scatter.46
  914.4 41.2 reduce-scatter.44
  964.4 126.3 all-reduce.2
  1094.1 54.2 reduce-scatter.42
  1150.6 27.1 reduce-scatter.40
  1209.6 39.8 reduce-scatter.50
  1252.6 41.2 reduce-scatter.48
  (9 shorter events, 236.3 us)
where the time goes:
time: 1310 us; the launch traced here: 1300 us
  waiting for transfers between devices  813 us (62%)
  matrix products  187 us (14%)
  blocking collectives  98.2 us (7%)
  other arithmetic  93.8 us (7%)
  local copies, waits for them, and re-layouts  65.7 us (5%)
  starting transfers between devices  29 us (2%)
  between operations  16.9 us (1%)
    all_gather x11, waiting for transfers between devices, gather_rows(): return lax.all_gather(values, 'tensor', axis=0, tiled=True)  200 us
    reduce_scatter x6, waiting for transfers between devices, sum_back(): lax.psum_scatter(term(jnp.int32(0), row_count * lax.axis_size('tensor'))....  167 us
    psum x1, waiting for transfers between devices, per_device(): lax.psum((enc_bias_grad, enc_norm_grad, enc_first_grad, enc_vector_grad,...  133 us
    all_gather x5, waiting for transfers between devices, fetch(): lax.all_gather(first_part, 'fsdp', axis=1, tiled=True)  88.4 us
    unnamed x35, waiting for transfers between devices  88.4 us
    reduce_scatter x5, waiting for transfers between devices, sum_rows(): lax.psum_scatter(term(jnp.int32(0), row_count * lax.axis_size('tensor'))....  68.8 us
    reduce_scatter x3, waiting for transfers between devices, reduce_weights(): lax.psum_scatter(grads.astype(jnp.bfloat16), 'fsdp', scatter_dimension=1,...  65.4 us
    all_gather x5, blocking collectives, fetch(): lax.all_gather(second_part, 'fsdp', axis=1, tiled=True)  54 us
  transfers between devices with their start and end apart: 45, of which 30 were waited for; matrix products, arithmetic and copies ran while one was open for 18% of the time, Pallas kernels for 0%

commit v1 on v0

v1 whole, which is shorter than its diff:
```python
import functools
import jax
import jax.numpy as jnp
from jax import lax
from jax.experimental import pallas as pl
from jax.experimental.pallas import tpu as pltpu
from jax.sharding import PartitionSpec as P

HD = 64
BF = jnp.bfloat16
F32 = jnp.float32


def bits_of(axis):
    count, bit, bits = lax.axis_size(axis), 1, []
    while bit < count:
        bits.append(bit)
        bit *= 2
    return bits


def swap(value, axis, mask):
    return lax.ppermute(value, axis, [(i, i ^ mask) for i in range(lax.axis_size(axis))])


def spread(value, axis, order):
    pieces = {0: value}
    for bit in order:
        for mask in list(pieces):
            pieces[mask | bit] = swap(pieces[mask], axis, bit)
    return [pieces[mask] for mask in sorted(pieces)]


def collect(pieces, axis, order):
    held = dict(enumerate(pieces))
    for bit in order:
        for mask in list(held):
            if mask & (2 * bit - 1):
                continue
            came = swap(held.pop(mask | bit).astype(BF), axis, bit).astype(F32)
            held[mask] = held[mask].astype(F32) + came
    return held[0]


def plane_orders():
    bits = bits_of("fsdp")
    return bits[1:] + bits[:1], bits[1:][::-1] + bits[:1]


def placed(pieces, index):
    lead = pieces[0].shape[0]
    rest = pieces[0].shape[1:]
    count = len(pieces)

    def kernel(index_ref, *refs):
        ins, out, sems = refs[:count], refs[count], refs[count + 1]
        copies = []
        for mask in range(count):
            copy = pltpu.make_async_copy(
                ins[mask], out.at[:, index_ref[0] ^ mask], sems.at[mask]
            )
            copy.start()
            copies.append(copy)
        for copy in copies:
            copy.wait()

    size = lead * count
    for extent in rest:
        size *= extent
    return pl.pallas_call(
        kernel,
        out_shape=jax.ShapeDtypeStruct((lead, count) + rest, pieces[0].dtype),
        in_specs=[pl.BlockSpec(memory_space=pltpu.SMEM)]
        + [pl.BlockSpec(memory_space=pl.ANY)] * count,
        out_specs=pl.BlockSpec(memory_space=pltpu.VMEM),
        scratch_shapes=[pltpu.SemaphoreType.DMA((count,))],
        compiler_params=pltpu.CompilerParams(vmem_limit_bytes=16 * 2**20),
        cost_estimate=pl.CostEstimate(flops=0, bytes_accessed=4 * size, transcendentals=0),
        name="placed",
    )(index[None], *pieces)


def gather_plane(shard, order):
    pieces = spread(shard, "fsdp", order)
    whole = placed(pieces, lax.axis_index("fsdp"))
    return whole.reshape(shard.shape[0], -1, shard.shape[2])


def fold(value, axis, order, at):
    index = lax.axis_index(axis)
    live = bits_of(axis)[::-1]
    for bit in order:
        dim = at + live.index(bit)
        live.remove(bit)
        mine = (index // bit) % 2
        keep = lax.dynamic_index_in_dim(value, mine, dim, False)
        send = lax.dynamic_index_in_dim(value, 1 - mine, dim, False)
        came = swap(send.astype(BF), axis, bit)
        value = keep.astype(F32) + came.astype(F32)
        if live:
            value = value.astype(BF)
    return value


def fold_plane(grads, first):
    bits = bits_of("fsdp")
    order = bits[:1] + (bits[1:] if first else bits[1:][::-1])
    count = lax.axis_size("fsdp")
    rows = grads.shape[1] // count
    split = grads.reshape((grads.shape[0],) + (2,) * len(bits) + (rows, grads.shape[2]))
    return fold(split, "fsdp", order, 1)


def product(left, right):
    return jnp.dot(left, right, preferred_element_type=F32)


def contract_last(left, right):
    return lax.dot_general(left, right, (((1,), (1,)), ((), ())), preferred_element_type=F32)


def contract_first(left, right):
    return lax.dot_general(left, right, (((0,), (0,)), ((), ())), preferred_element_type=F32)


def norm_rows(residual, gain_row, shift_row):
    center = residual - jnp.mean(residual, -1, keepdims=True)
    spread_ = jnp.mean(center * center, -1, keepdims=True)
    return center * lax.rsqrt(spread_ + 1e-05) * gain_row + shift_row


def norm_back(grad, summed, gain_row):
    center = summed - jnp.mean(summed, -1, keepdims=True)
    scale = lax.rsqrt(jnp.mean(center * center, -1, keepdims=True) + 1e-05)
    unit = center * scale
    inner = grad * gain_row
    grad_sum = scale * (
        inner
        - jnp.mean(inner, -1, keepdims=True)
        - unit * jnp.mean(inner * unit, -1, keepdims=True)
    )
    low = grad_sum.astype(BF)
    sums = jnp.stack(
        [jnp.sum(low.astype(F32), 0), jnp.sum(grad * unit, 0), jnp.sum(grad, 0)]
    )
    return grad_sum, low, sums


def exact_gelu(before):
    return jax.nn.gelu(before, approximate=False)


def token_ranges(places, seq_lens, pic_start, pic_len):
    count = seq_lens.shape[0]
    index = jnp.arange(count, dtype=jnp.int32)
    starts = jnp.sum(jnp.where(index[None, :] < index[:, None], seq_lens[None, :], 0), 1)
    stops = starts + seq_lens
    picked = (starts[None, :] <= places[:, None]) & (places[:, None] < stops[None, :])

    def take(values):
        return jnp.sum(jnp.where(picked, values[None, :], 0), 1)

    start, stop = take(starts), take(stops)
    ranges = []
    for k in range(pic_start.shape[1]):
        low = starts + pic_start[:, k]
        high = jnp.minimum(low + pic_len[:, k], stops)
        low, high = take(low), take(high)
        inside = (places >= low) & (places < high)
        ranges += [jnp.where(inside, low, 0), jnp.where(inside, high, 0)]
    return start, stop, ranges


def attend_forward(queries, window, allowed):
    token_count, feature_count = queries.shape
    head_count = feature_count // HD
    scaling = HD ** (-0.5)
    key_length = window.shape[1]
    key_heads = window[0].reshape(key_length, head_count, HD)
    value_heads = window[1].reshape(key_length, head_count, HD)
    query_heads = queries.reshape(token_count, head_count, HD)
    scores = (
        jnp.einsum("qhd,khd->hqk", query_heads, key_heads, preferred_element_type=F32) * scaling
    )
    scores = jnp.where(allowed[None], scores, -1e30)
    height = jnp.max(scores, -1, keepdims=True)
    block_total = height + jnp.log(jnp.sum(jnp.exp(scores - height), -1, keepdims=True))
    weights = jnp.exp(scores - block_total).astype(BF)
    mixture = jnp.einsum("hqk,khd->qhd", weights, value_heads, preferred_element_type=F32)
    return mixture.reshape(token_count, feature_count).astype(BF), block_total


def attend_backward(queries, window, grad_mix, totals, allowed):
    token_count, feature_count = queries.shape
    head_count = feature_count // HD
    scaling = HD ** (-0.5)
    key_length = window.shape[1]
    key_heads = window[0].reshape(key_length, head_count, HD)
    value_heads = window[1].reshape(key_length, head_count, HD)
    query_heads = queries.reshape(token_count, head_count, HD)
    grad_heads = grad_mix.reshape(token_count, head_count, HD)
    scores = (
        jnp.einsum("qhd,khd->hqk", query_heads, key_heads, preferred_element_type=F32) * scaling
    )
    scores = jnp.where(allowed[None], scores, -1e30)
    weights = jnp.exp(scores - totals)
    incoming = jnp.einsum("qhd,khd->hqk", grad_heads, value_heads, preferred_element_type=F32)
    inner = jnp.sum(incoming * weights, -1, keepdims=True)
    grad_scores = (weights * (incoming - inner)).astype(BF)
    block_grad = (
        jnp.einsum("hqk,khd->qhd", grad_scores, key_heads, preferred_element_type=F32) * scaling
    )
    query_grads = block_grad.reshape(token_count, feature_count)
    key_grads = (
        jnp.einsum("hqk,qhd->khd", grad_scores, query_heads, preferred_element_type=F32) * scaling
    )
    value_grads = jnp.einsum(
        "hqk,qhd->khd", weights.astype(BF), grad_heads, preferred_element_type=F32
    )
    window_grads = jnp.stack(
        [
            key_grads.reshape(key_length, feature_count),
            value_grads.reshape(key_length, feature_count),
        ]
    )
    return query_grads.astype(BF), window_grads


def halo(pair):
    peers = lax.axis_size("fsdp")
    up = [(i, i + 1) for i in range(peers - 1)]
    down = [(j, i) for i, j in up]
    before = lax.ppermute(pair, "fsdp", up)
    after = lax.ppermute(pair, "fsdp", down)
    return jnp.concatenate([before, pair, after], 1)


def return_keys(grads, token_count):
    peers = lax.axis_size("fsdp")
    up = [(i, i + 1) for i in range(peers - 1)]
    down = [(j, i) for i, j in up]
    below = grads[:, :token_count].astype(BF)
    owned = grads[:, token_count : 2 * token_count]
    above = grads[:, 2 * token_count :].astype(BF)
    below = lax.ppermute(below, "fsdp", down)
    above = lax.ppermute(above, "fsdp", up)
    return (owned + below.astype(F32) + above.astype(F32)).astype(BF)


def per_device(
    enc_in,
    dec_in,
    enc_cot,
    dec_cot,
    seq_lens,
    pic_start,
    pic_len,
    enc_attn_w,
    enc_attn_bias,
    enc_attn_norm,
    enc_ffn_w,
    enc_ffn_b1,
    enc_ffn_vec,
    self_attn_w,
    self_attn_bias,
    self_attn_norm,
    cross_attn_w,
    cross_attn_bias,
    cross_attn_norm,
    dec_ffn_w,
    dec_ffn_b1,
    dec_ffn_vec,
):
    rows = enc_in.shape[0]
    tensor_size = lax.axis_size("tensor")
    fsdp_size = lax.axis_size("fsdp")
    t_index = lax.axis_index("tensor")
    f_index = lax.axis_index("fsdp")
    tokens = rows * tensor_size
    features = enc_attn_w.shape[2]
    hidden = enc_ffn_w.shape[2]
    t_down = bits_of("tensor")[::-1]
    t_up = bits_of("tensor")
    wide_down = t_down[:-1]
    wide_up = t_up[1:]
    t_masks = range(tensor_size)
    wide_masks = range(0, tensor_size, 2)

    small = [
        enc_attn_bias, enc_attn_norm, enc_ffn_b1, enc_ffn_vec, self_attn_bias, self_attn_norm,
        cross_attn_bias, cross_attn_norm, dec_ffn_b1, dec_ffn_vec,
    ]
    widths = [item.size for item in small]
    packed = jnp.concatenate([item.reshape(-1) for item in small])
    everything = lax.all_gather(packed, "fsdp", axis=0).astype(F32)
    vectors, begin = [], 0
    for item, width in zip(small, widths):
        part = everything[:, begin : begin + width].reshape((fsdp_size,) + item.shape)
        vectors.append(jnp.moveaxis(part, 0, 1).reshape(item.shape[0], -1))
        begin += width
    (
        enc_bias, enc_norm, enc_b1, enc_vec, self_bias, self_norm,
        cross_bias, cross_norm, dec_b1, dec_vec,
    ) = vectors

    def local(row, width, mask=0):
        return lax.dynamic_slice_in_dim(row, (t_index ^ mask) * width, width, 0)

    def rows_at(values, mask):
        return lax.dynamic_slice_in_dim(values, (t_index ^ mask) * rows, rows, 0)

    base = f_index * tokens
    places = base + jnp.arange(tokens, dtype=jnp.int32)
    start, stop, pieces = token_ranges(places, seq_lens, pic_start, pic_len)
    keys = (base - tokens + jnp.arange(3 * tokens, dtype=jnp.int32))[None, :]
    both_mask = (keys >= start[:, None]) & (keys < stop[:, None])
    text_mask = (keys >= start[:, None]) & (keys <= places[:, None])
    for k in range(len(pieces) // 2):
        text_mask = text_mask | (
            (keys >= pieces[2 * k][:, None]) & (keys < pieces[2 * k + 1][:, None])
        )

    first_order, second_order = plane_orders()

    def tensor_pieces(shard):
        return jnp.stack(spread(shard, "tensor", t_down))

    def att_weights(shard):
        qkv = gather_plane(shard[:3], first_order)
        out = gather_plane(tensor_pieces(shard[3]), second_order)
        return qkv, out

    def cross_weights(shard):
        kv_out = gather_plane(
            jnp.concatenate([shard[1:3], tensor_pieces(shard[3])]), first_order
        )
        query = gather_plane(tensor_pieces(shard[0]), second_order)
        return kv_out[:2], kv_out[2:], query

    def ffn_weights(shard):
        wide = spread(shard, "tensor", wide_down)
        wide = [jnp.concatenate([piece[k] for piece in wide], 1)[None] for k in range(2)]
        return gather_plane(wide[0], first_order)[0], gather_plane(wide[1], second_order)[0]

    def later(value, ready):
        return lax.optimization_barrier((value, ready))[0]

    enc_qkv, enc_out_w = att_weights(enc_attn_w)
    enc_up, enc_down = ffn_weights(later(enc_ffn_w, enc_qkv))
    self_qkv, self_out_w = att_weights(later(self_attn_w, enc_up))
    cross_kv, cross_out_w, cross_query = cross_weights(later(cross_attn_w, self_qkv))
    dec_up, dec_down = ffn_weights(later(dec_ffn_w, cross_kv))

    def gather_rows(low):
        pieces_ = spread(low, "tensor", t_down)
        return placed([piece[None] for piece in pieces_], t_index).reshape(tokens, -1)

    def to_rows(values):
        return [rows_at(values, 0)] + [
            swap(rows_at(values, mask), "tensor", mask) for mask in t_masks[1:]
        ]

    def to_heads(pieces_):
        came = [pieces_[0]] + [swap(pieces_[mask], "tensor", mask) for mask in t_masks[1:]]
        return placed([piece[None] for piece in came], t_index).reshape(tokens, features)

    def out_projection(mixed, weight, residual, bias, norms):
        total = residual + bias[2]
        for mask in t_masks:
            total = total + contract_last(mixed[mask], weight[mask])
        return total, norm_rows(total, norms[0], norms[1])

    def self_forward(residual, low, weights, out_w, bias, norms, allowed):
        flat = gather_rows(low)
        queries = (product(flat, weights[0]) + local(bias[0], features)).astype(BF)
        key_rows = product(flat, weights[1]).astype(BF)
        value_rows = (product(flat, weights[2]) + local(bias[1], features)).astype(BF)
        window = halo(jnp.stack([key_rows, value_rows]))
        mixture, totals = attend_forward(queries, window, allowed)
        mixed = to_rows(mixture)
        summed, out = out_projection(mixed, out_w, residual, bias, norms)
        return out, (flat, queries, window, totals, mixed, summed)

    def cross_forward(residual, low, source_low, kv_w, out_w, query_w, bias, norms, allowed):
        flat = gather_rows(source_low)
        asked = [
            (product(low, query_w[mask]) + local(bias[0], features, mask)).astype(BF)
            for mask in t_masks
        ]
        queries = to_heads(asked)
        key_rows = product(flat, kv_w[0]).astype(BF)
        value_rows = (product(flat, kv_w[1]) + local(bias[1], features)).astype(BF)
        window = halo(jnp.stack([key_rows, value_rows]))
        mixture, totals = attend_forward(queries, window, allowed)
        mixed = to_rows(mixture)
        summed, out = out_projection(mixed, out_w, residual, bias, norms)
        return out, (flat, low, queries, window, totals, mixed, summed)

    def ffn_forward(residual, low, up, down, first, vec):
        pair = jnp.concatenate([low, swap(low, "tensor", 1)], 0)
        row = jnp.concatenate([local(first[0], hidden, mask) for mask in wide_masks])
        before = product(pair, up) + row
        active = exact_gelu(before).astype(BF)
        term = contract_last(active, down)
        summed = residual + vec[0] + term[:rows] + swap(term[rows:].astype(BF), "tensor", 1)
        return norm_rows(summed, vec[1], vec[2]), (pair, before, active, summed)

    def ffn_backward(grad_out, kept, up, down, vec):
        pair, before, active, summed = kept
        grad_sum, low, sums = norm_back(grad_out, summed, vec[1])
        grad_pair = jnp.concatenate([low, swap(low, "tensor", 1)], 0)
        grad_active = product(grad_pair, down)
        unused, pull = jax.vjp(exact_gelu, before)
        grad_before = pull(grad_active)[0].astype(BF)
        term = contract_last(grad_before, up)
        grad_in = grad_sum + term[:rows] + swap(term[rows:].astype(BF), "tensor", 1)
        grad_up = contract_first(pair, grad_before).astype(BF)
        grad_down = contract_first(grad_pair, active).astype(BF)
        first_sum = jnp.sum(grad_before.astype(F32), 0)
        return grad_in, (grad_up, grad_down), first_sum, sums

    def ffn_weight_grad(pair):
        done = []
        for k in range(2):
            own = fold_plane(pair[k][None], k == 0)[0]
            parts = [
                own[:, j * hidden : (j + 1) * hidden] for j in range(len(wide_masks))
            ]
            done.append(collect_wide(parts))
        return jnp.stack(done)

    def collect_wide(parts):
        held = {2 * j: part for j, part in enumerate(parts)}
        for bit in wide_up:
            for mask in list(held):
                if mask & (2 * bit - 1):
                    continue
                came = swap(held.pop(mask | bit).astype(BF), "tensor", bit).astype(F32)
                held[mask] = held[mask] + came
        return held[0]

    def out_grads(low, mixed):
        return jnp.stack([contract_first(low, piece).astype(BF) for piece in mixed])

    def att_core_back(grad_out, kept, out_w, norms, allowed):
        queries, window, totals, mixed, summed = kept
        grad_sum, low, sums = norm_back(grad_out, summed, norms[0])
        grad_mixed = [product(low, out_w[mask]).astype(BF) for mask in t_masks]
        grad_mix = to_heads(grad_mixed)
        grad_queries, grad_window = attend_backward(queries, window, grad_mix, totals, allowed)
        returned = return_keys(grad_window, tokens)
        return grad_sum, low, sums, grad_queries, returned[0], returned[1]

    def share(terms):
        blocks = []
        for mask in t_masks:
            total = 0.0
            for left, right in terms:
                total = total + contract_last(rows_at(left, mask), right)
            blocks.append(total)
        return collect(blocks, "tensor", t_up)

    def self_backward(grad_out, kept, weights, out_w, norms, allowed):
        flat, queries, window, totals, mixed, summed = kept
        grad_sum, low, sums, dq, dk, dv = att_core_back(
            grad_out, (queries, window, totals, mixed, summed), out_w, norms, allowed
        )
        grad_in = grad_sum + share([(dq, weights[0]), (dk, weights[1]), (dv, weights[2])])
        grad_w = jnp.stack([contract_first(flat, g).astype(BF) for g in (dq, dk, dv)])
        return grad_in, grad_w, out_grads(low, mixed), (sums, dq, dv)

    def cross_backward(grad_out, kept, kv_w, out_w, query_w, norms, allowed):
        flat, low_in, queries, window, totals, mixed, summed = kept
        grad_sum, low, sums, dq, dk, dv = att_core_back(
            grad_out, (queries, window, totals, mixed, summed), out_w, norms, allowed
        )
        grad_source = share([(dk, kv_w[0]), (dv, kv_w[1])])
        asked = to_rows(dq)
        grad_in = grad_sum
        for mask in t_masks:
            grad_in = grad_in + contract_last(asked[mask], query_w[mask])
        grad_kv = jnp.stack([contract_first(flat, g).astype(BF) for g in (dk, dv)])
        grad_query = jnp.stack([contract_first(low_in, piece).astype(BF) for piece in asked])
        return grad_in, grad_source, grad_kv, out_grads(low, mixed), grad_query, (sums, dq, dv)

    def tensor_sum(parts):
        return collect([parts[mask] for mask in t_masks], "tensor", t_up)

    def att_weight_grad(grad_w, grad_o):
        own = fold_plane(grad_w, True)
        out = tensor_sum(fold_plane(grad_o, False))
        return jnp.concatenate([own, out[None]])

    def cross_weight_grad(grad_kv, grad_o, grad_q):
        first = fold_plane(jnp.concatenate([grad_kv, grad_o]), True)
        out = tensor_sum(first[2:])
        query = tensor_sum(fold_plane(grad_q, False))
        return jnp.concatenate([query[None], first[:2], out[None]])

    enc_rows = enc_in.astype(F32)
    dec_rows = dec_in.astype(F32)
    hid, kept_enc = self_forward(
        enc_rows, enc_in, enc_qkv, enc_out_w, enc_bias, enc_norm, both_mask
    )
    encoded, kept_enc_ffn = ffn_forward(hid, hid.astype(BF), enc_up, enc_down, enc_b1, enc_vec)
    encoded_low = encoded.astype(BF)
    decoded, kept_self = self_forward(
        dec_rows, dec_in, self_qkv, self_out_w, self_bias, self_norm, text_mask
    )
    crossed, kept_cross = cross_forward(
        decoded, decoded.astype(BF), encoded_low, cross_kv, cross_out_w, cross_query,
        cross_bias, cross_norm, both_mask,
    )
    final, kept_dec_ffn = ffn_forward(
        crossed, crossed.astype(BF), dec_up, dec_down, dec_b1, dec_vec
    )

    grad_crossed, dec_pair, dec_first_sum, dec_sums = ffn_backward(
        dec_cot.astype(F32), kept_dec_ffn, dec_up, dec_down, dec_vec
    )
    dec_ffn_grad = ffn_weight_grad(dec_pair)
    grad_decoded, grad_encoded, cross_kv_g, cross_o_g, cross_q_g, cross_small = cross_backward(
        grad_crossed, kept_cross, cross_kv, cross_out_w, cross_query, cross_norm, both_mask
    )
    cross_grad = cross_weight_grad(cross_kv_g, cross_o_g, cross_q_g)
    grad_target, self_g, self_o_g, self_small = self_backward(
        grad_decoded, kept_self, self_qkv, self_out_w, self_norm, text_mask
    )
    self_grad = att_weight_grad(self_g, self_o_g)
    grad_hid, enc_pair, enc_first_sum, enc_sums = ffn_backward(
        enc_cot.astype(F32) + grad_encoded, kept_enc_ffn, enc_up, enc_down, enc_vec
    )
    enc_ffn_grad = ffn_weight_grad(enc_pair)
    grad_source, enc_g, enc_o_g, enc_small = self_backward(
        grad_hid, kept_enc, enc_qkv, enc_out_w, enc_norm, both_mask
    )
    enc_grad = att_weight_grad(enc_g, enc_o_g)

    def at_own(values, width, mask, length):
        return lax.dynamic_update_slice_in_dim(
            jnp.zeros((length,), F32), values, (t_index ^ mask) * width, 0
        )

    def att_small(parts):
        sums, dq, dv = parts
        width = sums.shape[1]
        query = at_own(jnp.sum(dq.astype(F32), 0), features, 0, width)
        value = at_own(jnp.sum(dv.astype(F32), 0), features, 0, width)
        return jnp.stack([query, value, sums[0]]), sums[1:]

    def ffn_small(first_sum, sums):
        length = hidden * tensor_size
        row = jnp.zeros((length,), F32)
        for j, mask in enumerate(wide_masks):
            part = first_sum[j * hidden : (j + 1) * hidden]
            row = lax.dynamic_update_slice_in_dim(row, part, (t_index ^ mask) * hidden, 0)
        return row[None], sums

    def reduce_small(items):
        flat = jnp.concatenate(
            [
                jnp.moveaxis(item.reshape(item.shape[0], fsdp_size, -1), 1, 0).reshape(
                    fsdp_size, -1
                )
                for item in items
            ],
            1,
        )
        bits = bits_of("fsdp")
        index = f_index
        live = flat
        for bit in bits[::-1]:
            half = live.shape[0] // 2
            mine = (index // bit) % 2
            keep = lax.dynamic_slice_in_dim(live, mine * half, half, 0)
            send = lax.dynamic_slice_in_dim(live, (1 - mine) * half, half, 0)
            live = keep + swap(send, "fsdp", bit)
        live = live[0]
        for bit in t_up:
            live = live + swap(live, "tensor", bit)
        out, begin_ = [], 0
        for item in items:
            width = item.size // fsdp_size
            out.append(live[begin_ : begin_ + width].reshape(item.shape[0], -1))
            begin_ += width
        return out

    dec_small = ffn_small(dec_first_sum, dec_sums)
    enc_f_small = ffn_small(enc_first_sum, enc_sums)
    early = reduce_small(
        [*att_small(self_small), *att_small(cross_small), *dec_small, *enc_f_small]
    )
    late = reduce_small([*att_small(enc_small)])

    return (
        encoded_low,
        final.astype(BF),
        grad_source,
        grad_target,
        enc_grad,
        late[0],
        late[1],
        enc_ffn_grad,
        early[6],
        early[7],
        self_grad,
        early[0],
        early[1],
        cross_grad,
        early[2],
        early[3],
        dec_ffn_grad,
        early[4],
        early[5],
    )


def solution(mesh):
    rows = P(("fsdp", "tensor"), None)
    weight = P(None, "fsdp", "tensor")
    vector = P(None, "fsdp")
    att, ffn = (weight, vector, vector), (weight, vector, vector)
    in_specs = (rows,) * 4 + (P(),) * 3 + (att + ffn + att + att + ffn)
    out_specs = (rows,) * 4 + (att + ffn + att + att + ffn)
    return jax.shard_map(
        per_device, mesh=mesh, in_specs=in_specs, out_specs=out_specs, check_vma=False
    )
```

time: 1310 us -> 995 us (0.76)
  waiting for transfers between devices: 813 us -> 378 us
  starting transfers between devices: 29 us -> 228 us
  blocking collectives: 98.2 us -> 9.25 us
  local copies, waits for them, and re-layouts: 65.7 us -> 90.8 us
    ppermute x12 -> x202, waiting for transfers between devices: 1.51 us -> 378 us  [the longest x190 378 us: swap(): lax.ppermute(value, axis, [(i, i ^ mask) for i in range(lax.axis_size(axi...]
    reduce_scatter x14 -> x0, waiting for transfers between devices: 301 us -> none  [the longest x6 167 us: sum_back(): lax.psum_scatter(term(jnp.int32(0), row_count * lax.axis_size('tensor'))....]
    all_gather x16 -> x0, waiting for transfers between devices: 289 us -> none  [the longest x11 200 us: gather_rows(): return lax.all_gather(values, 'tensor', axis=0, tiled=True)]
    ppermute x12 -> x202, starting transfers between devices: 26.6 us -> 228 us  [the longest x190 205 us: swap(): lax.ppermute(value, axis, [(i, i ^ mask) for i in range(lax.axis_size(axi...]
    psum x1 -> x0, waiting for transfers between devices: 133 us -> none  [per_device(): lax.psum((enc_bias_grad, enc_norm_grad, enc_first_grad, enc_vector_grad,...]
    all_gather x10 -> x1, blocking collectives: 98.2 us -> 9.25 us  [per_device(): everything = lax.all_gather(packed, 'fsdp', axis=0).astype(F32)]
    unnamed x35 -> x0, waiting for transfers between devices: 88.4 us -> none
    convert_element_type x17 -> x34, other arithmetic: 25.7 us -> 44.5 us  [the longest x3 23.4 us: attend_backward(): grad_scores = (weights * (incoming - inner)).astype(BF)]
  transfers between devices with their start and end apart: 45 -> 202, of which waited for: 30 -> 77; matrix products, arithmetic and copies ran while one was open for 18% -> 32% of each run, Pallas kernels for 0% -> 1%
where the time goes in v1:
time: 995 us; the launch traced here: 987 us
  waiting for transfers between devices  378 us (38%)
  starting transfers between devices  228 us (23%)
  matrix products  175 us (18%)
  local copies, waits for them, and re-layouts  90.8 us (9%)
  other arithmetic  89.8 us (9%)
    ppermute x190, waiting for transfers between devices, swap(): lax.ppermute(value, axis, [(i, i ^ mask) for i in range(lax.axis_size(axi...  378 us
    ppermute x190, starting transfers between devices, swap(): lax.ppermute(value, axis, [(i, i ^ mask) for i in range(lax.axis_size(axi...  205 us
    dot_general x28, matrix products, product(): return jnp.dot(left, right, preferred_element_type=F32)  32.5 us
    dot_general x52, matrix products, contract_last(): lax.dot_general(left, right, (((1,), (1,)), ((), ())), preferred_element_...  28 us
    dot_general x3, matrix products, attend_backward(): jnp.einsum('qhd,khd->hqk', grad_heads, value_heads, preferred_element_typ...  27.9 us
    unnamed x527, local copies, waits for them, and re-layouts  26.9 us
    dot_general x3, matrix products, attend_forward(): jnp.einsum('hqk,khd->qhd', weights, value_heads, preferred_element_type=F32)  24.2 us
    convert_element_type x3, other arithmetic, attend_backward(): grad_scores = (weights * (incoming - inner)).astype(BF)  23.4 us
  transfers between devices with their start and end apart: 202, of which 77 were waited for; matrix products, arithmetic and copies ran while one was open for 32% of the time, Pallas kernels for 1%

profile of v1, /device:TPU:0, one launch (start us, length us, event | category | flops | bytes accessed | tf_op | source)
XLA Modules:
  0.0 986.8 jit_solution(3219338829071437979)
XLA Ops:
  20.3 9.2 all-gather.1
  45.3 23.5 %collective-permute-done.71 = bf16[128,256]{1,0:T(8,128)(2,1)S(1)} collective-permute-done((bf16[128,256]{1,0:T(8,128)(2,1)S(1)}, bf16[128,256]{1,0:T(8,128)(2,1)S(1)}, u32[]{:S(2)}, u32[]{:S(2)}) %collective-permute-start.71) | collective-permute-done | bytes 65568 | tf_op jit(solution)/shard_map/ppermute | solution.py:23
  135.0 8.2 convolution_convert_fusion.32
  152.9 21.1 %collective-permute-done.23 = bf16[128,256]{0,1:T(8,128)(2,1)S(1)} collective-permute-done((bf16[128,256]{0,1:T(8,128)(2,1)S(1)}, bf16[128,256]{0,1:T(8,128)(2,1)S(1)}, u32[]{:S(2)}, u32[]{:S(2)}) %collective-permute-start.23) | collective-permute-done | bytes 65568 | tf_op jit(solution)/shard_map/ppermute | solution.py:23
  191.6 11.2 %collective-permute-done.32.refs_6_ = bf16[1,128,2048]{2,1,0:T(8,128)(2,1)S(1)} collective-permute-done((bf16[1,128,2048]{2,1,0:T(8,128)(2,1)S(1)}, bf16[1,128,2048]{2,1,0:T(8,128)(2,1)S(1)}, u32[]{:S(2)}, u32[]{:S(2)}) %collective-permute-start.32) | collective-permute-done | bytes 524320 | tf_op jit(solution)/shard_map/ppermute | solution.py:23
  204.0 8.2 collective-permute-done.37.refs_4_
  220.1 17.0 %collective-permute-done.74.refs_2_ = bf16[6,128,256]{2,1,0:T(8,128)(2,1)S(1)} collective-permute-done((bf16[6,128,256]{2,1,0:T(8,128)(2,1)S(1)}, bf16[6,128,256]{2,1,0:T(8,128)(2,1)S(1)}, u32[]{:S(2)}, u32[]{:S(2)}) %collective-permute-start.74) | collective-permute-done | bytes 393248 | tf_op jit(solution)/shard_map/ppermute | solution.py:23
  239.3 7.7 multiply_convert_fusion.4
  314.6 8.0 convolution_convert_fusion.30
  364.0 8.0 convolution_convert_fusion.28
  419.1 7.6 multiply_convert_fusion.3
  487.9 10.2 %multiply_reduce_fusion.2 = (f32[4,512]{1,0:T(4,128)S(1)}, f32[4,512,1536]{2,1,0:T(8,128)}) fusion(f32[4,512,1536]{2,1,0:T(8,128)} %copy-done.18, f32[4,512]{1,0:T(4,128)S(1)} %copy-done.180, pred[512,1536]{1,0:T(8,128)(4,1)S(1)} %copy-done.20, bf16[512,4,64]{0,2,1:T(8,128)(2,1)S(1)} %reshape_reshape.14, bf16[1536,4,64]{0,2,1:T(8,128)(2,1)S(1)} %bitcast.1110), kind=kOutput, calls=%fused_computation.5 | convolution fusion | flops 418379776 | bytes 27017216 | tf_op jit(solution)/shard_map/qhd,khd->hqk/dot_general | solution.py:207
  498.1 9.6 multiply_convert_fusion.2
  548.3 10.4 %multiply_reduce_fusion = (f32[4,512]{1,0:T(4,128)S(1)}, f32[4,512,1536]{2,1,0:T(8,128)}) fusion(f32[4,512,1536]{2,1,0:T(8,128)} %copy-done.17, f32[4,512]{1,0:T(4,128)S(1)} %log_add_fusion.1, pred[512,1536]{1,0:T(8,128)(4,1)S(1)} %copy-done.27, bf16[512,4,64]{0,2,1:T(8,128)(2,1)S(1)} %reshape_reshape.16, bf16[1536,4,64]{0,2,1:T(8,128)(2,1)} %bitcast.1108), kind=kOutput, calls=%fused_computation.1 | convolution fusion | flops 418379776 | bytes 27017216 | tf_op jit(solution)/shard_map/qhd,khd->hqk/dot_general | solution.py:207
  558.7 7.7 fusion.325
  608.3 8.6 collective-permute-done.144
  618.7 12.8 %collective-permute-done.124 = bf16[128,1024]{1,0:T(8,128)(2,1)S(1)} collective-permute-done((bf16[128,1024]{1,0:T(8,128)(2,1)S(1)}, bf16[128,1024]{1,0:T(8,128)(2,1)S(1)}, u32[]{:S(2)}, u32[]{:S(2)}) %collective-permute-start.124) | collective-permute-done | bytes 262176 | tf_op jit(solution)/shard_map/ppermute | solution.py:23
  792.4 8.4 collective-permute-start.155
  801.8 13.0 %collective-permute-done.155 = f32[4,640]{1,0:T(4,128)S(1)} collective-permute-done((f32[4,640]{1,0:T(4,128)S(1)}, f32[4,640]{1,0:T(4,128)S(1)}, u32[]{:S(2)}, u32[]{:S(2)}) %collective-permute-start.155) | collective-permute-done | bytes 10272 | tf_op jit(solution)/shard_map/ppermute | solution.py:23
  852.9 12.5 %collective-permute-done.189 = bf16[6,2,128,256]{3,2,0,1:T(8,128)(2,1)S(1)} collective-permute-done((bf16[6,2,128,256]{3,2,0,1:T(8,128)(2,1)S(1)}, bf16[6,2,128,256]{3,2,0,1:T(8,128)(2,1)S(1)}, u32[]{:S(2)}, u32[]{:S(2)}) %collective-permute-start.189) | collective-permute-done | bytes 786464 | tf_op jit(solution)/shard_map/ppermute | solution.py:23
  869.0 16.1 %collective-permute-done.190 = bf16[6,128,256]{2,1,0:T(8,128)(2,1)S(1)} collective-permute-done((bf16[6,128,256]{2,1,0:T(8,128)(2,1)S(1)}, bf16[6,128,256]{2,1,0:T(8,128)(2,1)S(1)}, u32[]{:S(2)}, u32[]{:S(2)}) %collective-permute-start.190) | collective-permute-done | bytes 393248 | tf_op jit(solution)/shard_map/ppermute | solution.py:23
  908.5 10.0 %collective-permute-done.193 = bf16[128,256]{1,0:T(8,128)(2,1)S(1)} collective-permute-done((bf16[128,256]{1,0:T(8,128)(2,1)S(1)}, bf16[128,256]{1,0:T(8,128)(2,1)S(1)}, u32[]{:S(2)}, u32[]{:S(2)}) %collective-permute-start.193) | collective-permute-done | bytes 65568 | tf_op jit(solution)/shard_map/ppermute | solution.py:23
  933.6 19.8 %collective-permute-done.165 = bf16[1,2,128,2048]{3,2,1,0:T(8,128)(2,1)S(1)} collective-permute-done((bf16[1,2,128,2048]{3,2,1,0:T(8,128)(2,1)S(1)}, bf16[1,2,128,2048]{3,2,1,0:T(8,128)(2,1)S(1)}, u32[]{:S(2)}, u32[]{:S(2)}) %collective-permute-start.165) | collective-permute-done | bytes 1048608 | tf_op jit(solution)/shard_map/ppermute | solution.py:23
  966.2 13.5 %collective-permute-done.163 = bf16[128,1024]{1,0:T(8,128)(2,1)S(1)} collective-permute-done((bf16[128,1024]{1,0:T(8,128)(2,1)S(1)}, bf16[128,1024]{1,0:T(8,128)(2,1)S(1)}, u32[]{:S(2)}, u32[]{:S(2)}) %collective-permute-start.163) | collective-permute-done | bytes 262176 | tf_op jit(solution)/shard_map/ppermute | solution.py:23
  (1348 shorter events, 698.0 us)
Async XLA Ops:
  1.6 38.0 %collective-permute-start.83 = (bf16[128,256]{1,0:T(8,128)(2,1)S(1)}, bf16[128,256]{1,0:T(8,128)(2,1)}, u32[]{:S(2)}, u32[]{:S(2)}) collective-permute-start(bf16[128,256]{1,0:T(8,128)(2,1)S(1)} %get-tuple-element.166), channel_id=1, source_target_pairs={{0,2},{1,3},{2,0},{3,1},{4,6},{5,7},{6,4},{7,5},{8,10},{9,11},{10,... | collective-permute-start | bytes 196616 | tf_op jit(solution)/shard_map/ppermute | solution.py:23
  8.8 69.5 %collective-permute-start.1 = (bf16[128,1024]{1,0:T(8,128)(2,1)}, bf16[128,1024]{1,0:T(8,128)(2,1)S(1)}, u32[]{:S(2)}, u32[]{:S(2)}) collective-permute-start(bf16[128,1024]{1,0:T(8,128)(2,1)} %param.22), channel_id=1, source_target_pairs={{0,2},{1,3},{2,0},{3,1},{4,6},{5,7},{6,4},{7,5},{8,10},{9,11},{10,... | collective-permute-start | bytes 786440 | tf_op jit(solution)/shard_map/ppermute | solution.py:23
  39.7 54.1 %collective-permute-start.26 = (bf16[2,128,1024]{2,1,0:T(8,128)(2,1)S(1)}, bf16[2,128,1024]{2,1,0:T(8,128)(2,1)S(1)}, u32[]{:S(2)}, u32[]{:S(2)}) collective-permute-start(bf16[2,128,1024]{2,1,0:T(8,128)(2,1)S(1)} %copy-done.141), channel_id=1, source_target_pairs={{0,2},{1,3},{2,0},{3,1},{4,6},{5,7},{6,4},{7,5},{8,10},{9,11},{10,... | collective-permute-start | bytes 1572872 | tf_op jit(solution)/shard_map/ppermute | solution.py:23
  114.3 37.2 %collective-permute-start.86 = (bf16[4,128,256]{2,1,0:T(8,128)(2,1)}, bf16[4,128,256]{2,1,0:T(8,128)(2,1)}, u32[]{:S(2)}, u32[]{:S(2)}) collective-permute-start(bf16[4,128,256]{2,1,0:T(8,128)(2,1)} %pad_maximum_fusion.38.refs_0_), channel_id=1, source_target_pairs={{0,8},{4,12},{8,0},{12,4},{16,24},{20,28},{24,16},{28,20},{1,9},{5... | collective-permute-start | bytes 786440 | tf_op jit(solution)/shard_map/ppermute | solution.py:23
  295.8 52.2 %collective-permute-start.80 = (bf16[2,512,256]{2,1,0:T(8,128)(2,1)}, bf16[2,512,256]{2,1,0:T(8,128)(2,1)}, u32[]{:S(2)}, u32[]{:S(2)}) collective-permute-start(bf16[2,512,256]{2,1,0:T(8,128)(2,1)} %pad_maximum_fusion.16), channel_id=1, source_target_pairs={{0,4},{4,8},{8,12},{12,16},{16,20},{20,24},{24,28},{1,5},{5,9},{9,... | collective-permute-start | bytes 1572872 | tf_op jit(solution)/shard_map/ppermute | solution.py:233
  298.5 49.4 %collective-permute-start.81 = (bf16[2,512,256]{2,1,0:T(8,128)(2,1)}, bf16[2,512,256]{2,1,0:T(8,128)(2,1)}, u32[]{:S(2)}, u32[]{:S(2)}) collective-permute-start(bf16[2,512,256]{2,1,0:T(8,128)(2,1)} %pad_maximum_fusion.16), channel_id=1, source_target_pairs={{4,0},{8,4},{12,8},{16,12},{20,16},{24,20},{28,24},{5,1},{9,5},{13... | collective-permute-start | bytes 1572872 | tf_op jit(solution)/shard_map/ppermute | solution.py:234
  342.5 43.5 %collective-permute-start.101 = (bf16[1,128,2048]{2,1,0:T(8,128)(2,1)S(1)}, bf16[1,128,2048]{2,1,0:T(8,128)(2,1)S(1)}, u32[]{:S(2)}, u32[]{:S(2)}) collective-permute-start(bf16[1,128,2048]{2,1,0:T(8,128)(2,1)S(1)} %maximum_bitcast_fusion.2.refs_0_), channel_id=1, source_target_pairs={{0,8},{4,12},{8,0},{12,4},{16,24},{20,28},{24,16},{28,20},{1,9},{5... | collective-permute-start | bytes 1572872 | tf_op jit(solution)/shard_map/ppermute | solution.py:23
  346.7 44.6 %collective-permute-start.103 = (bf16[1,128,2048]{2,1,0:T(8,128)(2,1)S(1)}, bf16[1,128,2048]{2,1,0:T(8,128)(2,1)S(1)}, u32[]{:S(2)}, u32[]{:S(2)}) collective-permute-start(bf16[1,128,2048]{2,1,0:T(8,128)(2,1)S(1)} %maximum_bitcast_fusion.2.refs_0_), channel_id=1, source_target_pairs={{0,16},{4,20},{8,24},{12,28},{16,0},{20,4},{24,8},{28,12},{1,17},{... | collective-permute-start | bytes 1572872 | tf_op jit(solution)/shard_map/ppermute | solution.py:23
  347.0 44.3 %collective-permute-start.100 = (bf16[1,128,2048]{2,1,0:T(8,128)(2,1)S(1)}, bf16[1,128,2048]{2,1,0:T(8,128)(2,1)S(1)}, u32[]{:S(2)}, u32[]{:S(2)}) collective-permute-start(bf16[1,128,2048]{2,1,0:T(8,128)(2,1)S(1)} %maximum_bitcast_fusion.2.refs_0_), channel_id=1, source_target_pairs={{0,4},{4,0},{8,12},{12,8},{16,20},{20,16},{24,28},{28,24},{1,5},{5... | collective-permute-start | bytes 1572872 | tf_op jit(solution)/shard_map/ppermute | solution.py:23
  457.0 283.6 %collective-permute-start.194 = (bf16[1,2,2,128,2048]{4,3,1,2,0:T(8,128)(2,1)}, bf16[1,2,2,128,2048]{4,3,1,2,0:T(8,128)(2,1)}, u32[]{:S(2)}, u32[]{:S(2)}) collective-permute-start(bf16[1,2,2,128,2048]{4,3,1,2,0:T(8,128)(2,1)} %bitcast.952), channel_id=1, source_target_pairs={{0,4},{4,0},{8,12},{12,8},{16,20},{20,16},{24,28},{28,24},{1,5},{5... | collective-permute-start | bytes 6291464 | tf_op jit(solution)/shard_map/ppermute | solution.py:23
  460.9 276.6 %collective-permute-start.198 = (bf16[1,2,2,128,2048]{4,3,2,1,0:T(8,128)(2,1)}, bf16[1,2,2,128,2048]{4,3,2,1,0:T(8,128)(2,1)}, u32[]{:S(2)}, u32[]{:S(2)}) collective-permute-start(bf16[1,2,2,128,2048]{4,3,2,1,0:T(8,128)(2,1)} %dynamic-slice_bitcast_fusion), channel_id=1, source_target_pairs={{0,4},{4,0},{8,12},{12,8},{16,20},{20,16},{24,28},{28,24},{1,5},{5... | collective-permute-start | bytes 6291464 | tf_op jit(solution)/shard_map/ppermute | solution.py:23
  542.1 38.3 %collective-permute-start.120 = (bf16[2,512,256]{1,2,0:T(8,128)(2,1)}, bf16[2,512,256]{1,2,0:T(8,128)(2,1)}, u32[]{:S(2)}, u32[]{:S(2)}) collective-permute-start(bf16[2,512,256]{1,2,0:T(8,128)(2,1)} %get-tuple-element.122), channel_id=1, source_target_pairs={{4,0},{8,4},{12,8},{16,12},{20,16},{24,20},{28,24},{5,1},{9,5},{13... | collective-permute-start | bytes 1572872 | tf_op jit(solution)/shard_map/ppermute | solution.py:245
  543.4 38.3 %collective-permute-start.121 = (bf16[2,512,256]{1,2,0:T(8,128)(2,1)}, bf16[2,512,256]{1,2,0:T(8,128)(2,1)}, u32[]{:S(2)}, u32[]{:S(2)}) collective-permute-start(bf16[2,512,256]{1,2,0:T(8,128)(2,1)} %get-tuple-element.123), channel_id=1, source_target_pairs={{0,4},{4,8},{8,12},{12,16},{16,20},{20,24},{24,28},{1,5},{5,9},{9,... | collective-permute-start | bytes 1572872 | tf_op jit(solution)/shard_map/ppermute | solution.py:246
  547.2 85.2 %collective-permute-start.182 = (bf16[4,2,2,128,256]{4,3,0,2,1:T(8,128)(2,1)}, bf16[4,2,2,128,256]{4,3,0,2,1:T(8,128)(2,1)}, u32[]{:S(2)}, u32[]{:S(2)}) collective-permute-start(bf16[4,2,2,128,256]{4,3,0,2,1:T(8,128)(2,1)} %bitcast.955), channel_id=1, source_target_pairs={{0,4},{4,0},{8,12},{12,8},{16,20},{20,16},{24,28},{28,24},{1,5},{5... | collective-permute-start | bytes 3145736 | tf_op jit(solution)/shard_map/ppermute | solution.py:23
  631.5 50.5 %collective-permute-start.173 = (bf16[3,2,2,128,256]{4,3,0,1,2:T(8,128)(2,1)}, bf16[3,2,2,128,256]{4,3,0,1,2:T(8,128)(2,1)}, u32[]{:S(2)}, u32[]{:S(2)}) collective-permute-start(bf16[3,2,2,128,256]{4,3,0,1,2:T(8,128)(2,1)} %bitcast.958), channel_id=1, source_target_pairs={{0,4},{4,0},{8,12},{12,8},{16,20},{20,16},{24,28},{28,24},{1,5},{5... | collective-permute-start | bytes 2359304 | tf_op jit(solution)/shard_map/ppermute | solution.py:23
  649.6 48.5 %collective-permute-start.183 = (bf16[4,2,128,256]{3,2,0,1:T(8,128)(2,1)}, bf16[4,2,128,256]{3,2,0,1:T(8,128)(2,1)}, u32[]{:S(2)}, u32[]{:S(2)}) collective-permute-start(bf16[4,2,128,256]{3,2,0,1:T(8,128)(2,1)} %dynamic-slice_bitcast_fusion.9), channel_id=1, source_target_pairs={{0,16},{4,20},{8,24},{12,28},{16,0},{20,4},{24,8},{28,12},{1,17},{... | collective-permute-start | bytes 1572872 | tf_op jit(solution)/shard_map/ppermute | solution.py:23
  703.9 76.7 %collective-permute-start.188 = (bf16[6,2,2,128,256]{4,3,0,1,2:T(8,128)(2,1)}, bf16[6,2,2,128,256]{4,3,0,1,2:T(8,128)(2,1)}, u32[]{:S(2)}, u32[]{:S(2)}) collective-permute-start(bf16[6,2,2,128,256]{4,3,0,1,2:T(8,128)(2,1)} %bitcast.954), channel_id=1, source_target_pairs={{0,4},{4,0},{8,12},{12,8},{16,20},{20,16},{24,28},{28,24},{1,5},{5... | collective-permute-start | bytes 4718600 | tf_op jit(solution)/shard_map/ppermute | solution.py:23
  704.0 196.3 %collective-permute-start.160 = (bf16[1,2,2,128,2048]{4,3,1,2,0:T(8,128)(2,1)}, bf16[1,2,2,128,2048]{4,3,1,2,0:T(8,128)(2,1)}, u32[]{:S(2)}, u32[]{:S(2)}) collective-permute-start(bf16[1,2,2,128,2048]{4,3,1,2,0:T(8,128)(2,1)} %bitcast.953), channel_id=1, source_target_pairs={{0,4},{4,0},{8,12},{12,8},{16,20},{20,16},{24,28},{28,24},{1,5},{5... | collective-permute-start | bytes 6291464 | tf_op jit(solution)/shard_map/ppermute | solution.py:23
  705.3 40.0 %collective-permute-start.174 = (bf16[3,2,128,256]{3,2,0,1:T(8,128)(2,1)}, bf16[3,2,128,256]{3,2,0,1:T(8,128)(2,1)}, u32[]{:S(2)}, u32[]{:S(2)}) collective-permute-start(bf16[3,2,128,256]{3,2,0,1:T(8,128)(2,1)} %dynamic-slice_bitcast_fusion.15), channel_id=1, source_target_pairs={{0,8},{4,12},{8,0},{12,4},{16,24},{20,28},{24,16},{28,20},{1,9},{5... | collective-permute-start | bytes 1179656 | tf_op jit(solution)/shard_map/ppermute | solution.py:23
  737.6 99.4 %collective-permute-start.149 = (bf16[4,2,2,128,256]{4,3,0,2,1:T(8,128)(2,1)S(1)}, bf16[4,2,2,128,256]{4,3,0,2,1:T(8,128)(2,1)S(1)}, u32[]{:S(2)}, u32[]{:S(2)}) collective-permute-start(bf16[4,2,2,128,256]{4,3,0,2,1:T(8,128)(2,1)S(1)} %bitcast.1146), channel_id=1, source_target_pairs={{0,4},{4,0},{8,12},{12,8},{16,20},{20,16},{24,28},{28,24},{1,5},{5... | collective-permute-start | bytes 3145736 | tf_op jit(solution)/shard_map/ppermute | solution.py:23
  780.7 68.8 %collective-permute-start.195 = (bf16[1,2,128,2048]{3,2,1,0:T(8,128)(2,1)S(1)}, bf16[1,2,128,2048]{3,2,1,0:T(8,128)(2,1)S(1)}, u32[]{:S(2)}, u32[]{:S(2)}) collective-permute-start(bf16[1,2,128,2048]{3,2,1,0:T(8,128)(2,1)S(1)} %dynamic-slice_bitcast_fusion.3), channel_id=1, source_target_pairs={{0,8},{4,12},{8,0},{12,4},{16,24},{20,28},{24,16},{28,20},{1,9},{5... | collective-permute-start | bytes 3145736 | tf_op jit(solution)/shard_map/ppermute | solution.py:23
  788.8 61.0 %collective-permute-start.199 = (bf16[1,2,128,2048]{3,2,1,0:T(8,128)(2,1)S(1)}, bf16[1,2,128,2048]{3,2,1,0:T(8,128)(2,1)S(1)}, u32[]{:S(2)}, u32[]{:S(2)}) collective-permute-start(bf16[1,2,128,2048]{3,2,1,0:T(8,128)(2,1)S(1)} %dynamic-slice_bitcast_fusion.2), channel_id=1, source_target_pairs={{0,16},{4,20},{8,24},{12,28},{16,0},{20,4},{24,8},{28,12},{1,17},{... | collective-permute-start | bytes 3145736 | tf_op jit(solution)/shard_map/ppermute | solution.py:23
  845.4 50.9 %collective-permute-start.164 = (bf16[1,2,2,128,2048]{4,3,2,1,0:T(8,128)(2,1)S(1)}, bf16[1,2,2,128,2048]{4,3,2,1,0:T(8,128)(2,1)S(1)}, u32[]{:S(2)}, u32[]{:S(2)}) collective-permute-start(bf16[1,2,2,128,2048]{4,3,2,1,0:T(8,128)(2,1)S(1)} %copy-done.109), channel_id=1, source_target_pairs={{0,4},{4,0},{8,12},{12,8},{16,20},{20,16},{24,28},{28,24},{1,5},{5... | collective-permute-start | bytes 6291464 | tf_op jit(solution)/shard_map/ppermute | solution.py:23
  896.3 59.5 %collective-permute-start.201 = (bf16[128,1024]{1,0:T(8,128)(2,1)S(1)}, bf16[128,1024]{1,0:T(8,128)(2,1)S(1)}, u32[]{:S(2)}, u32[]{:S(2)}) collective-permute-start(bf16[128,1024]{1,0:T(8,128)(2,1)S(1)} %slice.1122), channel_id=1, source_target_pairs={{0,2},{1,3},{2,0},{3,1},{4,6},{5,7},{6,4},{7,5},{8,10},{9,11},{10,... | collective-permute-start | bytes 786440 | tf_op jit(solution)/shard_map/ppermute | solution.py:23
  (429 other events, 5477.1 us)

commit v2 on v1

v2 whole, which is shorter than its diff:
```python
import functools
import jax
import jax.numpy as jnp
from jax import lax
from jax.experimental import pallas as pl
from jax.experimental.pallas import tpu as pltpu
from jax.sharding import PartitionSpec as P

HD = 64
BF = jnp.bfloat16
F32 = jnp.float32
PACE = 30000000000


def bits_of(axis):
    count, bit, bits = lax.axis_size(axis), 1, []
    while bit < count:
        bits.append(bit)
        bit *= 2
    return bits


def swap(value, axis, mask):
    return lax.ppermute(value, axis, [(i, i ^ mask) for i in range(lax.axis_size(axis))])


def join(value, *ready):
    return lax.optimization_barrier((value, ready))[0] if ready else value


def spread(value, axis, order, gates=()):
    pieces = {0: value}
    for k, bit in enumerate(order):
        for mask in list(pieces):
            piece = pieces[mask]
            if mask and k < len(gates):
                piece = join(piece, *gates[k])
            pieces[mask | bit] = swap(piece, axis, bit)
    if len(gates) > len(order):
        return [pieces[0]] + [join(pieces[mask], *gates[-1]) for mask in sorted(pieces)[1:]]
    return [pieces[mask] for mask in sorted(pieces)]


def total(items):
    out = items[0].astype(F32)
    for item in items[1:]:
        out = out + item.astype(F32)
    return out


def plane_orders():
    bits = bits_of("fsdp")
    return bits[1:] + bits[:1], bits[1:][::-1] + bits[:1]


def placed(parts, index, splits):
    arrays = [array for array, masks in parts]
    total = sum(len(masks) for array, masks in parts)
    rows, cols = arrays[0].shape[2:]

    def kernel(index_ref, *refs):
        ins, outs, sems = refs[: len(parts)], refs[len(parts) : -1], refs[-1]
        copies = []
        for (array, masks), ref in zip(parts, ins):
            for at, mask in enumerate(masks):
                first = 0
                for out, width in zip(outs, splits):
                    copy = pltpu.make_async_copy(
                        ref.at[at, first : first + width],
                        out.at[:, index_ref[0] ^ mask],
                        sems.at[len(copies)],
                    )
                    copy.start()
                    copies.append(copy)
                    first += width
        for copy in copies:
            copy.wait()

    outs = pl.pallas_call(
        kernel,
        out_shape=[
            jax.ShapeDtypeStruct((width, total, rows, cols), arrays[0].dtype) for width in splits
        ],
        in_specs=[pl.BlockSpec(memory_space=pltpu.SMEM)]
        + [pl.BlockSpec(memory_space=pl.ANY)] * len(arrays),
        out_specs=[pl.BlockSpec(memory_space=pltpu.VMEM)] * len(splits),
        scratch_shapes=[pltpu.SemaphoreType.DMA((total * len(splits),))],
        compiler_params=pltpu.CompilerParams(vmem_limit_bytes=32 * 2**20),
        cost_estimate=pl.CostEstimate(flops=PACE, bytes_accessed=1, transcendentals=0),
        name="placed",
    )(index[None], *arrays)
    return [out.reshape(out.shape[0], -1, cols) for out in outs]


def gather_plane(shard, order, splits):
    return Gather(shard[None], order, splits).result()


class Gather:
    def __init__(self, held, order, splits):
        self.held, self.masks, self.order, self.splits = held, [0], list(order), splits
        self.came = None

    def take(self, gate):
        if self.came is not None:
            came = join(self.came, *gate)
            self.held = jnp.concatenate([self.held, came], 0)
            self.masks = self.masks + [mask | self.bit for mask in self.masks]

    def hop(self, *gate):
        self.take(gate)
        self.bit = self.order.pop(0)
        self.came = swap(self.held, "fsdp", self.bit)
        return self.came

    def result(self):
        while self.order:
            self.hop()
        parts = [(self.held, self.masks), (self.came, [mask | self.bit for mask in self.masks])]
        return placed(parts, lax.axis_index("fsdp"), self.splits)


class Spread:
    def __init__(self, value, axis, bits):
        self.axis, self.pieces, self.level, self.last = axis, {0: value}, 0, len(bits)
        self.masks = [m for m in range(lax.axis_size(axis)) if m & ~sum(bits) == 0]

    def hop(self, *gate):
        self.level += 1
        new = []
        for mask in self.masks[::-1]:
            if mask.bit_count() == self.level:
                low = mask & -mask
                piece = self.pieces[mask ^ low]
                if mask != low:
                    piece = join(piece, *gate)
                self.pieces[mask] = swap(piece, self.axis, low)
                new.append(self.pieces[mask])
        return new

    def result(self, *gate):
        while self.level < self.last:
            self.hop()
        return [join(self.pieces[m], *(gate if m else ())) for m in self.masks]


class Share:
    def __init__(self, pieces, axis, bits):
        self.axis, self.held, self.came, self.level = axis, dict(enumerate(pieces)), {}, len(bits)
        self.terms = [pieces[0]]

    def hop(self, *gate):
        for mask, arrays in self.came.items():
            for array in arrays:
                self.held[mask] = self.held[mask].astype(F32) + join(array, *gate).astype(F32)
        self.came = {}
        new = []
        for mask in sorted(self.held)[::-1]:
            if mask and (mask.bit_count() == self.level or mask == 1):
                low = mask & -mask
                came = swap(self.held.pop(mask).astype(BF), self.axis, low)
                if mask == low:
                    self.terms.append(came)
                else:
                    self.came.setdefault(mask ^ low, []).append(came)
                new.append(came)
        self.level -= 1
        return new

    def result(self):
        while self.level > 0:
            self.hop()
        return self.terms


class Fold:
    def __init__(self, keep, send, order, at):
        bits = bits_of("fsdp")
        self.live, self.order, self.at = bits[1:][::-1], list(order), at
        split = keep.shape[:at] + (2,) * len(self.live) + keep.shape[at + 1 :]
        self.value, self.sent, self.bit = keep.reshape(split), send.reshape(split), bits[0]

    def hop(self, *gate):
        self.came = swap(join(self.sent, *gate), "fsdp", self.bit)
        return self.came

    def next(self, *gate):
        bit = self.order.pop(0)
        dim = self.at + self.live.index(bit)
        self.live.remove(bit)
        mine = (lax.axis_index("fsdp") // bit) % 2
        value, came = self.value, join(self.came, *gate)

        def pick(which):
            return lax.dynamic_index_in_dim(value, which, dim, False).astype(
                F32
            ) + lax.dynamic_index_in_dim(came, which, dim, False).astype(F32)

        self.value, self.sent, self.bit = pick(mine).astype(BF), pick(1 - mine).astype(BF), bit
        return self.hop()

    def result(self, *gate):
        while self.order:
            self.next(*gate)
            gate = ()
        return self.value.astype(F32) + join(self.came, *gate).astype(F32)


MIB = 2**20
HEAD_SCALE = HD ** (-0.5)


def run(kernel, scalars, arrays, outs, scratch, name, flops, grid=None, in_blocks=None, out_blocks=None):
    arrays = list(arrays)
    whole = pl.BlockSpec(memory_space=pltpu.VMEM)
    in_specs = [pl.BlockSpec(memory_space=pltpu.SMEM)] * len(scalars)
    in_specs += in_blocks if in_blocks else [whole] * len(arrays)
    extra = {"grid": grid} if grid else {}
    return pl.pallas_call(
        kernel,
        out_shape=[jax.ShapeDtypeStruct(shape, kind) for shape, kind in outs],
        in_specs=in_specs,
        out_specs=out_blocks if out_blocks else [whole] * len(outs),
        scratch_shapes=scratch,
        compiler_params=pltpu.CompilerParams(vmem_limit_bytes=40 * MIB),
        cost_estimate=pl.CostEstimate(
            flops=PACE, bytes_accessed=1, transcendentals=0
        ),
        name=name,
        **extra,
    )(*scalars, *arrays)


def dot(left, right, dims):
    return lax.dot_general(left, right, ((dims[:1], dims[1:]), ((), ())), preferred_element_type=F32)


def head_mask(rows, which, level):
    lane = lax.broadcasted_iota(jnp.int32, (rows, 128), 1)
    return jnp.where(lane // HD == which, level, 0.0).astype(BF)


def tile_allowed(meta, first, size, columns, ranges):
    place = lax.broadcasted_iota(jnp.int32, (size, columns), 0) + first
    allowed = (place >= meta[0:1]) & (place < meta[1:2])
    for k in range(1, ranges):
        allowed = allowed | ((place >= meta[2 * k : 2 * k + 1]) & (place < meta[2 * k + 1 : 2 * k + 2]))
    return allowed


def multiple(value, of):
    return pl.multiple_of(value, of)


def place_rows(ref, pieces, t_index):
    rows = pieces[0].shape[0]
    for mask, piece in enumerate(pieces):
        ref[pl.ds(multiple((t_index ^ mask) * rows, rows), rows), :] = piece[...]


def attend(queries, windows, meta, bounds, t_index, count, ranges):
    tokens, width = queries.shape
    heads, rows = width // HD, tokens // count
    block = min(256, tokens)
    tiles = 3 * tokens // block

    def kernel(bounds_ref, t_ref, meta_ref, q_ref, b_ref, w_ref, a_ref, *rest):
        o_refs, (ot_ref, lse_ref, keys, v_t, held, acc, nat) = rest[:count], rest[count:]
        for j, ref in enumerate((b_ref, w_ref, a_ref)):
            keys[j * tokens : (j + 1) * tokens, :] = ref[0]
            v_t[:, j * tokens : (j + 1) * tokens] = ref[1].T
        for i in range(tokens // block):
            low, high = bounds_ref[2 * i], bounds_ref[2 * i + 1]
            span = slice(i * block, (i + 1) * block)
            info = meta_ref[:, span]
            asked = []
            for h in range(heads):
                lanes = slice(h // 2 * 128, h // 2 * 128 + 128)
                asked.append(q_ref[span, lanes] * head_mask(block, h % 2, HEAD_SCALE))

            def scores(k, tops):
                first = multiple(k * block, block)
                allowed = tile_allowed(info, first, block, block, ranges)
                out = []
                for h in range(heads):
                    lanes = slice(h // 2 * 128, h // 2 * 128 + 128)
                    s = dot(keys[pl.ds(first, block), lanes], asked[h], (1, 1))
                    s = jnp.where(allowed, s, -1e30)
                    held[h, k] = s
                    out.append(jnp.maximum(tops[h], jnp.max(s, 0, keepdims=True)))
                return tuple(out)

            tops = lax.fori_loop(
                low, high, scores, tuple(jnp.full((1, block), -1e30, F32) for h in range(heads))
            )
            acc[...] = jnp.zeros_like(acc)

            def mixes(k, sums):
                first = multiple(k * block, block)
                out = []
                for h in range(heads):
                    p = jnp.exp(held[h, k] - tops[h])
                    out.append(sums[h] + jnp.sum(p, 0, keepdims=True))
                    some = slice(h * HD, (h + 1) * HD)
                    acc[some, :] += dot(v_t[some, pl.ds(first, block)], p.astype(BF), (1, 0))
                return tuple(out)

            sums = lax.fori_loop(
                low, high, mixes, tuple(jnp.zeros((1, block), F32) for h in range(heads))
            )
            for h in range(heads):
                some = slice(h * HD, (h + 1) * HD)
                acc[some, :] = acc[some, :] / sums[h]
                lse_ref[h : h + 1, span] = tops[h] + jnp.log(sums[h])
            ot_ref[:, span] = acc[...]
            nat[span, :] = acc[...].T.astype(BF)
        for mask in range(count):
            o_refs[mask][...] = nat[pl.ds(multiple((t_ref[0] ^ mask) * rows, rows), rows), :]

    out = run(
        kernel,
        [bounds, t_index],
        [meta, queries, *windows],
        [((rows, width), BF)] * count + [((width, tokens), F32), ((heads, tokens), F32)],
        [
            pltpu.VMEM((3 * tokens, width), BF),
            pltpu.VMEM((width, 3 * tokens), BF),
            pltpu.VMEM((heads, tiles, block, block), F32),
            pltpu.VMEM((width, block), F32),
            pltpu.VMEM((tokens, width), BF),
        ],
        "attend",
        4 * tokens * 3 * tokens * width * 4,
    )
    return out[:count], out[count], out[count + 1]


def attend_back(queries, windows, grads, mixed_t, totals, meta, bounds, t_index, count, ranges):
    tokens, width = queries.shape
    heads, rows = width // HD, tokens // count
    block = min(256, tokens)

    def kernel(bounds_ref, t_ref, meta_ref, q_ref, b_ref, w_ref, a_ref, ot_ref, lse_ref, *rest):
        g_refs = rest[:count]
        dq_ref, db_ref, dw_ref, da_ref, nat, keys, values, k_t, dk, dv, acc = rest[count:]
        place_rows(nat, g_refs, t_ref[0])
        for j, ref in enumerate((b_ref, w_ref, a_ref)):
            part = slice(j * tokens, (j + 1) * tokens)
            keys[part, :] = ref[0]
            values[part, :] = ref[1]
            k_t[:, part] = ref[0].T
        dk[...] = jnp.zeros_like(dk)
        dv[...] = jnp.zeros_like(dv)
        for i in range(tokens // block):
            low, high = bounds_ref[2 * i], bounds_ref[2 * i + 1]
            span = slice(i * block, (i + 1) * block)
            info = meta_ref[:, span]
            g_t = nat[span, :].astype(F32).T
            asked, given, inner = [], [], []
            for h in range(heads):
                lanes = slice(h // 2 * 128, h // 2 * 128 + 128)
                some = slice(h * HD, (h + 1) * HD)
                asked.append(q_ref[span, lanes] * head_mask(block, h % 2, HEAD_SCALE))
                given.append(nat[span, lanes] * head_mask(block, h % 2, 1.0))
                inner.append(jnp.sum(g_t[some] * ot_ref[some, span], 0, keepdims=True))
            acc[...] = jnp.zeros_like(acc)

            def step(k, carry):
                first = multiple(k * block, block)
                at = pl.ds(first, block)
                allowed = tile_allowed(info, first, block, block, ranges)
                for h in range(heads):
                    lanes = slice(h // 2 * 128, h // 2 * 128 + 128)
                    some = slice(h * HD, (h + 1) * HD)
                    s = dot(keys[at, lanes], asked[h], (1, 1))
                    p = jnp.exp(jnp.where(allowed, s, -1e30) - lse_ref[h : h + 1, span])
                    dp = dot(values[at, lanes], given[h], (1, 1))
                    ds = (p * (dp - inner[h])).astype(BF)
                    dv[at, lanes] += dot(p.astype(BF), given[h], (1, 0))
                    dk[at, lanes] += dot(ds, asked[h], (1, 0))
                    acc[some, :] += dot(k_t[some, at], ds, (1, 0))
                return carry

            lax.fori_loop(low, high, step, 0)
            dq_ref[span, :] = (acc[...] * HEAD_SCALE).T.astype(BF)
        for j, ref in enumerate((db_ref, dw_ref, da_ref)):
            part = slice(j * tokens, (j + 1) * tokens)
            ref[0] = dk[part, :].astype(ref.dtype)
            ref[1] = dv[part, :].astype(ref.dtype)

    pair = (2, tokens, width)
    return run(
        kernel,
        [bounds, t_index],
        [meta, queries, *windows, mixed_t, totals, *grads],
        [((tokens, width), BF), (pair, BF), (pair, F32), (pair, BF)],
        [
            pltpu.VMEM((tokens, width), BF),
            pltpu.VMEM((3 * tokens, width), BF),
            pltpu.VMEM((3 * tokens, width), BF),
            pltpu.VMEM((width, 3 * tokens), BF),
            pltpu.VMEM((3 * tokens, width), F32),
            pltpu.VMEM((3 * tokens, width), F32),
            pltpu.VMEM((width, block), F32),
        ],
        "attend_back",
        10 * tokens * 3 * tokens * width * 4,
    )


def project(pieces, weights, local, lines, t_index):
    count = len(pieces)
    rows, depth = pieces[0].shape
    tokens, width = rows * count, weights.shape[2]
    outputs = weights.shape[0]

    def kernel(t_ref, w_ref, local_ref, *rest):
        x_ref = rest[count]
        place_rows(x_ref, rest[:count], t_ref[0])
        x = x_ref[...]
        done = []
        for k, line in enumerate(lines):
            value = dot(x, w_ref[k], (1, 0))
            if line is not None:
                value = value + local_ref[0, line : line + 1, :]
            done.append(value.astype(BF))
        if outputs == 3:
            rest[count + 2][...] = done[0]
        rest[count + 1][0] = done[-2]
        rest[count + 1][1] = done[-1]

    outs = [((tokens, depth), BF), ((2, tokens, width), BF)]
    if outputs == 3:
        outs.append(((tokens, width), BF))
    return run(
        kernel, [t_index], [weights, local, *pieces], outs, [], "project",
        2 * tokens * depth * width * outputs,
    )


def project_rows(low, weight, local, line):
    count, depth, width = weight.shape

    def kernel(x_ref, w_ref, local_ref, *outs):
        for mask in range(count):
            outs[mask][...] = (
                dot(x_ref[...], w_ref[mask], (1, 0)) + local_ref[mask, line : line + 1, :]
            ).astype(BF)

    return run(
        kernel, [], [low, weight, local], [((low.shape[0], width), BF)] * count, [],
        "project_rows", 2 * low.shape[0] * depth * width * count,
    )


def normed(total, gain, shift):
    center = total - jnp.mean(total, -1, keepdims=True)
    scale = lax.rsqrt(jnp.mean(center * center, -1, keepdims=True) + 1e-05)
    return center * scale * gain + shift


def out_norm(mixed, weight, residual, vectors, line):
    count, depth, width = weight.shape
    shape = residual.shape

    def kernel(w_ref, r_ref, v_ref, *rest):
        total = r_ref[...].astype(F32) + v_ref[line : line + 1, :]
        for mask in range(count):
            total = total + dot(rest[mask][...], w_ref[mask], (1, 1))
        sum_ref, out_ref, low_ref = rest[count:]
        sum_ref[...] = total
        out = normed(total, v_ref[line + 1 : line + 2, :], v_ref[line + 2 : line + 3, :])
        out_ref[...] = out
        low_ref[...] = out.astype(BF)

    return run(
        kernel, [], [weight, residual, vectors, *mixed], [(shape, F32), (shape, F32), (shape, BF)],
        [], "out_norm", 2 * shape[0] * depth * width * count,
    )


def add_norm(terms, vectors, line):
    shape = terms[0].shape

    def kernel(v_ref, *rest):
        total = v_ref[line : line + 1, :]
        for ref in rest[: len(terms)]:
            total = total + ref[...].astype(F32)
        sum_ref, low_ref = rest[len(terms) :]
        sum_ref[...] = total
        out = normed(total, v_ref[line + 1 : line + 2, :], v_ref[line + 2 : line + 3, :])
        low_ref[...] = out.astype(BF)

    return run(
        kernel, [], [vectors, *terms], [(shape, F32), (shape, BF)], [], "add_norm", 1e6
    )


def ffn_blocks(views, rows, depth, hidden):
    step = min(512 // len(views) if len(views) < 4 else 128, hidden)
    row = pl.BlockSpec((rows, depth), lambda j: (0, 0))

    def weight(index):
        return pl.BlockSpec((1, depth, step), lambda j: (index, 0, j))

    tall = pl.BlockSpec((len(views), 2 * rows, step), lambda j: (0, 0, j))
    line = pl.BlockSpec((len(views), 1, step), lambda j: (0, 0, j))
    specs, arrays = [], []
    for array, up, down in views:
        specs += [weight(up), weight(down)]
        arrays += [array, array]
    return step, row, tall, line, specs, arrays


def ffn_up_down(own, other, views, first):
    rows, depth = own.shape
    hidden, count = views[0][0].shape[2], len(views)
    step, row, tall, line, specs, arrays = ffn_blocks(views, rows, depth, hidden)

    def kernel(own_ref, other_ref, b_ref, *rest):
        weights, (act_ref, slope_ref, keep_ref, send_ref, pair, acc) = rest[:-6], rest[-6:]
        j = pl.program_id(0)

        @pl.when(j == 0)
        def _():
            pair[:rows, :] = own_ref[...]
            pair[rows:, :] = other_ref[...]

        total = None
        for v in range(count):
            u = dot(pair[...], weights[2 * v][0], (1, 0)) + b_ref[v]
            phi = 0.5 * (1.0 + lax.erf(u * 0.7071067811865476))
            act = (u * phi).astype(BF)
            act_ref[v] = act
            slope_ref[v] = (phi + u * 0.3989422804014327 * jnp.exp(-0.5 * u * u)).astype(BF)
            term = dot(act, weights[2 * v + 1][0], (1, 1))
            total = term if total is None else total + term

        @pl.when(j == 0)
        def _():
            acc[...] = total

        @pl.when(j > 0)
        def _():
            acc[...] += total

        @pl.when(j == hidden // step - 1)
        def _():
            keep_ref[...] = acc[:rows, :]
            send_ref[...] = acc[rows:, :].astype(BF)

    wide = (count, 2 * rows, hidden)
    return run(
        kernel, [], [own, other, first, *arrays],
        [(wide, BF), (wide, BF), ((rows, depth), F32), ((rows, depth), BF)],
        [pltpu.VMEM((2 * rows, depth), BF), pltpu.VMEM((2 * rows, depth), F32)],
        "ffn_up_down", 8 * rows * depth * hidden * count, (hidden // step,),
        [row, row, line] + specs, [tall, tall, row, row],
    )


def ffn_down_up(own, other, views, slope):
    rows, depth = own.shape
    hidden, count = views[0][0].shape[2], len(views)
    step, row, tall, line, specs, arrays = ffn_blocks(views, rows, depth, hidden)

    def kernel(own_ref, other_ref, slope_ref, *rest):
        weights, (du_ref, sum_ref, keep_ref, send_ref, pair, acc) = rest[:-6], rest[-6:]
        j = pl.program_id(0)

        @pl.when(j == 0)
        def _():
            pair[:rows, :] = own_ref[...]
            pair[rows:, :] = other_ref[...]

        total = None
        for v in range(count):
            du = (dot(pair[...], weights[2 * v + 1][0], (1, 0)) * slope_ref[v].astype(F32)).astype(BF)
            du_ref[v] = du
            sum_ref[v] = jnp.sum(du.astype(F32), 0, keepdims=True)
            term = dot(du, weights[2 * v][0], (1, 1))
            total = term if total is None else total + term

        @pl.when(j == 0)
        def _():
            acc[...] = total

        @pl.when(j > 0)
        def _():
            acc[...] += total

        @pl.when(j == hidden // step - 1)
        def _():
            keep_ref[...] = acc[:rows, :]
            send_ref[...] = acc[rows:, :].astype(BF)

    return run(
        kernel, [], [own, other, slope, *arrays],
        [
            ((count, 2 * rows, hidden), BF), ((count, 1, hidden), F32),
            ((rows, depth), F32), ((rows, depth), BF),
        ],
        [pltpu.VMEM((2 * rows, depth), BF), pltpu.VMEM((2 * rows, depth), F32)],
        "ffn_down_up", 8 * rows * depth * hidden * count, (hidden // step,),
        [row, row, tall] + specs, [tall, line, row, row],
    )


def split_blocks(full, keep_ref, send_ref, at, core, blocks, size):
    for p in range(blocks // 2):
        mine = multiple((2 * p + core) * size, size)
        theirs = multiple((2 * p + 1 - core) * size, size)
        keep_ref[at + (p,)] = full[pl.ds(mine, size), :]
        send_ref[at + (p,)] = full[pl.ds(theirs, size), :]


def ffn_weight_grads(x_own, x_other, e_own, e_other, du, act, core, blocks):
    rows, depth = x_own.shape
    count, _, hidden = du.shape
    step = min(512, hidden)
    per = hidden // step
    size = depth // blocks
    split = core is not None

    def kernel(core_ref, x_ref, xo_ref, e_ref, eo_ref, du_ref, act_ref, *rest):
        outs, (xs, es, full) = rest[:-3], rest[-3:]

        @pl.when(pl.program_id(0) == 0)
        def _():
            xs[:rows, :] = x_ref[...]
            xs[rows:, :] = xo_ref[...]
            es[:rows, :] = e_ref[...]
            es[rows:, :] = eo_ref[...]

        up = dot(xs[...], du_ref[0], (0, 0)).astype(BF)
        down = dot(es[...], act_ref[0], (0, 0)).astype(BF)
        if split:
            full[...] = up
            split_blocks(full, outs[0], outs[1], (), core_ref[0], blocks, size)
            full[...] = down
            split_blocks(full, outs[2], outs[3], (), core_ref[0], blocks, size)
        else:
            outs[0][0] = up
            outs[0][1] = down

    row = pl.BlockSpec((rows, depth), lambda j: (0, 0))
    tall = pl.BlockSpec((1, 2 * rows, step), lambda j: (j // per, 0, j % per))
    if split:
        part = pl.BlockSpec((blocks // 2, size, step), lambda j: (0, 0, j))
        outs, out_blocks = [((blocks // 2, size, hidden * count), BF)] * 4, [part] * 4
    else:
        outs = [((2 * count, depth, hidden), BF)]
        out_blocks = [pl.BlockSpec((2, depth, step), lambda j: (j // per, 0, j % per))]
    return run(
        kernel, [core if split else jnp.zeros((1,), jnp.int32)],
        [x_own, x_other, e_own, e_other, du, act], outs,
        [
            pltpu.VMEM((2 * rows, depth), BF),
            pltpu.VMEM((2 * rows, depth), BF),
            pltpu.VMEM((depth, step), BF),
        ],
        "ffn_weight_grads", 8 * rows * depth * hidden * count, (count * per,),
        [row, row, row, row, tall, tall], out_blocks,
    )


def weight_grads(groups, core, blocks):
    arrays, places = [], []
    for group in groups:
        for pair in group:
            spot = []
            for array in pair:
                known = [i for i, a in enumerate(arrays) if a is array]
                if not known:
                    arrays.append(array)
                    known = [len(arrays) - 1]
                spot.append(known[0])
            places.append(spot)
    depth, width = groups[0][0][0].shape[1], groups[0][0][1].shape[1]
    size = depth // blocks
    count = len(arrays)

    def kernel(core_ref, *rest):
        outs, full = rest[count:-1], rest[-1]
        number = 0
        for g, group in enumerate(groups):
            for j in range(len(group)):
                left, right = places[number]
                value = dot(rest[left][...], rest[right][...], (0, 0)).astype(BF)
                if core is None:
                    outs[g][j] = value
                else:
                    full[...] = value
                    split_blocks(
                        full, outs[2 * g], outs[2 * g + 1], (j,), core_ref[0], blocks, size
                    )
                number += 1

    outs = []
    for group in groups:
        if core is None:
            outs.append(((len(group), depth, width), BF))
        else:
            outs += [((len(group), blocks // 2, size, width), BF)] * 2
    flops = sum(2 * left.shape[0] * depth * width for group in groups for left, right in group)
    return run(
        kernel, [jnp.zeros((1,), jnp.int32) if core is None else core], arrays, outs,
        [pltpu.VMEM((depth, width), BF)], "weight_grads", flops,
    )


def norm_grad_body(terms, summed, gain, grad_ref, low_ref, sums_ref):
    grad = terms[0][...].astype(F32)
    for ref in terms[1:]:
        grad = grad + ref[...].astype(F32)
    total = summed[...]
    center = total - jnp.mean(total, -1, keepdims=True)
    scale = lax.rsqrt(jnp.mean(center * center, -1, keepdims=True) + 1e-05)
    unit = center * scale
    inner = grad * gain
    out = scale * (
        inner - jnp.mean(inner, -1, keepdims=True) - unit * jnp.mean(inner * unit, -1, keepdims=True)
    )
    low = out.astype(BF)
    grad_ref[...] = out
    low_ref[...] = low
    sums_ref[0:1, :] = jnp.sum(low.astype(F32), 0, keepdims=True)
    sums_ref[1:2, :] = jnp.sum(grad * unit, 0, keepdims=True)
    sums_ref[2:3, :] = jnp.sum(grad, 0, keepdims=True)
    return low


def norm_grad(terms, summed, gain, line):
    shape = summed.shape

    def kernel(sum_ref, gain_ref, *rest):
        norm_grad_body(rest[: len(terms)], sum_ref, gain_ref[line : line + 1, :], *rest[len(terms) :])

    return run(
        kernel, [], [summed, gain, *terms], [(shape, F32), (shape, BF), ((3, shape[1]), F32)], [],
        "norm_grad", 1e6,
    )


def norm_out_grad(terms, summed, gain, line, weight):
    shape = summed.shape
    count, depth, width = weight.shape

    def kernel(sum_ref, gain_ref, w_ref, *rest):
        outs = rest[len(terms) :]
        low = norm_grad_body(rest[: len(terms)], sum_ref, gain_ref[line : line + 1, :], *outs[:3])
        for mask in range(count):
            outs[3 + mask][...] = dot(low, w_ref[mask], (1, 0)).astype(BF)

    return run(
        kernel, [], [summed, gain, weight, *terms],
        [(shape, F32), (shape, BF), ((3, shape[1]), F32)] + [((shape[0], width), BF)] * count, [],
        "norm_out_grad", 2 * shape[0] * depth * width * count,
    )


def input_grads(dq, own, below, above, weights, t_index, count):
    tokens, width = dq.shape
    rows, depth = tokens // count, weights.shape[1]
    ahead = weights.shape[0] - 2

    def kernel(t_ref, w_ref, dq_ref, own_ref, below_ref, above_ref, dk_ref, dv_ref, sums_ref, *rest):
        full = rest[count]
        for j, ref in enumerate((dk_ref, dv_ref)):
            ref[...] = (
                own_ref[j] + below_ref[j].astype(F32) + above_ref[j].astype(F32)
            ).astype(BF)
        sums_ref[0:1, :] = jnp.sum(dq_ref[...].astype(F32), 0, keepdims=True)
        sums_ref[1:2, :] = jnp.sum(dv_ref[...].astype(F32), 0, keepdims=True)
        total = dot(dk_ref[...], w_ref[ahead], (1, 1)) + dot(dv_ref[...], w_ref[ahead + 1], (1, 1))
        if ahead:
            total = total + dot(dq_ref[...], w_ref[0], (1, 1))
        full[...] = total
        for mask in range(count):
            part = full[pl.ds(multiple((t_ref[0] ^ mask) * rows, rows), rows), :]
            rest[mask][...] = part.astype(rest[mask].dtype)

    return run(
        kernel, [t_index], [weights, dq, own, below, above],
        [((tokens, width), BF)] * 2 + [((2, width), F32), ((rows, depth), F32)]
        + [((rows, depth), BF)] * (count - 1),
        [pltpu.VMEM((tokens, depth), F32)], "input_grads",
        2 * tokens * width * depth * weights.shape[0],
    )


def asked_grad(pieces, weight):
    count, depth, width = weight.shape
    rows = pieces[0].shape[0]

    def kernel(w_ref, *rest):
        total = dot(rest[0][...], w_ref[0], (1, 1))
        for mask in range(1, count):
            total = total + dot(rest[mask][...], w_ref[mask], (1, 1))
        rest[count][...] = total

    return run(
        kernel, [], [weight, *pieces], [((rows, depth), F32)], [], "asked_grad",
        2 * rows * depth * width * count,
    )[0]


def by_mask(values, t_index, count):
    tokens, width = values.shape
    rows = tokens // count

    def kernel(t_ref, x_ref, *outs):
        for mask in range(count):
            outs[mask][...] = x_ref[pl.ds(multiple((t_ref[0] ^ mask) * rows, rows), rows), :]

    return run(kernel, [t_index], [values], [((rows, width), BF)] * count, [], "by_mask", 1000)


def in_order(pieces, t_index):
    count = len(pieces)
    rows, width = pieces[0].shape

    def kernel(t_ref, *refs):
        place_rows(refs[count], refs[:count], t_ref[0])

    return run(
        kernel, [t_index], pieces, [((rows * count, width), BF)], [], "in_order", 1000
    )[0]


LINES = 32
ENC_ATT, ENC_FFN, SELF_ATT, CROSS_ATT, DEC_FFN, ENC_FIRST, DEC_FIRST = 0, 5, 8, 13, 18, 21, 25


def pack_small(arrays, width):
    def kernel(*refs):
        lines = []
        for ref in refs[:-1]:
            value = ref[...].astype(F32)
            if value.shape[1] > width:
                value = jnp.concatenate(
                    [value[:, i : i + width] for i in range(0, value.shape[1], width)], 0
                )
            lines.append(value)
        used = sum(value.shape[0] for value in lines)
        lines.append(jnp.zeros((LINES - used, width), F32))
        refs[-1][...] = jnp.concatenate(lines, 0).astype(BF)

    blocks = [pl.BlockSpec(array.shape, lambda i: (0, 0)) for array in arrays]
    return run(
        kernel, [], arrays, [((LINES, width), BF)], [], "pack_small", 0, (1,), blocks,
        [pl.BlockSpec((LINES, width), lambda i: (0, 0))],
    )[0]


def unpack_small(parts, t_index, count, features, wide_masks):
    peers, lines, width = parts.shape
    share_ = peers // count
    quarter = 4
    hidden = share_ * quarter * width

    def kernel(t_ref, x_ref, table, local, enc_ref, dec_ref):
        for f in range(peers):
            table[:, f * width : (f + 1) * width] = x_ref[f].astype(F32)
        for mask in range(count):
            local[mask] = table[:, pl.ds(multiple((t_ref[0] ^ mask) * features, 128), features)]
        for ref, first in ((enc_ref, ENC_FIRST), (dec_ref, DEC_FIRST)):
            for v, mask in enumerate(wide_masks):
                for f in range(share_):
                    for q in range(quarter):
                        at = (f * quarter + q) * width
                        ref[v, :, at : at + width] = local[
                            mask, first + q : first + q + 1, f * width : (f + 1) * width
                        ]

    first = ((len(wide_masks), 1, hidden), F32)
    return run(
        kernel, [t_index], [parts],
        [((lines, peers * width), F32), ((count, lines, features), F32), first, first], [],
        "unpack_small", 0,
    )


def pack_grads(sums, columns, firsts, t_index, peers, wide_masks):
    depth = sums[0].shape[1]
    width = depth // peers
    features = columns[0].shape[1]
    share_ = features // width
    quarter = 4
    arrays = list(sums) + list(columns) + list(firsts)

    def kernel(t_ref, *refs):
        out, table = refs[-2:]
        table[...] = jnp.zeros_like(table)
        own = pl.ds(multiple(t_ref[0] * features, 128), features)
        att = (ENC_ATT, SELF_ATT, CROSS_ATT)
        for first, s_ref, c_ref in zip(att, refs[:3], refs[5:8]):
            table[first + 2 : first + 5, :] = s_ref[...]
            table[first : first + 2, own] = c_ref[...]
        for first, s_ref in zip((ENC_FFN, DEC_FFN), refs[3:5]):
            table[first : first + 3, :] = s_ref[...]
        for first, f_ref in zip((ENC_FIRST, DEC_FIRST), refs[8:10]):
            for v, mask in enumerate(wide_masks):
                strip = []
                for q in range(quarter):
                    pieces = []
                    for f in range(share_):
                        at = (f * quarter + q) * width
                        pieces.append(f_ref[v, :, at : at + width])
                    strip.append(jnp.concatenate(pieces, 1))
                there = pl.ds(multiple((t_ref[0] ^ mask) * features, 128), features)
                table[first : first + quarter, there] = jnp.concatenate(strip, 0)
        for f in range(peers):
            out[f] = table[:, f * width : (f + 1) * width]

    return run(
        kernel, [t_index], arrays, [((peers, LINES, width), F32)],
        [pltpu.VMEM((LINES, depth), F32)], "pack_grads", 0,
    )[0]


def unpack_grads(terms, shapes):
    def kernel(*refs):
        value = refs[0][...]
        for ref in refs[1 : len(terms)]:
            value = value + ref[...]
        width = value.shape[1]
        line = 0
        for ref in refs[len(terms) :]:
            rows, columns = ref.shape
            for r in range(rows):
                for at in range(0, columns, width):
                    ref[r : r + 1, at : at + width] = value[line : line + 1, :]
                    line += 1

    return run(kernel, [], terms, [(shape, F32) for shape in shapes], [], "unpack_grads", 0)


def token_spans(seq_lens, pic_start, pic_len, base, tokens, block):
    count, pictures = pic_start.shape
    blocks = tokens // block

    def kernel(lens, starts, extents, base_ref, both, text, both_bounds, text_bounds):
        places = lax.broadcasted_iota(jnp.int32, (1, tokens), 1) + tokens
        zero = jnp.zeros((1, tokens), jnp.int32)
        begin, end = zero, zero
        low, high = [zero] * pictures, [zero] * pictures
        edges = [
            [jnp.int32(3 * tokens), jnp.int32(0), jnp.int32(tokens + (i + 1) * block)]
            for i in range(blocks)
        ]
        start = tokens - base_ref[0]
        for s in range(count):
            stop = start + lens[s]
            inside = (places >= start) & (places < stop)
            begin = jnp.where(inside, start, begin)
            end = jnp.where(inside, stop, end)
            spans = []
            for k in range(pictures):
                first = start + starts[s, k]
                last = jnp.minimum(first + extents[s, k], stop)
                member = inside & (places >= first) & (places < last)
                low[k] = jnp.where(member, first, low[k])
                high[k] = jnp.where(member, last, high[k])
                spans.append((first, last))
            for i in range(blocks):
                from_, to = tokens + i * block, tokens + (i + 1) * block
                meets = (start < to) & (stop > from_)
                edge = edges[i]
                edge[0] = jnp.where(meets, jnp.minimum(edge[0], start), edge[0])
                edge[1] = jnp.where(meets, jnp.maximum(edge[1], stop), edge[1])
                for first, last in spans:
                    touches = (first < to) & (last > from_)
                    edge[2] = jnp.where(touches, jnp.maximum(edge[2], last), edge[2])
            start = stop
        both[...] = jnp.concatenate([begin, end] + [zero] * 6, 0)
        seen = [begin, places + 1]
        for k in range(pictures):
            seen += [low[k], high[k]]
        text[...] = jnp.concatenate(seen + [zero] * (8 - len(seen)), 0)
        for i in range(blocks):
            first = lax.div(edges[i][0], jnp.int32(block))
            both_bounds[2 * i] = first
            both_bounds[2 * i + 1] = lax.div(edges[i][1] + (block - 1), jnp.int32(block))
            text_bounds[2 * i] = first
            text_bounds[2 * i + 1] = lax.div(edges[i][2] + (block - 1), jnp.int32(block))

    whole = pl.BlockSpec(memory_space=pltpu.VMEM)
    scalars = pl.BlockSpec(memory_space=pltpu.SMEM)
    return run(
        kernel, [seq_lens, pic_start, pic_len, base], [],
        [((8, tokens), jnp.int32)] * 2 + [((2 * blocks,), jnp.int32)] * 2, [], "token_spans", 0,
        None, None, [whole, whole, scalars, scalars],
    )


def per_device(
    enc_in,
    dec_in,
    enc_cot,
    dec_cot,
    seq_lens,
    pic_start,
    pic_len,
    enc_attn_w,
    enc_attn_bias,
    enc_attn_norm,
    enc_ffn_w,
    enc_ffn_b1,
    enc_ffn_vec,
    self_attn_w,
    self_attn_bias,
    self_attn_norm,
    cross_attn_w,
    cross_attn_bias,
    cross_attn_norm,
    dec_ffn_w,
    dec_ffn_b1,
    dec_ffn_vec,
):
    rows = enc_in.shape[0]
    tensor_size = lax.axis_size("tensor")
    fsdp_size = lax.axis_size("fsdp")
    t_index = lax.axis_index("tensor")
    f_index = lax.axis_index("fsdp")
    t_ref = t_index[None].astype(jnp.int32)
    core = (f_index % 2)[None].astype(jnp.int32)
    tokens = rows * tensor_size
    features = enc_attn_w.shape[2]
    hidden = enc_ffn_w.shape[2]
    t_down = bits_of("tensor")[::-1]
    t_up = bits_of("tensor")
    wide_down = t_down[:-1]
    wide_up = t_up[1:]
    t_masks = range(tensor_size)
    wide_masks = range(0, tensor_size, 2)

    small = [
        enc_attn_bias, enc_attn_norm, enc_ffn_vec, self_attn_bias, self_attn_norm,
        cross_attn_bias, cross_attn_norm, dec_ffn_vec, enc_ffn_b1, dec_ffn_b1,
    ]
    parts = lax.all_gather(pack_small(small, enc_attn_bias.shape[1]), "fsdp", axis=0)
    table, local, enc_first, dec_first = unpack_small(
        parts, t_ref, tensor_size, features, wide_masks
    )
    block = min(256, tokens)
    base = (f_index * tokens)[None].astype(jnp.int32)
    spans = token_spans(seq_lens, pic_start, pic_len, base, tokens, block)
    both = (spans[0], spans[2], 1)
    text = (spans[1], spans[3], 1 + pic_start.shape[1])

    first_order, second_order = plane_orders()

    def later(value, ready):
        return lax.optimization_barrier((value, ready))[0]

    def ffn_gather(shards):
        stack = shards[0] if len(shards) == 1 else jnp.concatenate(shards)
        whole = lax.all_gather(stack, "fsdp", axis=1, tiled=True)
        return [(whole, 2 * i, 2 * i + 1) for i in range(len(shards))]

    def exchange(pieces_):
        return [pieces_[0]] + [swap(pieces_[mask], "tensor", mask) for mask in t_masks[1:]]

    peers = fsdp_size
    up_pairs = [(i, i + 1) for i in range(peers - 1)]
    down_pairs = [(j, i) for i, j in up_pairs]

    def halo(pair):
        before = lax.ppermute(pair, "fsdp", up_pairs)
        after = lax.ppermute(pair, "fsdp", down_pairs)
        return before, pair, after

    def attend_fg(queries, window, mode):
        return attend(queries, window, mode[0], mode[1], t_ref, tensor_size, mode[2])

    def attend_back_fg(queries, window, grads, mixed_t, totals, mode):
        return attend_back(
            queries, window, grads, mixed_t, totals, mode[0], mode[1], t_ref, tensor_size, mode[2]
        )

    pending = [[], []]

    def due(*values):
        pending[1].extend(values)

    def fg(value):
        waits = pending.pop(0)
        pending.append([])
        return join(value, *waits)

    enc_pieces = spread(enc_in, "tensor", t_down)
    (enc_qkv,) = gather_plane(enc_attn_w[:3], first_order, [3])
    enc_out_shards = jnp.stack(spread(enc_attn_w[3], "tensor", t_down))[None]
    enc_own_views = ffn_gather([join(enc_ffn_w, enc_qkv)])
    plan = Gather(enc_out_shards, second_order, [tensor_size])
    due(plan.hop())
    flat_e, pair_e, query_e = project(
        enc_pieces, fg(enc_qkv), local, (ENC_ATT, None, ENC_ATT + 1), t_ref
    )
    k1 = query_e
    window_e = halo(pair_e)
    due(plan.hop(k1))
    self_plan = Gather(join(self_attn_w[:3], k1)[None], first_order, [3])
    due(self_plan.hop())
    dec_spread = Spread(join(dec_in, k1), "tensor", t_down)
    due(*dec_spread.hop())
    self_spread = Spread(join(self_attn_w[3], k1), "tensor", t_down)
    due(*self_spread.hop())

    mixed_e, mixed_t_e, totals_e = attend_fg(fg(query_e), window_e, both)
    k2 = totals_e
    mixed_e = exchange(mixed_e)
    plan.hop(k2)
    (enc_out_w,) = plan.result()
    due(*dec_spread.hop(k2), *self_spread.hop(k2))
    due(self_plan.hop(k2))

    summed_e, hid, hid_low = out_norm(
        [fg(mixed_e[0])] + mixed_e[1:], enc_out_w, enc_in, table, ENC_ATT + 2
    )
    k3 = hid_low
    hid_other = swap(hid_low, "tensor", 1)
    self_plan.hop(k3)
    (self_qkv,) = self_plan.result()
    dec_pieces = dec_spread.result()
    self_out_plan = Gather(
        jnp.stack(self_spread.result(k3))[None], second_order, [tensor_size]
    )
    due(self_out_plan.hop())
    enc_wide = Spread(join(enc_ffn_w, k3), "tensor", wide_down)
    enc_wide.hop()
    cross_spread = Spread(
        join(jnp.stack([cross_attn_w[3], cross_attn_w[0]]), k3), "tensor", t_down
    )
    due(*cross_spread.hop())

    flat_s, pair_s, query_s = project(
        fg(dec_pieces), self_qkv, local, (SELF_ATT, None, SELF_ATT + 1), t_ref
    )
    k4 = query_s
    window_s = halo(pair_s)
    due(self_out_plan.hop(k4))
    due(*cross_spread.hop(k4))
    enc_shards = enc_wide.result(k4)

    mixed_s, mixed_t_s, totals_s = attend_fg(fg(query_s), window_s, text)
    k5 = totals_s
    mixed_s = exchange(mixed_s)
    enc_views = enc_own_views + ffn_gather(join(enc_shards[1:], k5))
    self_out_plan.hop(k5)
    (self_out_w,) = self_out_plan.result()
    cross_pieces = cross_spread.result(k5)
    cross_shards = jnp.concatenate(
        [cross_attn_w[1:3]]
        + [piece[1:2] for piece in cross_pieces]
        + [piece[0:1] for piece in cross_pieces]
    )
    cross_plan = Gather(cross_shards[None], first_order, [2, tensor_size, tensor_size])
    due(cross_plan.hop())
    dec_wide = Spread(join(dec_ffn_w, k5), "tensor", wide_down)
    dec_wide.hop()

    summed_s, decoded, decoded_low = out_norm(
        [fg(mixed_s[0])] + mixed_s[1:], self_out_w, dec_in, table, SELF_ATT + 2
    )
    k6 = decoded_low
    cross_plan.hop(k6)
    dec_views = ffn_gather(dec_wide.result(k6))

    active_e, slope_e, keep, send = ffn_up_down(
        join(hid_low, k6), hid_other, enc_views, enc_first
    )
    k7 = keep
    came = swap(send, "tensor", 1)
    cross_plan.hop(k7)
    cross_kv, cross_query, cross_out_w = cross_plan.result()
    ffn_summed_e, encoded = add_norm([hid, keep, came], table, ENC_FFN)
    enc_rows = spread(encoded, "tensor", t_down)
    asked = exchange(
        project_rows(join(decoded_low, encoded), cross_query, local, CROSS_ATT)
    )

    flat_c, pair_c = project(
        enc_rows, cross_kv, local, (None, CROSS_ATT + 1), t_ref
    )
    window_c = halo(pair_c)
    query_c = in_order(asked, t_ref)
    mixed_c, mixed_t_c, totals_c = attend_fg(query_c, window_c, both)
    mixed_c = exchange(mixed_c)
    summed_c, crossed, crossed_low = out_norm(
        mixed_c, cross_out_w, decoded, table, CROSS_ATT + 2
    )
    crossed_other = swap(crossed_low, "tensor", 1)
    active_d, slope_d, keep, send = ffn_up_down(
        crossed_low, crossed_other, dec_views, dec_first
    )
    came = swap(send, "tensor", 1)
    ffn_summed_d, final = add_norm([crossed, keep, came], table, DEC_FFN)

    grad_sum_d, low_d, dec_sums = norm_grad([dec_cot], ffn_summed_d, table, DEC_FFN + 1)
    other_d = swap(low_d, "tensor", 1)
    du_d, dec_first_sum, keep, send = ffn_down_up(low_d, other_d, dec_views, slope_d)
    came = swap(send, "tensor", 1)
    dec_grads = ffn_weight_grads(
        crossed_low, crossed_other, low_d, other_d, join(du_d, send), active_d, None, fsdp_size
    )[0]
    dec_whole = lax.psum_scatter(dec_grads, "fsdp", scatter_dimension=1, tiled=True)

    grad_sum_c, low_c, sums_c, *given = norm_out_grad(
        [grad_sum_d, join(keep, dec_grads), came], summed_c, table, CROSS_ATT + 3, cross_out_w
    )
    given = exchange(given)
    dq_c, below, own, above = attend_back_fg(
        query_c, window_c, given, mixed_t_c, totals_c, both
    )
    below = lax.ppermute(below, "fsdp", down_pairs)
    above = lax.ppermute(above, "fsdp", up_pairs)
    asked_c = exchange(by_mask(dq_c, t_ref, tensor_size))
    dk_c, dv_c, columns_c, *blocks_c = input_grads(
        dq_c, own, below, above, cross_kv, t_ref, tensor_size
    )
    source = Share(blocks_c, "tensor", t_up)
    due(*source.hop())
    from_asked = asked_grad([join(asked_c[0], dk_c)] + asked_c[1:], cross_query)

    grad_sum_s, low_s, sums_s, *given = norm_out_grad(
        [fg(grad_sum_c), from_asked], summed_s, table, SELF_ATT + 3, self_out_w
    )
    b6 = low_s
    given = exchange(given)
    due(*source.hop(b6))
    cross_grads = weight_grads(
        [
            [(flat_c, join(dk_c, b6)), (flat_c, dv_c)]
            + [(low_c, piece) for piece in mixed_c]
            + [(decoded_low, piece) for piece in asked_c]
        ],
        core, fsdp_size,
    )
    cross_fold = Fold(cross_grads[0], cross_grads[1], second_order[:-1], 1)
    due(cross_fold.hop())
    dq_s, below, own, above = attend_back_fg(
        query_s, window_s, [fg(given[0])] + given[1:], mixed_t_s, totals_s, text
    )
    b7 = dq_s
    below = lax.ppermute(below, "fsdp", down_pairs)
    above = lax.ppermute(above, "fsdp", up_pairs)
    cross_fold.next(b7)
    grad_sum_f, low_f, enc_sums = norm_grad(
        [join(enc_cot, b7)] + source.result(), ffn_summed_e, table, ENC_FFN + 1
    )
    b9 = low_f
    other_f = swap(low_f, "tensor", 1)
    dk_s, dv_s, columns_s, *blocks_s = input_grads(
        dq_s, join(own, b9), below, above, self_qkv, t_ref, tensor_size
    )
    b8 = dk_s
    target = Share(blocks_s, "tensor", t_up)
    due(*target.hop())
    due(cross_fold.came)
    du_e, enc_first_sum, keep, send = ffn_down_up(
        fg(join(low_f, b8)), other_f, enc_views, slope_e
    )
    b10 = keep
    came = swap(send, "tensor", 1)
    due(*target.hop(b10))
    due(cross_fold.next(b10))
    enc_grads = ffn_weight_grads(
        hid_low, hid_other, low_f, other_f, join(du_e, send), active_e, core, fsdp_size
    )
    self_parts = weight_grads(
        [
            [(flat_s, join(dq_s, b10)), (flat_s, dk_s), (flat_s, dv_s)]
            + [(low_s, piece) for piece in mixed_s]
        ],
        core, fsdp_size,
    )
    due(enc_grads, self_parts)

    grad_sum_e, low_e, sums_e, *given = norm_out_grad(
        [grad_sum_f, fg(keep), came], summed_e, table, ENC_ATT + 3, enc_out_w
    )
    b11 = low_e
    given = exchange(given)
    enc_folds = [
        Fold(enc_grads[2 * i], enc_grads[2 * i + 1], (first_order, second_order)[i][:-1], 0)
        for i in range(2)
    ]
    for item in enc_folds:
        due(item.hop(b11))
    self_fold = Fold(self_parts[0], self_parts[1], first_order[:-1], 1)
    due(self_fold.hop(b11))
    cross_own = cross_fold.result(b11)
    cross_pieces = cross_own[2:].reshape((2, tensor_size) + cross_own.shape[1:])
    cross_share = Share([cross_pieces[:, mask] for mask in t_masks], "tensor", t_up)
    due(*cross_share.hop())
    dq_e, below, own, above = attend_back_fg(
        query_e, window_e, [fg(given[0])] + given[1:], mixed_t_e, totals_e, both
    )
    b12 = dq_e
    below = lax.ppermute(below, "fsdp", down_pairs)
    above = lax.ppermute(above, "fsdp", up_pairs)
    for item in enc_folds:
        due(item.next(b12))
    due(*cross_share.hop(b12))
    due(self_fold.next(b12))
    dk_e, dv_e, columns_e, *blocks_e = input_grads(
        dq_e, fg(own), below, above, enc_qkv, t_ref, tensor_size
    )
    b13 = dk_e
    enc_share = Share(blocks_e, "tensor", t_up)
    enc_share.hop()
    enc_att = weight_grads(
        [
            [(flat_e, dq_e), (flat_e, join(dk_e, tuple(blocks_e))), (flat_e, dv_e)],
            [(low_e, piece) for piece in mixed_e],
        ],
        core, fsdp_size,
    )
    enc_att_folds = [
        Fold(enc_att[2 * i], enc_att[2 * i + 1], (first_order, second_order)[i][:-1], 1)
        for i in range(2)
    ]
    for item in enc_att_folds:
        item.hop()
    enc_own = [item.result(b13) for item in enc_folds]
    self_own = self_fold.result(b13)

    def tensor_sum(pieces_):
        return total(Share(pieces_, "tensor", t_up).result())

    def wide_sum(pieces_):
        held = dict(zip(wide_masks, pieces_))
        for bit in wide_up:
            for mask in sorted(held):
                if mask not in held or mask & (2 * bit - 1):
                    continue
                came_ = swap(held.pop(mask | bit).astype(BF), "tensor", bit)
                held[mask] = held[mask].astype(F32) + came_.astype(F32)
        return held[0].astype(F32)

    wide_count = len(wide_masks)
    small_grads = pack_grads(
        [sums_e, sums_s, sums_c, enc_sums, dec_sums], [columns_e, columns_s, columns_c],
        [enc_first_sum, dec_first_sum], t_ref, fsdp_size, wide_masks,
    )
    for bit in bits_of("fsdp")[::-1]:
        half = small_grads.shape[0] // 2
        mine = (f_index // bit) % 2
        kept = lax.dynamic_slice_in_dim(small_grads, mine * half, half, 0)
        sent = lax.dynamic_slice_in_dim(small_grads, (1 - mine) * half, half, 0)
        small_grads = kept + swap(sent, "fsdp", bit)
    small_grads = small_grads[0]
    for bit in t_up[:-1]:
        small_grads = small_grads + swap(small_grads, "tensor", bit)
    small_out = unpack_grads(
        [small_grads, swap(small_grads, "tensor", t_up[-1])], [item.shape for item in small]
    )

    enc_share.hop()
    dec_ffn_grad = wide_sum(
        [join(dec_whole, b12)[2 * j : 2 * j + 2] for j in range(wide_count)]
    )
    enc_pair = jnp.stack(enc_own)
    enc_ffn_grad = wide_sum(
        [enc_pair[:, :, j * hidden : (j + 1) * hidden] for j in range(wide_count)]
    )
    self_grad = jnp.concatenate(
        [self_own[:3], tensor_sum([self_own[3 + mask] for mask in t_masks])[None]]
    )
    cross_pair = total(cross_share.result())
    cross_grad = jnp.concatenate([cross_pair[1:2], cross_own[:2], cross_pair[0:1]])
    enc_att_own, enc_att_out = [item.result() for item in enc_att_folds]
    enc_grad = jnp.concatenate(
        [enc_att_own, tensor_sum([enc_att_out[mask] for mask in t_masks])[None]]
    )
    grad_source = total([grad_sum_e] + enc_share.result())
    grad_target = total([grad_sum_s] + target.result())

    (
        enc_bias_g, enc_norm_g, enc_vec_g, self_bias_g, self_norm_g,
        cross_bias_g, cross_norm_g, dec_vec_g, enc_b1_g, dec_b1_g,
    ) = small_out
    return (
        encoded,
        final,
        grad_source,
        grad_target,
        enc_grad,
        enc_bias_g,
        enc_norm_g,
        enc_ffn_grad,
        enc_b1_g,
        enc_vec_g,
        self_grad,
        self_bias_g,
        self_norm_g,
        cross_grad,
        cross_bias_g,
        cross_norm_g,
        dec_ffn_grad,
        dec_b1_g,
        dec_vec_g,
    )


def solution(mesh):
    rows = P(("fsdp", "tensor"), None)
    weight = P(None, "fsdp", "tensor")
    vector = P(None, "fsdp")
    att, ffn = (weight, vector, vector), (weight, vector, vector)
    in_specs = (rows,) * 4 + (P(),) * 3 + (att + ffn + att + att + ffn)
    out_specs = (rows,) * 4 + (att + ffn + att + att + ffn)
    return jax.shard_map(
        per_device, mesh=mesh, in_specs=in_specs, out_specs=out_specs, check_vma=False
    )
```

time: 995 us -> 728 us (0.73)
  matrix products: 175 us -> 0 us
  Pallas kernels: 9.61 us -> 89.5 us
  other arithmetic: 89.8 us -> 33.8 us
  waiting for transfers between devices: 378 us -> 331 us
  local copies, waits for them, and re-layouts: 90.8 us -> 49.1 us
  starting transfers between devices: 228 us -> 190 us
  between operations: 6.33 us -> 16.9 us
    dot_general x126 -> x0, matrix products: 175 us -> none  [the longest x28 32.5 us: product(): return jnp.dot(left, right, preferred_element_type=F32)]
    pallas_call x17 -> x45, Pallas kernels: 9.61 us -> 89.5 us  [the longest x40 85 us: run(): pl.pallas_call(kernel, out_shape=[jax.ShapeDtypeStruct(shape, kind) for s...]
    ppermute x190 -> x110, waiting for transfers between devices: 378 us -> 302 us  [swap(): lax.ppermute(value, axis, [(i, i ^ mask) for i in range(lax.axis_size(axi...]
    ppermute x190 -> x110, starting transfers between devices: 205 us -> 169 us  [swap(): lax.ppermute(value, axis, [(i, i ^ mask) for i in range(lax.axis_size(axi...]
    convert_element_type x34 -> x18, other arithmetic: 44.5 us -> 15.6 us  [the longest x6 13 us: next(): pick(mine).astype(BF)]
    slice x42 -> x8, local copies, waits for them, and re-layouts: 27.3 us -> 2.11 us  [the longest x1 1.08 us: per_device(): join(dec_whole, b12)[2 * j:2 * j + 2]]
    all_gather x0 -> x3, waiting for transfers between devices: none -> 24.9 us  [ffn_gather(): whole = lax.all_gather(stack, 'fsdp', axis=1, tiled=True)]
    reduce_sum x23 -> x0, other arithmetic: 22.5 us -> none  [the longest x3 10.6 us: attend_forward(): jnp.sum(jnp.exp(scores - height), -1, keepdims=True)]
  transfers between devices with their start and end apart: 202 -> 126, of which waited for: 77 -> 52; matrix products, arithmetic and copies ran while one was open for 32% -> 7% of each run, Pallas kernels for 1% -> 11%
where the time goes in v2:
time: 728 us; the launch traced here: 719 us
  waiting for transfers between devices  331 us (45%)
  starting transfers between devices  190 us (26%)
  Pallas kernels  89.5 us (12%)
  local copies, waits for them, and re-layouts  49.1 us (7%)
  other arithmetic  33.8 us (5%)
  between operations  16.9 us (2%)
  blocking collectives  8.49 us (1%)
    ppermute x110, waiting for transfers between devices, swap(): lax.ppermute(value, axis, [(i, i ^ mask) for i in range(lax.axis_size(axi...  302 us
    ppermute x110, starting transfers between devices, swap(): lax.ppermute(value, axis, [(i, i ^ mask) for i in range(lax.axis_size(axi...  169 us
    pallas_call x40, Pallas kernels, run(): pl.pallas_call(kernel, out_shape=[jax.ShapeDtypeStruct(shape, kind) for s...  85 us
    unnamed x362, local copies, waits for them, and re-layouts  37.4 us
    all_gather x3, waiting for transfers between devices, ffn_gather(): whole = lax.all_gather(stack, 'fsdp', axis=1, tiled=True)  24.9 us
  transfers between devices with their start and end apart: 126, of which 52 were waited for; matrix products, arithmetic and copies ran while one was open for 7% of the time, Pallas kernels for 11%

profile of v2, /device:TPU:0, one launch (start us, length us, event | category | flops | bytes accessed | tf_op | source)
XLA Modules:
  0.0 718.8 jit_solution(6835312670408864105)
XLA Ops:
  25.4 8.5 %all-gather = bf16[256,128]{1,0:T(8,128)(2,1)S(1)} all-gather(bf16[32,128]{1,0:T(8,128)(2,1)S(1)} %pack_small.1), channel_id=2, replica_groups=mesh['fsdp'=8,'tensor'=4] {'fsdp'}, dimensions={0}, use_global_device_ids=true | all-gather | bytes 73728 | tf_op jit(solution)/shard_map/all_gather | solution.py:1042
  60.2 15.6 %collective-permute-done.10 = bf16[2,4,128,256]{3,2,1,0:T(8,128)(2,1)S(1)} collective-permute-done((bf16[2,4,128,256]{3,2,1,0:T(8,128)(2,1)S(1)}, bf16[2,4,128,256]{3,2,1,0:T(8,128)(2,1)S(1)}, u32[]{:S(2)}, u32[]{:S(2)}) %collective-permute-start.10) | collective-permute-done | bytes 524320 | tf_op jit(solution)/shard_map/ppermute | solution.py:24
  80.7 13.5 %collective-permute-done.17 = bf16[128,256]{1,0:T(8,128)(2,1)S(1)} collective-permute-done((bf16[128,256]{1,0:T(8,128)(2,1)S(1)}, bf16[128,256]{1,0:T(8,128)(2,1)S(1)}, u32[]{:S(2)}, u32[]{:S(2)}) %collective-permute-start.17) | collective-permute-done | bytes 65568 | tf_op jit(solution)/shard_map/ppermute | solution.py:24
  115.2 7.3 %collective-permute-done.22 = bf16[128,256]{1,0:T(8,128)(2,1)S(1)} collective-permute-done((bf16[128,256]{1,0:T(8,128)(2,1)S(1)}, bf16[128,256]{1,0:T(8,128)(2,1)S(1)}, u32[]{:S(2)}, u32[]{:S(2)}) %collective-permute-start.22) | collective-permute-done | bytes 65568 | tf_op jit(solution)/shard_map/ppermute | solution.py:24
  138.5 15.8 %collective-permute-done.28 = bf16[2,128,256]{2,1,0:T(8,128)(2,1)} collective-permute-done((bf16[2,128,256]{2,1,0:T(8,128)(2,1)S(1)}, bf16[2,128,256]{2,1,0:T(8,128)(2,1)}, u32[]{:S(2)}, u32[]{:S(2)}) %collective-permute-start.28) | collective-permute-done | bytes 131104 | tf_op jit(solution)/shard_map/ppermute | solution.py:24
  162.6 8.2 %collective-permute-done.27 = bf16[2,4,128,256]{3,2,1,0:T(8,128)(2,1)} collective-permute-done((bf16[2,4,128,256]{3,2,1,0:T(8,128)(2,1)}, bf16[2,4,128,256]{3,2,1,0:T(8,128)(2,1)}, u32[]{:S(2)}, u32[]{:S(2)}) %collective-permute-start.27) | collective-permute-done | bytes 524320 | tf_op jit(solution)/shard_map/ppermute | solution.py:24
  186.7 21.3 %collective-permute-done.40 = bf16[1,10,128,256]{3,2,1,0:T(8,128)(2,1)S(1)} collective-permute-done((bf16[1,10,128,256]{3,2,1,0:T(8,128)(2,1)}, bf16[1,10,128,256]{3,2,1,0:T(8,128)(2,1)S(1)}, u32[]{:S(2)}, u32[]{:S(2)}) %collective-permute-start.40) | collective-permute-done | bytes 655392 | tf_op jit(solution)/shard_map/ppermute | solution.py:24
  210.8 12.8 %all-gather.7.cloned.1.call-done.rest_2_.rest_3_ = bf16[2,1024,1024]{2,1,0:T(8,128)(2,1)} async-done(((bf16[2,128,1024]{2,1,0:T(8,128)(2,1)}), bf16[2,1024,1024]{2,1,0:T(8,128)(2,1)}) %all-gather.7.cloned.1.call-update) | async-done | bytes 4194320 | tf_op jit(solution)/shard_map/all_gather | solution.py:1059
  237.8 7.0 collective-permute-done.41
  251.8 17.5 %collective-permute-done.55 = bf16[2,128,1024]{2,1,0:T(8,128)(2,1)S(1)} collective-permute-done((bf16[2,128,1024]{2,1,0:T(8,128)(2,1)S(1)}, bf16[2,128,1024]{2,1,0:T(8,128)(2,1)S(1)}, u32[]{:S(2)}, u32[]{:S(2)}) %collective-permute-start.55) | collective-permute-done | bytes 524320 | tf_op jit(solution)/shard_map/ppermute | solution.py:24
  317.4 12.0 %all-gather.9.cloned.1.call-done.rest_0_.rest_1_.rest_2_.rest_3_ = bf16[4,1024,1024]{2,1,0:T(8,128)(2,1)} async-done(((bf16[4,128,1024]{2,1,0:T(8,128)(2,1)}), bf16[4,1024,1024]{2,1,0:T(8,128)(2,1)}) %all-gather.9.cloned.1.call-update) | async-done | bytes 8388624 | tf_op jit(solution)/shard_map/all_gather | solution.py:1059
  338.5 7.6 %collective-permute-done.56.rest_2_ = bf16[128,1024]{1,0:T(8,128)(2,1)S(1)} collective-permute-done((bf16[128,1024]{1,0:T(8,128)(2,1)S(1)}, bf16[128,1024]{1,0:T(8,128)(2,1)S(1)}, u32[]{:S(2)}, u32[]{:S(2)}) %collective-permute-start.56) | collective-permute-done | bytes 262176 | tf_op jit(solution)/shard_map/ppermute | solution.py:24
  348.2 8.9 %collective-permute-done.57.other_ref.eo_ref = bf16[128,1024]{1,0:T(8,128)(2,1)S(1)} collective-permute-done((bf16[128,1024]{1,0:T(8,128)(2,1)S(1)}, bf16[128,1024]{1,0:T(8,128)(2,1)S(1)}, u32[]{:S(2)}, u32[]{:S(2)}) %collective-permute-start.57) | collective-permute-done | bytes 262176 | tf_op jit(solution)/shard_map/ppermute | solution.py:24
  416.5 10.1 %collective-permute-start.75 = (bf16[10,2,2,128,256]{4,3,0,2,1:T(8,128)(2,1)}, bf16[10,2,2,128,256]{4,3,0,2,1:T(8,128)(2,1)}, u32[]{:S(2)}, u32[]{:S(2)}) collective-permute-start(bf16[10,2,2,128,256]{4,3,0,2,1:T(8,128)(2,1)} %copy.57), channel_id=1, source_target_pairs={{0,4},{4,0},{8,12},{12,8},{16,20},{20,16},{24,28},{28,24},{1,5},{5... | collective-permute-start | bytes 7864328 | tf_op jit(solution)/shard_map/ppermute | solution.py:24
  450.6 26.1 %collective-permute-start.79 = (bf16[10,2,128,256]{3,2,0,1:T(8,128)(2,1)}, bf16[10,2,128,256]{3,2,0,1:T(8,128)(2,1)}, u32[]{:S(2)}, u32[]{:S(2)}) collective-permute-start(bf16[10,2,128,256]{3,2,0,1:T(8,128)(2,1)} %get-tuple-element.478), channel_id=1, source_target_pairs={{0,16},{4,20},{8,24},{12,28},{16,0},{20,4},{24,8},{28,12},{1,17},{... | collective-permute-start | bytes 3932168 | tf_op jit(solution)/shard_map/ppermute | solution.py:24
  493.6 9.9 %collective-permute-done.79 = bf16[10,2,128,256]{3,2,0,1:T(8,128)(2,1)} collective-permute-done((bf16[10,2,128,256]{3,2,0,1:T(8,128)(2,1)}, bf16[10,2,128,256]{3,2,0,1:T(8,128)(2,1)}, u32[]{:S(2)}, u32[]{:S(2)}) %collective-permute-start.79) | collective-permute-done | bytes 1310752 | tf_op jit(solution)/shard_map/ppermute | solution.py:24
  514.5 7.4 %collective-permute-done.82 = bf16[10,128,256]{2,1,0:T(8,128)(2,1)S(1)} collective-permute-done((bf16[10,128,256]{2,1,0:T(8,128)(2,1)S(1)}, bf16[10,128,256]{2,1,0:T(8,128)(2,1)S(1)}, u32[]{:S(2)}, u32[]{:S(2)}) %collective-permute-start.82) | collective-permute-done | bytes 655392 | tf_op jit(solution)/shard_map/ppermute | solution.py:24
  589.2 11.3 %collective-permute-done.95 = bf16[128,1024]{1,0:T(8,128)(2,1)S(1)} collective-permute-done((bf16[128,1024]{1,0:T(8,128)(2,1)S(1)}, bf16[128,1024]{1,0:T(8,128)(2,1)S(1)}, u32[]{:S(2)}, u32[]{:S(2)}) %collective-permute-start.95) | collective-permute-done | bytes 262176 | tf_op jit(solution)/shard_map/ppermute | solution.py:24
  613.4 13.6 %collective-permute-done.112 = bf16[2,128,2048]{2,1,0:T(8,128)(2,1)S(1)} collective-permute-done((bf16[2,128,2048]{2,1,0:T(8,128)(2,1)S(1)}, bf16[2,128,2048]{2,1,0:T(8,128)(2,1)S(1)}, u32[]{:S(2)}, u32[]{:S(2)}) %collective-permute-start.112) | collective-permute-done | bytes 1048608 | tf_op jit(solution)/shard_map/ppermute | solution.py:24
  627.0 9.8 %collective-permute-done.116 = bf16[7,128,256]{2,1,0:T(8,128)(2,1)S(1)} collective-permute-done((bf16[7,128,256]{2,1,0:T(8,128)(2,1)S(1)}, bf16[7,128,256]{2,1,0:T(8,128)(2,1)S(1)}, u32[]{:S(2)}, u32[]{:S(2)}) %collective-permute-start.116) | collective-permute-done | bytes 458784 | tf_op jit(solution)/shard_map/ppermute | solution.py:24
  649.6 9.7 %collective-permute-done.111 = bf16[128,2048]{1,0:T(8,128)(2,1)S(1)} collective-permute-done((bf16[128,2048]{1,0:T(8,128)(2,1)S(1)}, bf16[128,2048]{1,0:T(8,128)(2,1)S(1)}, u32[]{:S(2)}, u32[]{:S(2)}) %collective-permute-start.111) | collective-permute-done | bytes 524320 | tf_op jit(solution)/shard_map/ppermute | solution.py:24
  670.2 8.1 %collective-permute-done.102 = bf16[128,256]{1,0:T(8,128)(2,1)} collective-permute-done((bf16[128,256]{1,0:T(8,128)(2,1)}, bf16[128,256]{1,0:T(8,128)(2,1)}, u32[]{:S(2)}, u32[]{:S(2)}) %collective-permute-start.102) | collective-permute-done | bytes 65568 | tf_op jit(solution)/shard_map/ppermute | solution.py:24
  678.3 22.0 %collective-permute-done.104 = bf16[128,256]{1,0:T(8,128)(2,1)} collective-permute-done((bf16[128,256]{1,0:T(8,128)(2,1)}, bf16[128,256]{1,0:T(8,128)(2,1)}, u32[]{:S(2)}, u32[]{:S(2)}) %collective-permute-start.104) | collective-permute-done | bytes 65568 | tf_op jit(solution)/shard_map/ppermute | solution.py:24
  703.2 7.5 %collective-permute-done.121 = bf16[2,128,1024]{2,1,0:T(8,128)(2,1)S(1)} collective-permute-done((bf16[2,128,1024]{2,1,0:T(8,128)(2,1)S(1)}, bf16[2,128,1024]{2,1,0:T(8,128)(2,1)S(1)}, u32[]{:S(2)}, u32[]{:S(2)}) %collective-permute-start.121) | collective-permute-done | bytes 524320 | tf_op jit(solution)/shard_map/ppermute | solution.py:24
  (719 shorter events, 410.2 us)
Async XLA Ops:
  7.2 203.6 %all-gather.5.cloned.1.call-start = ((), (), s32[]{:S(2)}) async-start(), calls=%async_computation.1 | async-start | bytes 4718592 | tf_op jit(solution)/shard_map/all_gather | solution.py:1059
  115.1 108.5 %all-gather.7.cloned.1.call-start = ((), (), s32[]{:S(2)}) async-start(), calls=%async_computation.2 | async-start | bytes 4718592 | tf_op jit(solution)/shard_map/all_gather | solution.py:1059
  122.9 33.2 %collective-permute-start.38 = (bf16[2,128,1024]{2,1,0:T(8,128)(2,1)}, bf16[2,128,1024]{2,1,0:T(8,128)(2,1)}, u32[]{:S(2)}, u32[]{:S(2)}) collective-permute-start(bf16[2,128,1024]{2,1,0:T(8,128)(2,1)} %param.32), channel_id=1, source_target_pairs={{0,2},{1,3},{2,0},{3,1},{4,6},{5,7},{6,4},{7,5},{8,10},{9,11},{10,... | collective-permute-start | bytes 1572872 | tf_op jit(solution)/shard_map/ppermute | solution.py:24
  154.3 56.4 %collective-permute-start.37 = (bf16[128,1024]{1,0:T(8,128)(2,1)S(1)}, bf16[128,1024]{1,0:T(8,128)(2,1)S(1)}, u32[]{:S(2)}, u32[]{:S(2)}) collective-permute-start(bf16[128,1024]{1,0:T(8,128)(2,1)S(1)} %get-tuple-element.291.own_ref.x_ref), channel_id=1, source_target_pairs={{0,1},{1,0},{2,3},{3,2},{4,5},{5,4},{6,7},{7,6},{8,9},{9,8},{10,11... | collective-permute-start | bytes 786440 | tf_op jit(solution)/shard_map/ppermute | solution.py:24
  176.6 152.8 %all-gather.9.cloned.1.call-start = ((), (), s32[]{:S(2)}) async-start(), calls=%async_computation.3 | async-start | bytes 9437184 | tf_op jit(solution)/shard_map/all_gather | solution.py:1059
  209.3 35.5 %collective-permute-start.41 = (bf16[2,10,128,256]{3,2,1,0:T(8,128)(2,1)}, bf16[2,10,128,256]{3,2,1,0:T(8,128)(2,1)S(1)}, u32[]{:S(2)}, u32[]{:S(2)}) collective-permute-start(bf16[2,10,128,256]{3,2,1,0:T(8,128)(2,1)} %pad_maximum_fusion.1), channel_id=1, source_target_pairs={{0,16},{4,20},{8,24},{12,28},{16,0},{20,4},{24,8},{28,12},{1,17},{... | collective-permute-start | bytes 3932168 | tf_op jit(solution)/shard_map/ppermute | solution.py:24
  236.8 32.6 %collective-permute-start.55 = (bf16[2,128,1024]{2,1,0:T(8,128)(2,1)S(1)}, bf16[2,128,1024]{2,1,0:T(8,128)(2,1)S(1)}, u32[]{:S(2)}, u32[]{:S(2)}) collective-permute-start(bf16[2,128,1024]{2,1,0:T(8,128)(2,1)S(1)} %copy-done.165), channel_id=1, source_target_pairs={{0,2},{1,3},{2,0},{3,1},{4,6},{5,7},{6,4},{7,5},{8,10},{9,11},{10,... | collective-permute-start | bytes 1572872 | tf_op jit(solution)/shard_map/ppermute | solution.py:24
  270.4 396.7 %reduce-scatter.2.cloned.1.call-start = ((), (), s32[]{:S(2)}) async-start(), calls=%async_computation.4 | async-start | bytes 9437184 | tf_op jit(solution)/shard_map/reduce_scatter | solution.py:1208
  441.7 34.9 %collective-permute-start.76 = (bf16[128,1024]{1,0:T(8,128)(2,1)S(1)}, bf16[128,1024]{1,0:T(8,128)(2,1)S(1)}, u32[]{:S(2)}, u32[]{:S(2)}) collective-permute-start(bf16[128,1024]{1,0:T(8,128)(2,1)S(1)} %get-tuple-element.386.own_ref.e_ref), channel_id=1, source_target_pairs={{0,1},{1,0},{2,3},{3,2},{4,5},{5,4},{6,7},{7,6},{8,9},{9,8},{10,11... | collective-permute-start | bytes 786440 | tf_op jit(solution)/shard_map/ppermute | solution.py:24
  443.7 39.7 %collective-permute-start.77 = (bf16[128,1024]{1,0:T(8,128)(2,1)S(1)}, bf16[128,1024]{1,0:T(8,128)(2,1)S(1)}, u32[]{:S(2)}, u32[]{:S(2)}) collective-permute-start(bf16[128,1024]{1,0:T(8,128)(2,1)S(1)} %get-tuple-element.389), channel_id=1, source_target_pairs={{0,1},{1,0},{2,3},{3,2},{4,5},{5,4},{6,7},{7,6},{8,9},{9,8},{10,11... | collective-permute-start | bytes 786440 | tf_op jit(solution)/shard_map/ppermute | solution.py:24
  445.1 48.5 %collective-permute-start.78 = (bf16[128,1024]{1,0:T(8,128)(2,1)S(1)}, bf16[128,1024]{1,0:T(8,128)(2,1)}, u32[]{:S(2)}, u32[]{:S(2)}) collective-permute-start(bf16[128,1024]{1,0:T(8,128)(2,1)S(1)} %get-tuple-element.390), channel_id=1, source_target_pairs={{0,1},{1,0},{2,3},{3,2},{4,5},{5,4},{6,7},{7,6},{8,9},{9,8},{10,11... | collective-permute-start | bytes 786440 | tf_op jit(solution)/shard_map/ppermute | solution.py:24
  450.6 53.0 %collective-permute-start.79 = (bf16[10,2,128,256]{3,2,0,1:T(8,128)(2,1)}, bf16[10,2,128,256]{3,2,0,1:T(8,128)(2,1)}, u32[]{:S(2)}, u32[]{:S(2)}) collective-permute-start(bf16[10,2,128,256]{3,2,0,1:T(8,128)(2,1)} %get-tuple-element.478), channel_id=1, source_target_pairs={{0,16},{4,20},{8,24},{12,28},{16,0},{20,4},{24,8},{28,12},{1,17},{... | collective-permute-start | bytes 3932168 | tf_op jit(solution)/shard_map/ppermute | solution.py:24
  483.5 40.0 %collective-permute-start.81 = (bf16[128,1024]{1,0:T(8,128)(2,1)S(1)}, bf16[128,1024]{1,0:T(8,128)(2,1)}, u32[]{:S(2)}, u32[]{:S(2)}) collective-permute-start(bf16[128,1024]{1,0:T(8,128)(2,1)S(1)} %add_convert_fusion.13), channel_id=1, source_target_pairs={{0,2},{1,3},{2,0},{3,1},{4,6},{5,7},{6,4},{7,5},{8,10},{9,11},{10,... | collective-permute-start | bytes 786440 | tf_op jit(solution)/shard_map/ppermute | solution.py:24
  521.9 30.8 %collective-permute-start.86 = (bf16[2,2,128,2048]{3,2,1,0:T(8,128)(2,1)S(1)}, bf16[2,2,128,2048]{3,2,1,0:T(8,128)(2,1)}, u32[]{:S(2)}, u32[]{:S(2)}) collective-permute-start(bf16[2,2,128,2048]{3,2,1,0:T(8,128)(2,1)S(1)} %bitcast.214), channel_id=1, source_target_pairs={{0,4},{4,0},{8,12},{12,8},{16,20},{20,16},{24,28},{28,24},{1,5},{5... | collective-permute-start | bytes 6291464 | tf_op jit(solution)/shard_map/ppermute | solution.py:24
  548.8 55.1 %collective-permute-start.115 = (bf16[7,2,128,256]{3,2,0,1:T(8,128)(2,1)}, bf16[7,2,128,256]{3,2,0,1:T(8,128)(2,1)S(1)}, u32[]{:S(2)}, u32[]{:S(2)}) collective-permute-start(bf16[7,2,128,256]{3,2,0,1:T(8,128)(2,1)} %get-tuple-element.482), channel_id=1, source_target_pairs={{0,8},{4,12},{8,0},{12,4},{16,24},{20,28},{24,16},{28,20},{1,9},{5... | collective-permute-start | bytes 2752520 | tf_op jit(solution)/shard_map/ppermute | solution.py:24
  554.5 32.2 %collective-permute-start.93 = (bf16[128,1024]{1,0:T(8,128)(2,1)S(1)}, bf16[128,1024]{1,0:T(8,128)(2,1)S(1)}, u32[]{:S(2)}, u32[]{:S(2)}) collective-permute-start(bf16[128,1024]{1,0:T(8,128)(2,1)S(1)} %get-tuple-element.428), channel_id=1, source_target_pairs={{0,1},{1,0},{2,3},{3,2},{4,5},{5,4},{6,7},{7,6},{8,9},{9,8},{10,11... | collective-permute-start | bytes 786440 | tf_op jit(solution)/shard_map/ppermute | solution.py:24
  558.2 46.5 %collective-permute-start.99 = (bf16[4,2,2,128,256]{4,3,0,2,1:T(8,128)(2,1)S(1)}, bf16[4,2,2,128,256]{4,3,0,2,1:T(8,128)(2,1)S(1)}, u32[]{:S(2)}, u32[]{:S(2)}) collective-permute-start(bf16[4,2,2,128,256]{4,3,0,2,1:T(8,128)(2,1)S(1)} %copy.66), channel_id=1, source_target_pairs={{0,4},{4,0},{8,12},{12,8},{16,20},{20,16},{24,28},{28,24},{1,5},{5... | collective-permute-start | bytes 3145736 | tf_op jit(solution)/shard_map/ppermute | solution.py:24
  604.0 32.9 %collective-permute-start.116 = (bf16[7,128,256]{2,1,0:T(8,128)(2,1)S(1)}, bf16[7,128,256]{2,1,0:T(8,128)(2,1)S(1)}, u32[]{:S(2)}, u32[]{:S(2)}) collective-permute-start(bf16[7,128,256]{2,1,0:T(8,128)(2,1)S(1)} %fusion.27), channel_id=1, source_target_pairs={{0,16},{4,20},{8,24},{12,28},{16,0},{20,4},{24,8},{28,12},{1,17},{... | collective-permute-start | bytes 1376264 | tf_op jit(solution)/shard_map/ppermute | solution.py:24
  604.3 37.7 %collective-permute-start.97 = (bf16[3,2,128,256]{3,2,0,1:T(8,128)(2,1)S(1)}, bf16[3,2,128,256]{3,2,0,1:T(8,128)(2,1)S(1)}, u32[]{:S(2)}, u32[]{:S(2)}) collective-permute-start(bf16[3,2,128,256]{3,2,0,1:T(8,128)(2,1)S(1)} %get-tuple-element.490), channel_id=1, source_target_pairs={{0,8},{4,12},{8,0},{12,4},{16,24},{20,28},{24,16},{28,20},{1,9},{5... | collective-permute-start | bytes 1179656 | tf_op jit(solution)/shard_map/ppermute | solution.py:24
  605.0 44.2 %collective-permute-start.100 = (bf16[4,2,128,256]{3,2,0,1:T(8,128)(2,1)S(1)}, bf16[4,2,128,256]{3,2,0,1:T(8,128)(2,1)S(1)}, u32[]{:S(2)}, u32[]{:S(2)}) collective-permute-start(bf16[4,2,128,256]{3,2,0,1:T(8,128)(2,1)S(1)} %get-tuple-element.486), channel_id=1, source_target_pairs={{0,16},{4,20},{8,24},{12,28},{16,0},{20,4},{24,8},{28,12},{1,17},{... | collective-permute-start | bytes 1572872 | tf_op jit(solution)/shard_map/ppermute | solution.py:24
  611.6 47.7 %collective-permute-start.111 = (bf16[128,2048]{1,0:T(8,128)(2,1)S(1)}, bf16[128,2048]{1,0:T(8,128)(2,1)S(1)}, u32[]{:S(2)}, u32[]{:S(2)}) collective-permute-start(bf16[128,2048]{1,0:T(8,128)(2,1)S(1)} %fusion.21), channel_id=1, source_target_pairs={{0,16},{4,20},{8,24},{12,28},{16,0},{20,4},{24,8},{28,12},{1,17},{... | collective-permute-start | bytes 1572872 | tf_op jit(solution)/shard_map/ppermute | solution.py:24
  661.4 40.7 %collective-permute-start.114 = (bf16[2,128,1024]{2,1,0:T(8,128)(2,1)}, bf16[2,128,1024]{2,1,0:T(8,128)(2,1)S(1)}, u32[]{:S(2)}, u32[]{:S(2)}) collective-permute-start(bf16[2,128,1024]{2,1,0:T(8,128)(2,1)} %fusion.7), channel_id=1, source_target_pairs={{0,2},{1,3},{2,0},{3,1},{4,6},{5,7},{6,4},{7,5},{8,10},{9,11},{10,... | collective-permute-start | bytes 1572872 | tf_op jit(solution)/shard_map/ppermute | solution.py:24
  666.0 34.3 %collective-permute-start.104 = (bf16[128,256]{1,0:T(8,128)(2,1)}, bf16[128,256]{1,0:T(8,128)(2,1)}, u32[]{:S(2)}, u32[]{:S(2)}) collective-permute-start(bf16[128,256]{1,0:T(8,128)(2,1)} %fusion.45), channel_id=1, source_target_pairs={{0,2},{1,3},{2,0},{3,1},{4,6},{5,7},{6,4},{7,5},{8,10},{9,11},{10,... | collective-permute-start | bytes 196616 | tf_op jit(solution)/shard_map/ppermute | solution.py:24
  668.2 42.5 %collective-permute-start.121 = (bf16[2,128,1024]{2,1,0:T(8,128)(2,1)S(1)}, bf16[2,128,1024]{2,1,0:T(8,128)(2,1)S(1)}, u32[]{:S(2)}, u32[]{:S(2)}) collective-permute-start(bf16[2,128,1024]{2,1,0:T(8,128)(2,1)S(1)} %slice.150), channel_id=1, source_target_pairs={{0,2},{1,3},{2,0},{3,1},{4,6},{5,7},{6,4},{7,5},{8,10},{9,11},{10,... | collective-permute-start | bytes 1572872 | tf_op jit(solution)/shard_map/ppermute | solution.py:24
  (278 other events, 3279.5 us)
Sparse Core Ops, SparseCore 0:
  115.3 47.6 all-gather.4
  176.7 46.8 all-gather.6
  270.5 58.8 all-gather.8
  380.4 85.3 reduce-scatter.1

commit v3 on v2

--- a/solution.py
+++ b/solution.py
@@ -56,7 +56,14 @@
 def placed(parts, index, splits):
     arrays = [array for array, masks in parts]
     total = sum(len(masks) for array, masks in parts)
-    rows, cols = arrays[0].shape[2:]
+    cols = arrays[0].shape[-1]
+    shapes = [
+        (width, total, arrays[0].shape[2], cols)
+        if isinstance(width, int)
+        else (width[0], total, width[1], cols)
+        for width in splits
+    ]
+    moves_ = total * sum(1 if isinstance(width, int) else width[0] for width in splits)
 
     def kernel(index_ref, *refs):
         ins, outs, sems = refs[: len(parts)], refs[len(parts) : -1], refs[-1]
@@ -65,26 +72,30 @@
             for at, mask in enumerate(masks):
                 first = 0
                 for out, width in zip(outs, splits):
-                    copy = pltpu.make_async_copy(
-                        ref.at[at, first : first + width],
-                        out.at[:, index_ref[0] ^ mask],
-                        sems.at[len(copies)],
-                    )
-                    copy.start()
-                    copies.append(copy)
-                    first += width
+                    if isinstance(width, int):
+                        moves = [(ref.at[at, first : first + width], out.at[:, index_ref[0] ^ mask])]
+                        first += width
+                    else:
+                        moves = []
+                        for line in range(width[0]):
+                            moves.append(
+                                (ref.at[at, first : first + width[1]], out.at[line, index_ref[0] ^ mask])
+                            )
+                            first += width[1]
+                    for source, target in moves:
+                        copy = pltpu.make_async_copy(source, target, sems.at[len(copies)])
+                        copy.start()
+                        copies.append(copy)
         for copy in copies:
             copy.wait()
 
     outs = pl.pallas_call(
         kernel,
-        out_shape=[
-            jax.ShapeDtypeStruct((width, total, rows, cols), arrays[0].dtype) for width in splits
-        ],
+        out_shape=[jax.ShapeDtypeStruct(shape, arrays[0].dtype) for shape in shapes],
         in_specs=[pl.BlockSpec(memory_space=pltpu.SMEM)]
         + [pl.BlockSpec(memory_space=pl.ANY)] * len(arrays),
         out_specs=[pl.BlockSpec(memory_space=pltpu.VMEM)] * len(splits),
-        scratch_shapes=[pltpu.SemaphoreType.DMA((total * len(splits),))],
+        scratch_shapes=[pltpu.SemaphoreType.DMA((moves_,))],
         compiler_params=pltpu.CompilerParams(vmem_limit_bytes=32 * 2**20),
         cost_estimate=pl.CostEstimate(flops=PACE, bytes_accessed=1, transcendentals=0),
         name="placed",
@@ -94,6 +105,13 @@
 
 def gather_plane(shard, order, splits):
     return Gather(shard[None], order, splits).result()
+
+
+def reach(value, axis, masks):
+    pieces = {0: value}
+    for mask in masks:
+        pieces[mask] = swap(value, axis, mask)
+    return [pieces[mask] for mask in sorted(pieces)]
 
 
 class Gather:
@@ -146,29 +164,28 @@
 
 class Share:
     def __init__(self, pieces, axis, bits):
-        self.axis, self.held, self.came, self.level = axis, dict(enumerate(pieces)), {}, len(bits)
-        self.terms = [pieces[0]]
+        self.axis, self.held, self.bits = axis, dict(enumerate(pieces)), list(bits)
+        self.came, self.terms = None, [pieces[0]]
 
     def hop(self, *gate):
-        for mask, arrays in self.came.items():
-            for array in arrays:
-                self.held[mask] = self.held[mask].astype(F32) + join(array, *gate).astype(F32)
-        self.came = {}
-        new = []
-        for mask in sorted(self.held)[::-1]:
-            if mask and (mask.bit_count() == self.level or mask == 1):
-                low = mask & -mask
-                came = swap(self.held.pop(mask).astype(BF), self.axis, low)
-                if mask == low:
-                    self.terms.append(came)
+        if self.came is not None:
+            came = join(self.came, *gate)
+            for at, mask in enumerate(self.kept):
+                if mask == 0:
+                    self.terms.append(came[at])
                 else:
-                    self.came.setdefault(mask ^ low, []).append(came)
-                new.append(came)
-        self.level -= 1
-        return new
+                    self.held[mask] = self.held[mask].astype(F32) + came[at].astype(F32)
+            self.came = None
+        if self.bits:
+            bit = self.bits.pop(0)
+            sent = [mask for mask in sorted(self.held) if mask & bit]
+            self.kept = [mask ^ bit for mask in sent]
+            stack = jnp.stack([self.held.pop(mask).astype(BF) for mask in sent])
+            self.came = swap(stack, self.axis, bit)
+        return self.came
 
     def result(self):
-        while self.level > 0:
+        while self.bits or self.came is not None:
             self.hop()
         return self.terms
 
@@ -255,7 +272,7 @@
 def place_rows(ref, pieces, t_index):
     rows = pieces[0].shape[0]
     for mask, piece in enumerate(pieces):
-        ref[pl.ds(multiple((t_index ^ mask) * rows, rows), rows), :] = piece[...]
+        ref[pl.ds(multiple((t_index ^ mask) * rows, rows), rows), :] = piece[:, : ref.shape[1]]
 
 
 def attend(queries, windows, meta, bounds, t_index, count, ranges):
@@ -410,7 +427,7 @@
 
 def project(pieces, weights, local, lines, t_index):
     count = len(pieces)
-    rows, depth = pieces[0].shape
+    rows, depth = pieces[0].shape[0], weights.shape[1]
     tokens, width = rows * count, weights.shape[2]
     outputs = weights.shape[0]
 
@@ -497,24 +514,25 @@
 
 
 def ffn_blocks(views, rows, depth, hidden):
-    step = min(512 // len(views) if len(views) < 4 else 128, hidden)
+    step = views[0][0].shape[2]
     row = pl.BlockSpec((rows, depth), lambda j: (0, 0))
 
-    def weight(index):
-        return pl.BlockSpec((1, depth, step), lambda j: (index, 0, j))
+    def weight(first):
+        return pl.BlockSpec((1, depth, step), lambda j: (first + j, 0, 0))
 
     tall = pl.BlockSpec((len(views), 2 * rows, step), lambda j: (0, 0, j))
     line = pl.BlockSpec((len(views), 1, step), lambda j: (0, 0, j))
     specs, arrays = [], []
-    for array, up, down in views:
-        specs += [weight(up), weight(down)]
-        arrays += [array, array]
+    for up, up_first, down, down_first in views:
+        specs += [weight(up_first), weight(down_first)]
+        arrays += [up, down]
     return step, row, tall, line, specs, arrays
 
 
 def ffn_up_down(own, other, views, first):
     rows, depth = own.shape
-    hidden, count = views[0][0].shape[2], len(views)
+    hidden = first.shape[2]
+    count = len(views)
     step, row, tall, line, specs, arrays = ffn_blocks(views, rows, depth, hidden)
 
     def kernel(own_ref, other_ref, b_ref, *rest):
@@ -561,7 +579,8 @@
 
 def ffn_down_up(own, other, views, slope):
     rows, depth = own.shape
-    hidden, count = views[0][0].shape[2], len(views)
+    hidden = slope.shape[2]
+    count = len(views)
     step, row, tall, line, specs, arrays = ffn_blocks(views, rows, depth, hidden)
 
     def kernel(own_ref, other_ref, slope_ref, *rest):
@@ -844,24 +863,29 @@
             lines.append(value)
         used = sum(value.shape[0] for value in lines)
         lines.append(jnp.zeros((LINES - used, width), F32))
-        refs[-1][...] = jnp.concatenate(lines, 0).astype(BF)
+        whole = jnp.concatenate(lines, 0)
+        refs[-1][...] = jnp.concatenate([whole[: LINES // 2], whole[LINES // 2 :]], 1).astype(BF)
 
     blocks = [pl.BlockSpec(array.shape, lambda i: (0, 0)) for array in arrays]
-    return run(
-        kernel, [], arrays, [((LINES, width), BF)], [], "pack_small", 0, (1,), blocks,
-        [pl.BlockSpec((LINES, width), lambda i: (0, 0))],
+    shape = (LINES // 2, 2 * width)
+    return run(
+        kernel, [], arrays, [(shape, BF)], [], "pack_small", 0, (1,), blocks,
+        [pl.BlockSpec(shape, lambda i: (0, 0))],
     )[0]
 
 
 def unpack_small(parts, t_index, count, features, wide_masks):
-    peers, lines, width = parts.shape
+    peers, lines, width = parts.shape[0], LINES, parts.shape[2] // 2
     share_ = peers // count
     quarter = 4
     hidden = share_ * quarter * width
 
     def kernel(t_ref, x_ref, table, local, enc_ref, dec_ref):
         for f in range(peers):
-            table[:, f * width : (f + 1) * width] = x_ref[f].astype(F32)
+            value = x_ref[f].astype(F32)
+            span = slice(f * width, (f + 1) * width)
+            table[: lines // 2, span] = value[:, :width]
+            table[lines // 2 :, span] = value[:, width:]
         for mask in range(count):
             local[mask] = table[:, pl.ds(multiple((t_ref[0] ^ mask) * features, 128), features)]
         for ref, first in ((enc_ref, ENC_FIRST), (dec_ref, DEC_FIRST)):
@@ -1034,15 +1058,12 @@
     wide_up = t_up[1:]
     t_masks = range(tensor_size)
     wide_masks = range(0, tensor_size, 2)
+    wide_count = len(wide_masks)
 
     small = [
         enc_attn_bias, enc_attn_norm, enc_ffn_vec, self_attn_bias, self_attn_norm,
         cross_attn_bias, cross_attn_norm, dec_ffn_vec, enc_ffn_b1, dec_ffn_b1,
     ]
-    parts = lax.all_gather(pack_small(small, enc_attn_bias.shape[1]), "fsdp", axis=0)
-    table, local, enc_first, dec_first = unpack_small(
-        parts, t_ref, tensor_size, features, wide_masks
-    )
     block = min(256, tokens)
     base = (f_index * tokens)[None].astype(jnp.int32)
     spans = token_spans(seq_lens, pic_start, pic_len, base, tokens, block)
@@ -1054,13 +1075,61 @@
     def later(value, ready):
         return lax.optimization_barrier((value, ready))[0]
 
-    def ffn_gather(shards):
-        stack = shards[0] if len(shards) == 1 else jnp.concatenate(shards)
-        whole = lax.all_gather(stack, "fsdp", axis=1, tiled=True)
-        return [(whole, 2 * i, 2 * i + 1) for i in range(len(shards))]
+    class Pair:
+        def __init__(self, halves, splits):
+            self.plans = [
+                Gather(half[None], order, split)
+                for half, order, split in zip(halves, (first_order, second_order), splits)
+            ]
+
+        def hop(self, *gate):
+            if self.plans[0].came is not None:
+                came_ = join([plan.came for plan in self.plans], *gate)
+                for plan, value in zip(self.plans, came_):
+                    plan.came = value
+                gate = ()
+            return [plan.hop(*gate) for plan in self.plans]
+
+        def result(self):
+            return [plan.result() for plan in self.plans]
+
+    slices = hidden // features
+
+    def ffn_slices(shard):
+        cut = shard.reshape(2, rows, slices, features)
+        return jnp.moveaxis(cut, 2, 1).reshape(2 * slices, rows, features)
+
+    def ffn_halves(shards):
+        cut = [ffn_slices(shard) for shard in shards]
+        half = (wide_count + 1) // 2
+        return cut[:half], cut[half:]
+
+    def ffn_views(low, high):
+        views = []
+        for array in (low, high):
+            for at in range(0, array.shape[0], 2 * slices):
+                views.append((array, at, array, at + slices))
+        return views
 
     def exchange(pieces_):
-        return [pieces_[0]] + [swap(pieces_[mask], "tensor", mask) for mask in t_masks[1:]]
+        held = dict(enumerate(pieces_))
+        for bit in t_up:
+            moved = [mask for mask in t_masks if mask & bit]
+            came_ = swap(jnp.stack([held[mask] for mask in moved]), "tensor", bit)
+            for at, mask in enumerate(moved):
+                held[mask] = came_[at]
+        return [held[mask] for mask in t_masks]
+
+    def doubled(value):
+        held = {0: value}
+        for bit in t_down:
+            known = sorted(held)
+            came_ = swap(jnp.stack([held[mask] for mask in known]), "tensor", bit)
+            gate = yield came_
+            came_ = join(came_, *(gate or ()))
+            for at, mask in enumerate(known):
+                held[mask | bit] = came_[at]
+        yield [held[mask] for mask in t_masks]
 
     peers = fsdp_size
     up_pairs = [(i, i + 1) for i in range(peers - 1)]
@@ -1079,6 +1148,73 @@
             queries, window, grads, mixed_t, totals, mode[0], mode[1], t_ref, tensor_size, mode[2]
         )
 
+    class Folds:
+        def __init__(self, parts_, at):
+            self.folds = [
+                Fold(parts_[2 * k], parts_[2 * k + 1], order[:-1], at)
+                for k, order in enumerate((first_order, second_order))
+            ]
+
+        def hop(self, *gate):
+            return [fold.hop(*gate) for fold in self.folds]
+
+        def next(self, *gate):
+            came_ = join([fold.came for fold in self.folds], *gate)
+            for fold, value in zip(self.folds, came_):
+                fold.came = value
+            return [fold.next() for fold in self.folds]
+
+        def result(self, *gate):
+            return [fold.result(*gate) for fold in self.folds]
+
+    class SmallSum:
+        def __init__(self, value):
+            self.value, self.came = value, None
+            self.bits = [("fsdp", bit) for bit in bits_of("fsdp")[::-1]]
+            self.bits += [("tensor", bit) for bit in t_up]
+
+        def hop(self):
+            if self.came is not None:
+                self.value = self.value + self.came
+            axis, bit = self.bits.pop(0)
+            sent = self.value
+            if axis == "fsdp":
+                half = self.value.shape[0] // 2
+                mine = (f_index // bit) % 2
+                sent = lax.dynamic_slice_in_dim(self.value, (1 - mine) * half, half, 0)
+                self.value = lax.dynamic_slice_in_dim(self.value, mine * half, half, 0)
+            self.came = swap(sent, axis, bit)
+
+        def result(self):
+            while self.bits:
+                self.hop()
+            return [self.value[0], self.came[0]]
+
+    class WideShare:
+        def __init__(self, halves):
+            self.held = {
+                mask: halves[:, :, j * hidden : (j + 1) * hidden]
+                for j, mask in enumerate(wide_masks)
+            }
+            self.bits = list(wide_up)
+
+        def hop(self):
+            bit = self.bits.pop(0)
+            new = []
+            for mask in sorted(self.held):
+                if mask not in self.held or mask & (2 * bit - 1):
+                    continue
+                came_ = swap(self.held.pop(mask | bit).astype(BF), "tensor", bit)
+                self.held[mask] = self.held[mask] + came_.astype(F32)
+                new.append(came_)
+            self.came = new
+            return new
+
+        def result(self):
+            while self.bits:
+                self.hop()
+            return self.held[0]
+
     pending = [[], []]
 
     def due(*values):
@@ -1089,105 +1225,113 @@
         pending.append([])
         return join(value, *waits)
 
-    enc_pieces = spread(enc_in, "tensor", t_down)
-    (enc_qkv,) = gather_plane(enc_attn_w[:3], first_order, [3])
-    enc_out_shards = jnp.stack(spread(enc_attn_w[3], "tensor", t_down))[None]
-    enc_own_views = ffn_gather([join(enc_ffn_w, enc_qkv)])
-    plan = Gather(enc_out_shards, second_order, [tensor_size])
-    due(plan.hop())
+    packed = pack_small(small, enc_attn_bias.shape[1])
+    depth = enc_in.shape[1]
+    enc_pieces = reach(
+        jnp.concatenate([enc_in, enc_attn_w[3]], 1), "tensor", t_masks[:0:-1]
+    )
+    first_shard = jnp.concatenate([enc_attn_w[:3].reshape(-1, features), packed])
+    qkv_plan = Gather(first_shard[None], first_order, [(3, rows), (1, packed.shape[0])])
+    qkv_plan.hop()
+    enc_qkv, parts = qkv_plan.result()
+    table, local, enc_first, dec_first = unpack_small(
+        parts.reshape(fsdp_size, -1, features), t_ref, tensor_size, features, wide_masks
+    )
+    plan1 = Pair(
+        (self_attn_w[:3], jnp.stack([piece[:, depth:] for piece in enc_pieces])),
+        ([3], [tensor_size]),
+    )
+    due(plan1.hop())
+    dec_steps = doubled(
+        join(
+            jnp.concatenate([dec_in, self_attn_w[3], cross_attn_w[3], cross_attn_w[0]], 1),
+            *enc_pieces[1:],
+        )
+    )
+    due(next(dec_steps))
+
     flat_e, pair_e, query_e = project(
-        enc_pieces, fg(enc_qkv), local, (ENC_ATT, None, ENC_ATT + 1), t_ref
-    )
-    k1 = query_e
+        fg(enc_pieces), enc_qkv, local, (ENC_ATT, None, ENC_ATT + 1), t_ref
+    )
     window_e = halo(pair_e)
-    due(plan.hop(k1))
-    self_plan = Gather(join(self_attn_w[:3], k1)[None], first_order, [3])
-    due(self_plan.hop())
-    dec_spread = Spread(join(dec_in, k1), "tensor", t_down)
-    due(*dec_spread.hop())
-    self_spread = Spread(join(self_attn_w[3], k1), "tensor", t_down)
-    due(*self_spread.hop())
+    r1 = (window_e[0], window_e[2])
+    plan1.hop(*r1)
+    dec_pieces = dec_steps.send(r1)
 
     mixed_e, mixed_t_e, totals_e = attend_fg(fg(query_e), window_e, both)
-    k2 = totals_e
     mixed_e = exchange(mixed_e)
-    plan.hop(k2)
-    (enc_out_w,) = plan.result()
-    due(*dec_spread.hop(k2), *self_spread.hop(k2))
-    due(self_plan.hop(k2))
+    r2 = tuple(mixed_e[1:])
+    plan1.hop(*r2)
+    (self_qkv,), (enc_out_w,) = plan1.result()
+    enc_wide = Spread(join(enc_ffn_w, *r2), "tensor", wide_down)
+    enc_wide.hop()
+    for step in range(len(t_down) - 1):
+        dec_pieces = dec_steps.send(r2)
 
     summed_e, hid, hid_low = out_norm(
-        [fg(mixed_e[0])] + mixed_e[1:], enc_out_w, enc_in, table, ENC_ATT + 2
-    )
-    k3 = hid_low
+        fg(mixed_e), enc_out_w, enc_in, table, ENC_ATT + 2
+    )
     hid_other = swap(hid_low, "tensor", 1)
-    self_plan.hop(k3)
-    (self_qkv,) = self_plan.result()
-    dec_pieces = dec_spread.result()
-    self_out_plan = Gather(
-        jnp.stack(self_spread.result(k3))[None], second_order, [tensor_size]
-    )
-    due(self_out_plan.hop())
-    enc_wide = Spread(join(enc_ffn_w, k3), "tensor", wide_down)
-    enc_wide.hop()
-    cross_spread = Spread(
-        join(jnp.stack([cross_attn_w[3], cross_attn_w[0]]), k3), "tensor", t_down
-    )
-    due(*cross_spread.hop())
-
+    r3 = (hid_other,)
     flat_s, pair_s, query_s = project(
-        fg(dec_pieces), self_qkv, local, (SELF_ATT, None, SELF_ATT + 1), t_ref
-    )
-    k4 = query_s
+        fg(join(dec_pieces, hid_low)), self_qkv, local, (SELF_ATT, None, SELF_ATT + 1), t_ref
+    )
+    spare = [join(piece, *r3)[:, depth:] for piece in dec_pieces]
+
+    def spare_part(which):
+        return [piece[None, :, which * features : (which + 1) * features] for piece in spare]
+
+    low_shards, high_shards = ffn_halves(enc_wide.result(*r3))
+    low_count, high_count = len(low_shards) * 2 * slices, len(high_shards) * 2 * slices
+    plan2 = Pair(
+        (
+            jnp.concatenate(low_shards + spare_part(0) + [cross_attn_w[1:3]]),
+            jnp.concatenate(high_shards + spare_part(1) + spare_part(2)),
+        ),
+        ([low_count, tensor_size, 2], [high_count, tensor_size, tensor_size]),
+    )
+    plan2.hop()
     window_s = halo(pair_s)
-    due(self_out_plan.hop(k4))
-    due(*cross_spread.hop(k4))
-    enc_shards = enc_wide.result(k4)
-
+    r4 = (window_s[0], window_s[2])
     mixed_s, mixed_t_s, totals_s = attend_fg(fg(query_s), window_s, text)
-    k5 = totals_s
     mixed_s = exchange(mixed_s)
-    enc_views = enc_own_views + ffn_gather(join(enc_shards[1:], k5))
-    self_out_plan.hop(k5)
-    (self_out_w,) = self_out_plan.result()
-    cross_pieces = cross_spread.result(k5)
-    cross_shards = jnp.concatenate(
-        [cross_attn_w[1:3]]
-        + [piece[1:2] for piece in cross_pieces]
-        + [piece[0:1] for piece in cross_pieces]
-    )
-    cross_plan = Gather(cross_shards[None], first_order, [2, tensor_size, tensor_size])
-    due(cross_plan.hop())
-    dec_wide = Spread(join(dec_ffn_w, k5), "tensor", wide_down)
+    r5 = tuple(mixed_s[1:])
+    plan2.hop(*r5)
+    dec_wide = Spread(join(dec_ffn_w, *r5), "tensor", wide_down)
     dec_wide.hop()
+    plan2.hop(*r5)
+    (low_views, self_out_w, cross_kv), (high_views, cross_out_w, cross_query) = plan2.result()
+    enc_views = ffn_views(low_views, high_views)
+    active_e, slope_e, keep, send = ffn_up_down(hid_low, hid_other, enc_views, enc_first)
+    came = swap(send, "tensor", 1)
+    r7 = (came,)
+    low_shards, high_shards = ffn_halves(dec_wide.result(send))
+    plan4 = Pair(
+        (jnp.concatenate(low_shards), jnp.concatenate(high_shards)), ([low_count], [high_count])
+    )
+    plan4.hop()
 
     summed_s, decoded, decoded_low = out_norm(
-        [fg(mixed_s[0])] + mixed_s[1:], self_out_w, dec_in, table, SELF_ATT + 2
-    )
-    k6 = decoded_low
-    cross_plan.hop(k6)
-    dec_views = ffn_gather(dec_wide.result(k6))
-
-    active_e, slope_e, keep, send = ffn_up_down(
-        join(hid_low, k6), hid_other, enc_views, enc_first
-    )
-    k7 = keep
-    came = swap(send, "tensor", 1)
-    cross_plan.hop(k7)
-    cross_kv, cross_query, cross_out_w = cross_plan.result()
-    ffn_summed_e, encoded = add_norm([hid, keep, came], table, ENC_FFN)
+        join(mixed_s, send), self_out_w, dec_in, table, SELF_ATT + 2
+    )
+    ffn_summed_e, encoded = add_norm(
+        [hid, join(keep, decoded_low), came], table, ENC_FFN
+    )
     enc_rows = spread(encoded, "tensor", t_down)
-    asked = exchange(
-        project_rows(join(decoded_low, encoded), cross_query, local, CROSS_ATT)
-    )
+    plan4.hop(encoded)
+    asked = exchange(project_rows(join(decoded_low, encoded), cross_query, local, CROSS_ATT))
+    query_c = in_order(asked, t_ref)
 
     flat_c, pair_c = project(
         enc_rows, cross_kv, local, (None, CROSS_ATT + 1), t_ref
     )
     window_c = halo(pair_c)
-    query_c = in_order(asked, t_ref)
+    r9 = (window_c[0], window_c[2])
+    plan4.hop(*r9)
     mixed_c, mixed_t_c, totals_c = attend_fg(query_c, window_c, both)
     mixed_c = exchange(mixed_c)
+    (low_views,), (high_views,) = plan4.result()
+    dec_views = ffn_views(low_views, high_views)
     summed_c, crossed, crossed_low = out_norm(
         mixed_c, cross_out_w, decoded, table, CROSS_ATT + 2
     )
@@ -1203,114 +1347,126 @@
     du_d, dec_first_sum, keep, send = ffn_down_up(low_d, other_d, dec_views, slope_d)
     came = swap(send, "tensor", 1)
     dec_grads = ffn_weight_grads(
-        crossed_low, crossed_other, low_d, other_d, join(du_d, send), active_d, None, fsdp_size
-    )[0]
-    dec_whole = lax.psum_scatter(dec_grads, "fsdp", scatter_dimension=1, tiled=True)
+        crossed_low, crossed_other, low_d, other_d, join(du_d, send), active_d, core, fsdp_size
+    )
+    dec_fold = Folds(dec_grads, 0)
+    due(dec_fold.hop())
 
     grad_sum_c, low_c, sums_c, *given = norm_out_grad(
-        [grad_sum_d, join(keep, dec_grads), came], summed_c, table, CROSS_ATT + 3, cross_out_w
+        [fg(grad_sum_d), join(keep, dec_grads), came], summed_c, table, CROSS_ATT + 3, cross_out_w
     )
     given = exchange(given)
+    b2 = tuple(given[1:])
+    due(dec_fold.next(*b2))
     dq_c, below, own, above = attend_back_fg(
-        query_c, window_c, given, mixed_t_c, totals_c, both
+        query_c, window_c, fg(given), mixed_t_c, totals_c, both
     )
     below = lax.ppermute(below, "fsdp", down_pairs)
     above = lax.ppermute(above, "fsdp", up_pairs)
     asked_c = exchange(by_mask(dq_c, t_ref, tensor_size))
+    b3 = (below, above)
+    due(dec_fold.next(*b3))
     dk_c, dv_c, columns_c, *blocks_c = input_grads(
-        dq_c, own, below, above, cross_kv, t_ref, tensor_size
+        dq_c, fg(own), below, above, cross_kv, t_ref, tensor_size
     )
     source = Share(blocks_c, "tensor", t_up)
-    due(*source.hop())
+    due(source.hop())
     from_asked = asked_grad([join(asked_c[0], dk_c)] + asked_c[1:], cross_query)
-
-    grad_sum_s, low_s, sums_s, *given = norm_out_grad(
-        [fg(grad_sum_c), from_asked], summed_s, table, SELF_ATT + 3, self_out_w
-    )
-    b6 = low_s
-    given = exchange(given)
-    due(*source.hop(b6))
     cross_grads = weight_grads(
         [
-            [(flat_c, join(dk_c, b6)), (flat_c, dv_c)]
-            + [(low_c, piece) for piece in mixed_c]
-            + [(decoded_low, piece) for piece in asked_c]
+            [(flat_c, join(dk_c, from_asked)), (flat_c, dv_c)]
+            + [(decoded_low, piece) for piece in asked_c],
+            [(low_c, piece) for piece in mixed_c],
         ],
         core, fsdp_size,
     )
-    cross_fold = Fold(cross_grads[0], cross_grads[1], second_order[:-1], 1)
+    cross_fold = Folds(cross_grads, 1)
     due(cross_fold.hop())
+
+    grad_sum_s, low_s, sums_s, *given = norm_out_grad(
+        [fg(join(grad_sum_c, cross_grads)), from_asked], summed_s, table, SELF_ATT + 3, self_out_w
+    )
+    given = exchange(given)
+    b6 = tuple(given[1:])
+    source.hop(*b6)
+    due(cross_fold.next(*b6))
     dq_s, below, own, above = attend_back_fg(
-        query_s, window_s, [fg(given[0])] + given[1:], mixed_t_s, totals_s, text
-    )
-    b7 = dq_s
+        query_s, window_s, fg(given), mixed_t_s, totals_s, text
+    )
     below = lax.ppermute(below, "fsdp", down_pairs)
     above = lax.ppermute(above, "fsdp", up_pairs)
-    cross_fold.next(b7)
+    b7 = (below, above)
+    due(cross_fold.next(*b7))
+    dec_wide_share = WideShare(jnp.stack(dec_fold.result(*b7)))
+    due(dec_wide_share.hop())
     grad_sum_f, low_f, enc_sums = norm_grad(
-        [join(enc_cot, b7)] + source.result(), ffn_summed_e, table, ENC_FFN + 1
-    )
-    b9 = low_f
+        [fg(join(enc_cot, dq_s))] + source.result(), ffn_summed_e, table, ENC_FFN + 1
+    )
     other_f = swap(low_f, "tensor", 1)
     dk_s, dv_s, columns_s, *blocks_s = input_grads(
-        dq_s, join(own, b9), below, above, self_qkv, t_ref, tensor_size
+        dq_s, join(own, low_f), below, above, self_qkv, t_ref, tensor_size
     )
     b8 = dk_s
     target = Share(blocks_s, "tensor", t_up)
-    due(*target.hop())
-    due(cross_fold.came)
-    du_e, enc_first_sum, keep, send = ffn_down_up(
-        fg(join(low_f, b8)), other_f, enc_views, slope_e
-    )
-    b10 = keep
-    came = swap(send, "tensor", 1)
-    due(*target.hop(b10))
-    due(cross_fold.next(b10))
-    enc_grads = ffn_weight_grads(
-        hid_low, hid_other, low_f, other_f, join(du_e, send), active_e, core, fsdp_size
-    )
+    due(target.hop())
     self_parts = weight_grads(
         [
-            [(flat_s, join(dq_s, b10)), (flat_s, dk_s), (flat_s, dv_s)]
+            [(flat_s, join(dq_s, b8)), (flat_s, dk_s), (flat_s, dv_s)]
             + [(low_s, piece) for piece in mixed_s]
         ],
         core, fsdp_size,
     )
-    due(enc_grads, self_parts)
+    self_fold = Fold(self_parts[0], self_parts[1], first_order[:-1], 1)
+    due(self_fold.hop())
+    du_e, enc_first_sum, keep, send = ffn_down_up(
+        fg(join(low_f, self_parts)), other_f, enc_views, slope_e
+    )
+    came = swap(send, "tensor", 1)
+    b10 = came
+    due(target.hop(b10))
+    due(self_fold.next(b10))
+    enc_grads = ffn_weight_grads(
+        hid_low, hid_other, low_f, other_f, join(du_e, send), active_e, core, fsdp_size
+    )
+    enc_fold = Folds(enc_grads, 0)
+    due(enc_fold.hop())
 
     grad_sum_e, low_e, sums_e, *given = norm_out_grad(
-        [grad_sum_f, fg(keep), came], summed_e, table, ENC_ATT + 3, enc_out_w
-    )
-    b11 = low_e
+        [grad_sum_f, fg(join(keep, enc_grads)), came], summed_e, table, ENC_ATT + 3, enc_out_w
+    )
     given = exchange(given)
-    enc_folds = [
-        Fold(enc_grads[2 * i], enc_grads[2 * i + 1], (first_order, second_order)[i][:-1], 0)
-        for i in range(2)
-    ]
-    for item in enc_folds:
-        due(item.hop(b11))
-    self_fold = Fold(self_parts[0], self_parts[1], first_order[:-1], 1)
-    due(self_fold.hop(b11))
-    cross_own = cross_fold.result(b11)
-    cross_pieces = cross_own[2:].reshape((2, tensor_size) + cross_own.shape[1:])
-    cross_share = Share([cross_pieces[:, mask] for mask in t_masks], "tensor", t_up)
-    due(*cross_share.hop())
+    b11 = tuple(given[1:])
+    due(enc_fold.next(*b11))
+    due(self_fold.next(*b11))
     dq_e, below, own, above = attend_back_fg(
-        query_e, window_e, [fg(given[0])] + given[1:], mixed_t_e, totals_e, both
-    )
-    b12 = dq_e
+        query_e, window_e, fg(given), mixed_t_e, totals_e, both
+    )
     below = lax.ppermute(below, "fsdp", down_pairs)
     above = lax.ppermute(above, "fsdp", up_pairs)
-    for item in enc_folds:
-        due(item.next(b12))
-    due(*cross_share.hop(b12))
-    due(self_fold.next(b12))
+    b12 = (below, above)
+    enc_fold.next(*b12)
+    cross_first, cross_outs = cross_fold.result(*b12)
+    self_own = self_fold.result(*b12)
+    late_share = Share(
+        [
+            jnp.stack([cross_first[2 + mask], cross_outs[mask], self_own[3 + mask]])
+            for mask in t_masks
+        ],
+        "tensor", t_up,
+    )
     dk_e, dv_e, columns_e, *blocks_e = input_grads(
         dq_e, fg(own), below, above, enc_qkv, t_ref, tensor_size
     )
     b13 = dk_e
     enc_share = Share(blocks_e, "tensor", t_up)
     enc_share.hop()
+    small_sum = SmallSum(
+        pack_grads(
+            [sums_e, sums_s, sums_c, enc_sums, dec_sums], [columns_e, columns_s, columns_c],
+            [enc_first_sum, dec_first_sum], t_ref, fsdp_size, wide_masks,
+        )
+    )
+    small_sum.hop()
     enc_att = weight_grads(
         [
             [(flat_e, dq_e), (flat_e, join(dk_e, tuple(blocks_e))), (flat_e, dv_e)],
@@ -1318,63 +1474,38 @@
         ],
         core, fsdp_size,
     )
-    enc_att_folds = [
-        Fold(enc_att[2 * i], enc_att[2 * i + 1], (first_order, second_order)[i][:-1], 1)
-        for i in range(2)
-    ]
-    for item in enc_att_folds:
-        item.hop()
-    enc_own = [item.result(b13) for item in enc_folds]
-    self_own = self_fold.result(b13)
-
-    def tensor_sum(pieces_):
-        return total(Share(pieces_, "tensor", t_up).result())
-
-    def wide_sum(pieces_):
-        held = dict(zip(wide_masks, pieces_))
-        for bit in wide_up:
-            for mask in sorted(held):
-                if mask not in held or mask & (2 * bit - 1):
-                    continue
-                came_ = swap(held.pop(mask | bit).astype(BF), "tensor", bit)
-                held[mask] = held[mask].astype(F32) + came_.astype(F32)
-        return held[0].astype(F32)
-
-    wide_count = len(wide_masks)
-    small_grads = pack_grads(
-        [sums_e, sums_s, sums_c, enc_sums, dec_sums], [columns_e, columns_s, columns_c],
-        [enc_first_sum, dec_first_sum], t_ref, fsdp_size, wide_masks,
-    )
-    for bit in bits_of("fsdp")[::-1]:
-        half = small_grads.shape[0] // 2
-        mine = (f_index // bit) % 2
-        kept = lax.dynamic_slice_in_dim(small_grads, mine * half, half, 0)
-        sent = lax.dynamic_slice_in_dim(small_grads, (1 - mine) * half, half, 0)
-        small_grads = kept + swap(sent, "fsdp", bit)
-    small_grads = small_grads[0]
-    for bit in t_up[:-1]:
-        small_grads = small_grads + swap(small_grads, "tensor", bit)
-    small_out = unpack_grads(
-        [small_grads, swap(small_grads, "tensor", t_up[-1])], [item.shape for item in small]
-    )
-
+    att_folds = Folds(enc_att, 1)
+    att_folds.hop()
+
+    def meet(*items):
+        for item, came_ in zip(items, join([item.came for item in items])):
+            item.came = came_
+
+    meet(enc_share, small_sum, *att_folds.folds, *enc_fold.folds)
+    att_folds.next()
     enc_share.hop()
-    dec_ffn_grad = wide_sum(
-        [join(dec_whole, b12)[2 * j : 2 * j + 2] for j in range(wide_count)]
-    )
-    enc_pair = jnp.stack(enc_own)
-    enc_ffn_grad = wide_sum(
-        [enc_pair[:, :, j * hidden : (j + 1) * hidden] for j in range(wide_count)]
-    )
-    self_grad = jnp.concatenate(
-        [self_own[:3], tensor_sum([self_own[3 + mask] for mask in t_masks])[None]]
-    )
-    cross_pair = total(cross_share.result())
-    cross_grad = jnp.concatenate([cross_pair[1:2], cross_own[:2], cross_pair[0:1]])
-    enc_att_own, enc_att_out = [item.result() for item in enc_att_folds]
-    enc_grad = jnp.concatenate(
-        [enc_att_own, tensor_sum([enc_att_out[mask] for mask in t_masks])[None]]
-    )
+    small_sum.hop()
+    enc_wide_share = WideShare(jnp.stack(enc_fold.result()))
+    enc_wide_share.hop()
+    meet(small_sum, *att_folds.folds)
+    att_folds.next()
+    small_sum.hop()
+    late_share.hop()
+    meet(late_share, small_sum, *att_folds.folds)
+    enc_att_own, enc_att_out = att_folds.result()
+    out_share = Share([enc_att_out[mask] for mask in t_masks], "tensor", t_up)
+    out_share.hop()
+    late_share.hop()
+    small_sum.hop()
+    meet(out_share, late_share, small_sum)
+    out_share.hop()
+    small_out = unpack_grads(small_sum.result(), [item.shape for item in small])
+    enc_grad = jnp.concatenate([enc_att_own, total(out_share.result())[None]])
+    dec_ffn_grad = dec_wide_share.result()
+    enc_ffn_grad = enc_wide_share.result()
+    late = total(late_share.result())
+    cross_grad = jnp.concatenate([late[0:1], cross_first[:2], late[1:2]])
+    self_grad = jnp.concatenate([self_own[:3], late[2:3]])
     grad_source = total([grad_sum_e] + enc_share.result())
     grad_target = total([grad_sum_s] + target.result())
 

time: 728 us -> 694 us (0.953)
  starting transfers between devices: 190 us -> 149 us
  waiting for transfers between devices: 331 us -> 355 us
  between operations: 16.9 us -> 4.57 us
  blocking collectives: 8.49 us -> 0 us
    ppermute x110 -> x99, waiting for transfers between devices: 302 us -> 350 us  [swap(): lax.ppermute(value, axis, [(i, i ^ mask) for i in range(lax.axis_size(axi...]
    ppermute x110 -> x99, starting transfers between devices: 169 us -> 124 us  [swap(): lax.ppermute(value, axis, [(i, i ^ mask) for i in range(lax.axis_size(axi...]
    all_gather x3 -> x0, waiting for transfers between devices: 24.9 us -> none  [ffn_gather(): whole = lax.all_gather(stack, 'fsdp', axis=1, tiled=True)]
    all_gather x1 -> x0, blocking collectives: 8.49 us -> none  [per_device(): lax.all_gather(pack_small(small, enc_attn_bias.shape[1]), 'fsdp', axis=0)]
    unnamed x362 -> x385, local copies, waits for them, and re-layouts: 37.4 us -> 34.5 us
    convert_element_type x6 -> x9, other arithmetic: 13 us -> 15.1 us  [next(): pick(mine).astype(BF)]
  transfers between devices with their start and end apart: 126 -> 111, of which waited for: 52 -> 62; matrix products, arithmetic and copies ran while one was open for 7% -> 6% of each run, Pallas kernels for 11% -> 10%
where the time goes in v3:
time: 694 us; the launch traced here: 685 us
  waiting for transfers between devices  355 us (51%)
  starting transfers between devices  149 us (21%)
  Pallas kernels  94 us (14%)
  local copies, waits for them, and re-layouts  43.7 us (6%)
  other arithmetic  39 us (6%)
    ppermute x99, waiting for transfers between devices, swap(): lax.ppermute(value, axis, [(i, i ^ mask) for i in range(lax.axis_size(axi...  350 us
    ppermute x99, starting transfers between devices, swap(): lax.ppermute(value, axis, [(i, i ^ mask) for i in range(lax.axis_size(axi...  124 us
    pallas_call x40, Pallas kernels, run(): pl.pallas_call(kernel, out_shape=[jax.ShapeDtypeStruct(shape, kind) for s...  87.2 us
    unnamed x385, local copies, waits for them, and re-layouts  34.5 us
    convert_element_type x9, other arithmetic, next(): pick(mine).astype(BF)  15.1 us
  transfers between devices with their start and end apart: 111, of which 62 were waited for; matrix products, arithmetic and copies ran while one was open for 6% of the time, Pallas kernels for 10%

profile of v3, /device:TPU:0, one launch (start us, length us, event | category | flops | bytes accessed | tf_op | source)
XLA Modules:
  0.0 685.0 jit_solution(16515888410037568533)
XLA Ops:
  47.3 11.6 %collective-permute-done.12 = bf16[1,128,1792]{2,1,0:T(8,128)(2,1)S(1)} collective-permute-done((bf16[1,128,1792]{2,1,0:T(8,128)(2,1)S(1)}, bf16[1,128,1792]{2,1,0:T(8,128)(2,1)S(1)}, u32[]{:S(2)}, u32[]{:S(2)}) %collective-permute-start.12) | collective-permute-done | bytes 458784 | tf_op jit(solution)/shard_map/ppermute | solution.py:24
  74.1 7.0 %collective-permute-done.14 = bf16[2,128,256]{2,1,0:T(8,128)(2,1)S(1)} collective-permute-done((bf16[2,128,256]{2,1,0:T(8,128)(2,1)S(1)}, bf16[2,128,256]{2,1,0:T(8,128)(2,1)S(1)}, u32[]{:S(2)}, u32[]{:S(2)}) %collective-permute-start.14) | collective-permute-done | bytes 131104 | tf_op jit(solution)/shard_map/ppermute | solution.py:24
  86.8 21.6 %collective-permute-done.17 = bf16[2,128,1792]{2,1,0:T(8,128)(2,1)S(1)} collective-permute-done((bf16[2,128,1792]{2,1,0:T(8,128)(2,1)S(1)}, bf16[2,128,1792]{2,1,0:T(8,128)(2,1)S(1)}, u32[]{:S(2)}, u32[]{:S(2)}) %collective-permute-start.17) | collective-permute-done | bytes 917536 | tf_op jit(solution)/shard_map/ppermute | solution.py:24
  141.1 10.3 %collective-permute-done.18 = bf16[1,14,128,256]{3,2,1,0:T(8,128)(2,1)S(1)} collective-permute-done((bf16[1,14,128,256]{3,2,1,0:T(8,128)(2,1)S(1)}, bf16[1,14,128,256]{3,2,1,0:T(8,128)(2,1)S(1)}, u32[]{:S(2)}, u32[]{:S(2)}) %collective-permute-start.18) | collective-permute-done | bytes 917536 | tf_op jit(solution)/shard_map/ppermute | solution.py:24
  156.4 41.1 %collective-permute-done.26 = bf16[2,14,128,256]{3,2,1,0:T(8,128)(2,1)S(1)} collective-permute-done((bf16[2,14,128,256]{3,2,1,0:T(8,128)(2,1)S(1)}, bf16[2,14,128,256]{3,2,1,0:T(8,128)(2,1)S(1)}, u32[]{:S(2)}, u32[]{:S(2)}) %collective-permute-start.26) | collective-permute-done | bytes 1835040 | tf_op jit(solution)/shard_map/ppermute | solution.py:24
  221.9 7.5 %collective-permute-done.42 = bf16[2,128,1024]{2,1,0:T(8,128)(2,1)} collective-permute-done((bf16[2,128,1024]{2,1,0:T(8,128)(2,1)}, bf16[2,128,1024]{2,1,0:T(8,128)(2,1)}, u32[]{:S(2)}, u32[]{:S(2)}) %collective-permute-start.42) | collective-permute-done | bytes 524320 | tf_op jit(solution)/shard_map/ppermute | solution.py:24
  239.7 9.9 %collective-permute-done.31 = bf16[2,128,256]{2,1,0:T(8,128)(2,1)S(1)} collective-permute-done((bf16[2,128,256]{2,1,0:T(8,128)(2,1)S(1)}, bf16[2,128,256]{2,1,0:T(8,128)(2,1)S(1)}, u32[]{:S(2)}, u32[]{:S(2)}) %collective-permute-start.31) | collective-permute-done | bytes 131104 | tf_op jit(solution)/shard_map/ppermute | solution.py:24
  284.9 17.3 %collective-permute-start.46 = (bf16[4,8,128,256]{3,2,1,0:T(8,128)(2,1)S(1)}, bf16[4,8,128,256]{3,2,1,0:T(8,128)(2,1)S(1)}, u32[]{:S(2)}, u32[]{:S(2)}) collective-permute-start(bf16[4,8,128,256]{3,2,1,0:T(8,128)(2,1)S(1)} %pad_maximum_fusion.3.refs_0_), channel_id=1, source_target_pairs={{0,4},{4,0},{8,12},{12,8},{16,20},{20,16},{24,28},{28,24},{1,5},{5... | collective-permute-start | bytes 6291464 | tf_op jit(solution)/shard_map/ppermute | solution.py:24
  329.5 6.6 collective-permute-done.49.other_ref.eo_ref
  362.1 6.6 collective-permute-done.52
  382.1 8.3 %attend_back.3 = (bf16[512,256]{1,0:T(8,128)(2,1)S(1)}, bf16[2,512,256]{2,1,0:T(8,128)(2,1)S(1)}, f32[2,512,256]{2,1,0:T(8,128)S(1)}, bf16[2,512,256]{2,1,0:T(8,128)(2,1)S(1)}) custom-call(s32[4]{0:T(128)S(1)} %copy-done.159, s32[1]{0:T(128)} %bitcast.t_ref, s32[8,512]{1,0:T(8,128)S(1)} %copy-done.143, bf16[512,256]{1,0:T(8,128)(2,1)S(1)} %copy-done.127, ...), custom_call_target="tpu_custom_call" | custom-call | flops 30000001024 | bytes 1 | tf_op jit(solution)/shard_map/attend_back/pallas_call | solution.py:236
  400.0 9.0 %collective-permute-done.60 = bf16[2,128,256]{2,1,0:T(8,128)(2,1)} collective-permute-done((bf16[2,128,256]{2,1,0:T(8,128)(2,1)}, bf16[2,128,256]{2,1,0:T(8,128)(2,1)}, u32[]{:S(2)}, u32[]{:S(2)}) %collective-permute-start.60) | collective-permute-done | bytes 131104 | tf_op jit(solution)/shard_map/ppermute | solution.py:24
  439.4 9.2 %collective-permute-done.64 = bf16[2,128,256]{2,1,0:T(8,128)(2,1)S(1)} collective-permute-done((bf16[2,128,256]{2,1,0:T(8,128)(2,1)S(1)}, bf16[2,128,256]{2,1,0:T(8,128)(2,1)S(1)}, u32[]{:S(2)}, u32[]{:S(2)}) %collective-permute-start.64) | collective-permute-done | bytes 131104 | tf_op jit(solution)/shard_map/ppermute | solution.py:24
  469.5 9.4 %collective-permute-done.69 = bf16[4,2,128,256]{3,2,0,1:T(8,128)(2,1)S(1)} collective-permute-done((bf16[4,2,128,256]{3,2,0,1:T(8,128)(2,1)S(1)}, bf16[4,2,128,256]{3,2,0,1:T(8,128)(2,1)S(1)}, u32[]{:S(2)}, u32[]{:S(2)}) %collective-permute-start.69) | collective-permute-done | bytes 524320 | tf_op jit(solution)/shard_map/ppermute | solution.py:24
  478.8 7.8 %collective-permute-done.68 = bf16[6,2,128,256]{3,2,0,1:T(8,128)(2,1)S(1)} collective-permute-done((bf16[6,2,128,256]{3,2,0,1:T(8,128)(2,1)S(1)}, bf16[6,2,128,256]{3,2,0,1:T(8,128)(2,1)S(1)}, u32[]{:S(2)}, u32[]{:S(2)}) %collective-permute-start.68) | collective-permute-done | bytes 786464 | tf_op jit(solution)/shard_map/ppermute | solution.py:24
  529.5 15.4 %collective-permute-done.82 = bf16[1,128,1024]{2,1,0:T(8,128)(2,1)S(1)} collective-permute-done((bf16[1,128,1024]{2,1,0:T(8,128)(2,1)S(1)}, bf16[1,128,1024]{2,1,0:T(8,128)(2,1)S(1)}, u32[]{:S(2)}, u32[]{:S(2)}) %collective-permute-start.82) | collective-permute-done | bytes 262176 | tf_op jit(solution)/shard_map/ppermute | solution.py:24
  548.8 8.5 %attend_back.5 = (bf16[512,256]{1,0:T(8,128)(2,1)S(1)}, bf16[2,512,256]{2,1,0:T(8,128)(2,1)S(1)}, f32[2,512,256]{2,1,0:T(8,128)S(1)}, bf16[2,512,256]{2,1,0:T(8,128)(2,1)S(1)}) custom-call(s32[4]{0:T(128)S(1)} %copy-done.160, s32[1]{0:T(128)} %bitcast.t_ref, s32[8,512]{1,0:T(8,128)S(1)} %copy-done.144, bf16[512,256]{1,0:T(8,128)(2,1)S(1)} %copy-done.123, ...), custom_call_target="tpu_custom_call" | custom-call | flops 30000001024 | bytes 1 | tf_op jit(solution)/shard_map/attend_back/pallas_call | solution.py:236
  570.5 9.9 %collective-permute-done.88 = bf16[7,128,256]{2,1,0:T(8,128)(2,1)S(1)} collective-permute-done((bf16[7,128,256]{2,1,0:T(8,128)(2,1)S(1)}, bf16[7,128,256]{2,1,0:T(8,128)(2,1)S(1)}, u32[]{:S(2)}, u32[]{:S(2)}) %collective-permute-start.88) | collective-permute-done | bytes 458784 | tf_op jit(solution)/shard_map/ppermute | solution.py:24
  582.9 13.0 %collective-permute-done.86 = bf16[2,128,2048]{2,1,0:T(8,128)(2,1)S(1)} collective-permute-done((bf16[2,128,2048]{2,1,0:T(8,128)(2,1)S(1)}, bf16[2,128,2048]{2,1,0:T(8,128)(2,1)S(1)}, u32[]{:S(2)}, u32[]{:S(2)}) %collective-permute-start.86) | collective-permute-done | bytes 1048608 | tf_op jit(solution)/shard_map/ppermute | solution.py:24
  595.9 7.0 %collective-permute-done.87 = bf16[2,128,2048]{2,1,0:T(8,128)(2,1)S(1)} collective-permute-done((bf16[2,128,2048]{2,1,0:T(8,128)(2,1)S(1)}, bf16[2,128,2048]{2,1,0:T(8,128)(2,1)S(1)}, u32[]{:S(2)}, u32[]{:S(2)}) %collective-permute-start.87) | collective-permute-done | bytes 1048608 | tf_op jit(solution)/shard_map/ppermute | solution.py:24
  629.8 8.7 %collective-permute-done.110 = bf16[1,3,128,256]{3,2,1,0:T(8,128)(2,1)S(1)} collective-permute-done((bf16[1,3,128,256]{3,2,1,0:T(8,128)(2,1)S(1)}, bf16[1,3,128,256]{3,2,1,0:T(8,128)(2,1)S(1)}, u32[]{:S(2)}, u32[]{:S(2)}) %collective-permute-start.110) | collective-permute-done | bytes 196640 | tf_op jit(solution)/shard_map/ppermute | solution.py:24
  642.0 9.1 %collective-permute-done.107 = bf16[128,2048]{1,0:T(8,128)(2,1)S(1)} collective-permute-done((bf16[128,2048]{1,0:T(8,128)(2,1)S(1)}, bf16[128,2048]{1,0:T(8,128)(2,1)S(1)}, u32[]{:S(2)}, u32[]{:S(2)}) %collective-permute-start.107) | collective-permute-done | bytes 524320 | tf_op jit(solution)/shard_map/ppermute | solution.py:24
  655.5 7.8 %collective-permute-done.92 = bf16[1,128,1024]{2,1,0:T(8,128)(2,1)S(1)} collective-permute-done((bf16[1,128,1024]{2,1,0:T(8,128)(2,1)S(1)}, bf16[1,128,1024]{2,1,0:T(8,128)(2,1)S(1)}, u32[]{:S(2)}, u32[]{:S(2)}) %collective-permute-start.92) | collective-permute-done | bytes 262176 | tf_op jit(solution)/shard_map/ppermute | solution.py:24
  667.8 6.8 collective-permute-done.108
  (773 shorter events, 411.1 us)
Async XLA Ops:
  2.5 30.0 %collective-permute-start.5 = (bf16[128,1280]{1,0:T(8,128)(2,1)S(1)}, bf16[128,1280]{1,0:T(8,128)(2,1)S(1)}, u32[]{:S(2)}, u32[]{:S(2)}) collective-permute-start(bf16[128,1280]{1,0:T(8,128)(2,1)S(1)} %pad_maximum_fusion.26.rest_0_), channel_id=1, source_target_pairs={{0,3},{1,2},{2,1},{3,0},{4,7},{5,6},{6,5},{7,4},{8,11},{9,10},{10,... | collective-permute-start | bytes 983048 | tf_op jit(solution)/shard_map/ppermute | solution.py:24
  7.6 27.9 %collective-permute-start.4 = (bf16[128,1280]{1,0:T(8,128)(2,1)S(1)}, bf16[128,1280]{1,0:T(8,128)(2,1)S(1)}, u32[]{:S(2)}, u32[]{:S(2)}) collective-permute-start(bf16[128,1280]{1,0:T(8,128)(2,1)S(1)} %pad_maximum_fusion.26.rest_0_), channel_id=1, source_target_pairs={{0,2},{1,3},{2,0},{3,1},{4,6},{5,7},{6,4},{7,5},{8,10},{9,11},{10,... | collective-permute-start | bytes 983048 | tf_op jit(solution)/shard_map/ppermute | solution.py:24
  7.6 27.9 %collective-permute-start.3 = (bf16[128,1280]{1,0:T(8,128)(2,1)S(1)}, bf16[128,1280]{1,0:T(8,128)(2,1)S(1)}, u32[]{:S(2)}, u32[]{:S(2)}) collective-permute-start(bf16[128,1280]{1,0:T(8,128)(2,1)S(1)} %pad_maximum_fusion.26.rest_0_), channel_id=1, source_target_pairs={{0,1},{1,0},{2,3},{3,2},{4,5},{5,4},{6,7},{7,6},{8,9},{9,8},{10,11... | collective-permute-start | bytes 983048 | tf_op jit(solution)/shard_map/ppermute | solution.py:24
  18.3 28.9 %collective-permute-start.6 = (bf16[1,3,128,256]{3,2,1,0:T(8,128)(2,1)}, bf16[1,3,128,256]{3,2,1,0:T(8,128)(2,1)}, u32[]{:S(2)}, u32[]{:S(2)}) collective-permute-start(bf16[1,3,128,256]{3,2,1,0:T(8,128)(2,1)} %slice_bitcast_fusion.6), channel_id=1, source_target_pairs={{0,8},{4,12},{8,0},{12,4},{16,24},{20,28},{24,16},{28,20},{1,9},{5... | collective-permute-start | bytes 589832 | tf_op jit(solution)/shard_map/ppermute | solution.py:24
  71.9 36.5 %collective-permute-start.17 = (bf16[2,128,1792]{2,1,0:T(8,128)(2,1)S(1)}, bf16[2,128,1792]{2,1,0:T(8,128)(2,1)S(1)}, u32[]{:S(2)}, u32[]{:S(2)}) collective-permute-start(bf16[2,128,1792]{2,1,0:T(8,128)(2,1)S(1)} %pad_maximum_fusion.11), channel_id=1, source_target_pairs={{0,1},{1,0},{2,3},{3,2},{4,5},{5,4},{6,7},{7,6},{8,9},{9,8},{10,11... | collective-permute-start | bytes 2752520 | tf_op jit(solution)/shard_map/ppermute | solution.py:24
  81.1 37.2 %collective-permute-start.19 = (bf16[2,128,1024]{2,1,0:T(8,128)(2,1)S(1)}, bf16[2,128,1024]{2,1,0:T(8,128)(2,1)S(1)}, u32[]{:S(2)}, u32[]{:S(2)}) collective-permute-start(bf16[2,128,1024]{2,1,0:T(8,128)(2,1)S(1)} %copy-done.175), channel_id=1, source_target_pairs={{0,2},{1,3},{2,0},{3,1},{4,6},{5,7},{6,4},{7,5},{8,10},{9,11},{10,... | collective-permute-start | bytes 1572872 | tf_op jit(solution)/shard_map/ppermute | solution.py:24
  122.3 29.1 %collective-permute-start.18 = (bf16[1,14,128,256]{3,2,1,0:T(8,128)(2,1)S(1)}, bf16[1,14,128,256]{3,2,1,0:T(8,128)(2,1)S(1)}, u32[]{:S(2)}, u32[]{:S(2)}) collective-permute-start(bf16[1,14,128,256]{3,2,1,0:T(8,128)(2,1)S(1)} %bitcast.482), channel_id=1, source_target_pairs={{0,8},{4,12},{8,0},{12,4},{16,24},{20,28},{24,16},{28,20},{1,9},{5... | collective-permute-start | bytes 2752520 | tf_op jit(solution)/shard_map/ppermute | solution.py:24
  151.6 49.8 %collective-permute-start.27 = (bf16[2,16,128,256]{3,2,1,0:T(8,128)(2,1)S(1)}, bf16[2,16,128,256]{3,2,1,0:T(8,128)(2,1)S(1)}, u32[]{:S(2)}, u32[]{:S(2)}) collective-permute-start(bf16[2,16,128,256]{3,2,1,0:T(8,128)(2,1)S(1)} %pad_maximum_fusion.2), channel_id=1, source_target_pairs={{0,8},{4,12},{8,0},{12,4},{16,24},{20,28},{24,16},{28,20},{1,9},{5... | collective-permute-start | bytes 6291464 | tf_op jit(solution)/shard_map/ppermute | solution.py:24
  156.4 41.2 %collective-permute-start.26 = (bf16[2,14,128,256]{3,2,1,0:T(8,128)(2,1)S(1)}, bf16[2,14,128,256]{3,2,1,0:T(8,128)(2,1)S(1)}, u32[]{:S(2)}, u32[]{:S(2)}) collective-permute-start(bf16[2,14,128,256]{3,2,1,0:T(8,128)(2,1)S(1)} %pad_maximum_fusion.5), channel_id=1, source_target_pairs={{0,16},{4,20},{8,24},{12,28},{16,0},{20,4},{24,8},{28,12},{1,17},{... | collective-permute-start | bytes 5505032 | tf_op jit(solution)/shard_map/ppermute | solution.py:24
  206.1 43.6 %collective-permute-start.41 = (bf16[1,8,128,256]{3,2,1,0:T(8,128)(2,1)}, bf16[1,8,128,256]{3,2,1,0:T(8,128)(2,1)}, u32[]{:S(2)}, u32[]{:S(2)}) collective-permute-start(bf16[1,8,128,256]{3,2,1,0:T(8,128)(2,1)} %bitcast.69), channel_id=1, source_target_pairs={{0,8},{4,12},{8,0},{12,4},{16,24},{20,28},{24,16},{28,20},{1,9},{5... | collective-permute-start | bytes 1572872 | tf_op jit(solution)/shard_map/ppermute | solution.py:24
  251.1 31.7 %collective-permute-start.44 = (bf16[2,8,128,256]{3,2,1,0:T(8,128)(2,1)S(1)}, bf16[2,8,128,256]{3,2,1,0:T(8,128)(2,1)S(1)}, u32[]{:S(2)}, u32[]{:S(2)}) collective-permute-start(bf16[2,8,128,256]{3,2,1,0:T(8,128)(2,1)S(1)} %pad_maximum_fusion.9), channel_id=1, source_target_pairs={{0,16},{4,20},{8,24},{12,28},{16,0},{20,4},{24,8},{28,12},{1,17},{... | collective-permute-start | bytes 3145736 | tf_op jit(solution)/shard_map/ppermute | solution.py:24
  373.2 36.8 %collective-permute-start.55 = (bf16[2,128,2048]{2,1,0:T(8,128)(2,1)}, bf16[2,128,2048]{2,1,0:T(8,128)(2,1)}, u32[]{:S(2)}, u32[]{:S(2)}) collective-permute-start(bf16[2,128,2048]{2,1,0:T(8,128)(2,1)} %get-tuple-element.538), channel_id=1, source_target_pairs={{0,8},{4,12},{8,0},{12,4},{16,24},{20,28},{24,16},{28,20},{1,9},{5... | collective-permute-start | bytes 3145736 | tf_op jit(solution)/shard_map/ppermute | solution.py:24
  382.1 27.9 %collective-permute-start.56 = (bf16[2,128,2048]{2,1,0:T(8,128)(2,1)}, bf16[2,128,2048]{2,1,0:T(8,128)(2,1)}, u32[]{:S(2)}, u32[]{:S(2)}) collective-permute-start(bf16[2,128,2048]{2,1,0:T(8,128)(2,1)} %get-tuple-element.536), channel_id=1, source_target_pairs={{0,16},{4,20},{8,24},{12,28},{16,0},{20,4},{24,8},{28,12},{1,17},{... | collective-permute-start | bytes 3145736 | tf_op jit(solution)/shard_map/ppermute | solution.py:24
  448.6 38.0 %collective-permute-start.70 = (bf16[1,128,1024]{2,1,0:T(8,128)(2,1)S(1)}, bf16[1,128,1024]{2,1,0:T(8,128)(2,1)S(1)}, u32[]{:S(2)}, u32[]{:S(2)}) collective-permute-start(bf16[1,128,1024]{2,1,0:T(8,128)(2,1)S(1)} %fusion.54), channel_id=1, source_target_pairs={{0,2},{1,3},{2,0},{3,1},{4,6},{5,7},{6,4},{7,5},{8,10},{9,11},{10,... | collective-permute-start | bytes 786440 | tf_op jit(solution)/shard_map/ppermute | solution.py:24
  459.1 27.6 %collective-permute-start.68 = (bf16[6,2,128,256]{3,2,0,1:T(8,128)(2,1)S(1)}, bf16[6,2,128,256]{3,2,0,1:T(8,128)(2,1)S(1)}, u32[]{:S(2)}, u32[]{:S(2)}) collective-permute-start(bf16[6,2,128,256]{3,2,0,1:T(8,128)(2,1)S(1)} %get-tuple-element.544), channel_id=1, source_target_pairs={{0,8},{4,12},{8,0},{12,4},{16,24},{20,28},{24,16},{28,20},{1,9},{5... | collective-permute-start | bytes 2359304 | tf_op jit(solution)/shard_map/ppermute | solution.py:24
  466.6 29.0 %collective-permute-start.75 = (bf16[2,128,1024]{2,1,0:T(8,128)(2,1)}, bf16[2,128,1024]{2,1,0:T(8,128)(2,1)S(1)}, u32[]{:S(2)}, u32[]{:S(2)}) collective-permute-start(bf16[2,128,1024]{2,1,0:T(8,128)(2,1)} %fusion.7), channel_id=1, source_target_pairs={{0,2},{1,3},{2,0},{3,1},{4,6},{5,7},{6,4},{7,5},{8,10},{9,11},{10,... | collective-permute-start | bytes 1572872 | tf_op jit(solution)/shard_map/ppermute | solution.py:24
  515.5 31.9 %collective-permute-start.84 = (bf16[2,2,128,2048]{3,2,1,0:T(8,128)(2,1)S(1)}, bf16[2,2,128,2048]{3,2,1,0:T(8,128)(2,1)}, u32[]{:S(2)}, u32[]{:S(2)}) collective-permute-start(bf16[2,2,128,2048]{3,2,1,0:T(8,128)(2,1)S(1)} %bitcast.445), channel_id=1, source_target_pairs={{0,4},{4,0},{8,12},{12,8},{16,20},{20,16},{24,28},{28,24},{1,5},{5... | collective-permute-start | bytes 6291464 | tf_op jit(solution)/shard_map/ppermute | solution.py:24
  516.0 31.4 %collective-permute-start.85 = (bf16[2,2,128,2048]{3,2,1,0:T(8,128)(2,1)S(1)}, bf16[2,2,128,2048]{3,2,1,0:T(8,128)(2,1)S(1)}, u32[]{:S(2)}, u32[]{:S(2)}) collective-permute-start(bf16[2,2,128,2048]{3,2,1,0:T(8,128)(2,1)S(1)} %bitcast.444), channel_id=1, source_target_pairs={{0,4},{4,0},{8,12},{12,8},{16,20},{20,16},{24,28},{28,24},{1,5},{5... | collective-permute-start | bytes 6291464 | tf_op jit(solution)/shard_map/ppermute | solution.py:24
  566.6 29.3 %collective-permute-start.86 = (bf16[2,128,2048]{2,1,0:T(8,128)(2,1)S(1)}, bf16[2,128,2048]{2,1,0:T(8,128)(2,1)S(1)}, u32[]{:S(2)}, u32[]{:S(2)}) collective-permute-start(bf16[2,128,2048]{2,1,0:T(8,128)(2,1)S(1)} %get-tuple-element.534), channel_id=1, source_target_pairs={{0,8},{4,12},{8,0},{12,4},{16,24},{20,28},{24,16},{28,20},{1,9},{5... | collective-permute-start | bytes 3145736 | tf_op jit(solution)/shard_map/ppermute | solution.py:24
  568.5 34.5 %collective-permute-start.87 = (bf16[2,128,2048]{2,1,0:T(8,128)(2,1)S(1)}, bf16[2,128,2048]{2,1,0:T(8,128)(2,1)S(1)}, u32[]{:S(2)}, u32[]{:S(2)}) collective-permute-start(bf16[2,128,2048]{2,1,0:T(8,128)(2,1)S(1)} %get-tuple-element.532), channel_id=1, source_target_pairs={{0,16},{4,20},{8,24},{12,28},{16,0},{20,4},{24,8},{28,12},{1,17},{... | collective-permute-start | bytes 3145736 | tf_op jit(solution)/shard_map/ppermute | solution.py:24
  581.1 43.2 %collective-permute-start.109 = (bf16[2,3,128,256]{3,2,1,0:T(8,128)(2,1)S(1)}, bf16[2,3,128,256]{3,2,1,0:T(8,128)(2,1)S(1)}, u32[]{:S(2)}, u32[]{:S(2)}) collective-permute-start(bf16[2,3,128,256]{3,2,1,0:T(8,128)(2,1)S(1)} %maximum_maximum_fusion), channel_id=1, source_target_pairs={{0,1},{1,0},{2,3},{3,2},{4,5},{5,4},{6,7},{7,6},{8,9},{9,8},{10,11... | collective-permute-start | bytes 1179656 | tf_op jit(solution)/shard_map/ppermute | solution.py:24
  604.2 36.1 %collective-permute-start.91 = (bf16[2,128,1024]{2,1,0:T(8,128)(2,1)S(1)}, bf16[2,128,1024]{2,1,0:T(8,128)(2,1)S(1)}, u32[]{:S(2)}, u32[]{:S(2)}) collective-permute-start(bf16[2,128,1024]{2,1,0:T(8,128)(2,1)S(1)} %pad_maximum_fusion.19), channel_id=1, source_target_pairs={{0,1},{1,0},{2,3},{3,2},{4,5},{5,4},{6,7},{7,6},{8,9},{9,8},{10,11... | collective-permute-start | bytes 1572872 | tf_op jit(solution)/shard_map/ppermute | solution.py:24
  607.7 33.0 %collective-permute-start.96 = (bf16[4,2,2,128,256]{4,3,0,2,1:T(8,128)(2,1)S(1)}, bf16[4,2,2,128,256]{4,3,0,2,1:T(8,128)(2,1)S(1)}, u32[]{:S(2)}, u32[]{:S(2)}) collective-permute-start(bf16[4,2,2,128,256]{4,3,0,2,1:T(8,128)(2,1)S(1)} %copy.58), channel_id=1, source_target_pairs={{0,4},{4,0},{8,12},{12,8},{16,20},{20,16},{24,28},{28,24},{1,5},{5... | collective-permute-start | bytes 3145736 | tf_op jit(solution)/shard_map/ppermute | solution.py:24
  607.8 43.7 %collective-permute-start.93 = (bf16[3,2,2,128,256]{4,3,0,2,1:T(8,128)(2,1)S(1)}, bf16[3,2,2,128,256]{4,3,0,2,1:T(8,128)(2,1)S(1)}, u32[]{:S(2)}, u32[]{:S(2)}) collective-permute-start(bf16[3,2,2,128,256]{4,3,0,2,1:T(8,128)(2,1)S(1)} %copy.55), channel_id=1, source_target_pairs={{0,4},{4,0},{8,12},{12,8},{16,20},{20,16},{24,28},{28,24},{1,5},{5... | collective-permute-start | bytes 2359304 | tf_op jit(solution)/shard_map/ppermute | solution.py:24
  (275 other events, 3445.6 us)

commit v4 on v3

--- a/solution.py
+++ b/solution.py
@@ -1099,23 +1099,28 @@
         cut = shard.reshape(2, rows, slices, features)
         return jnp.moveaxis(cut, 2, 1).reshape(2 * slices, rows, features)
 
-    def ffn_halves(shards):
-        cut = [ffn_slices(shard) for shard in shards]
-        half = (wide_count + 1) // 2
-        return cut[:half], cut[half:]
-
-    def ffn_views(low, high):
+    def ups(shards):
+        return [ffn_slices(shard)[:slices] for shard in shards]
+
+    def downs(shards):
+        return [ffn_slices(shard)[slices:] for shard in shards]
+
+    def ffn_views(*arrays):
         views = []
-        for array in (low, high):
-            for at in range(0, array.shape[0], 2 * slices):
-                views.append((array, at, array, at + slices))
+        for up, down in arrays:
+            for at in range(0, up.shape[0], slices):
+                views.append((up, at, down, at))
         return views
 
-    def exchange(pieces_):
+    far = (wide_count - 1) * slices
+
+    def exchange(pieces_, *hold):
         held = dict(enumerate(pieces_))
         for bit in t_up:
             moved = [mask for mask in t_masks if mask & bit]
             came_ = swap(jnp.stack([held[mask] for mask in moved]), "tensor", bit)
+            if bit == 1:
+                came_ = join(came_, *hold)
             for at, mask in enumerate(moved):
                 held[mask] = came_[at]
         return [held[mask] for mask in t_masks]
@@ -1215,10 +1220,10 @@
                 self.hop()
             return self.held[0]
 
-    pending = [[], []]
-
-    def due(*values):
-        pending[1].extend(values)
+    pending = [[], [], [], []]
+
+    def due(*values, lag=2):
+        pending[lag - 1].extend(values)
 
     def fg(value):
         waits = pending.pop(0)
@@ -1238,8 +1243,13 @@
         parts.reshape(fsdp_size, -1, features), t_ref, tensor_size, features, wide_masks
     )
     plan1 = Pair(
-        (self_attn_w[:3], jnp.stack([piece[:, depth:] for piece in enc_pieces])),
-        ([3], [tensor_size]),
+        (
+            jnp.concatenate([self_attn_w[:3]] + ups([enc_ffn_w])),
+            jnp.concatenate(
+                [piece[None, :, depth:] for piece in enc_pieces] + downs([enc_ffn_w])
+            ),
+        ),
+        ([3, slices], [tensor_size, slices]),
     )
     due(plan1.hop())
     dec_steps = doubled(
@@ -1259,10 +1269,10 @@
     dec_pieces = dec_steps.send(r1)
 
     mixed_e, mixed_t_e, totals_e = attend_fg(fg(query_e), window_e, both)
-    mixed_e = exchange(mixed_e)
+    mixed_e = exchange(mixed_e, dec_pieces)
     r2 = tuple(mixed_e[1:])
     plan1.hop(*r2)
-    (self_qkv,), (enc_out_w,) = plan1.result()
+    (self_qkv, own_up), (enc_out_w, own_down) = plan1.result()
     enc_wide = Spread(join(enc_ffn_w, *r2), "tensor", wide_down)
     enc_wide.hop()
     for step in range(len(t_down) - 1):
@@ -1281,14 +1291,13 @@
     def spare_part(which):
         return [piece[None, :, which * features : (which + 1) * features] for piece in spare]
 
-    low_shards, high_shards = ffn_halves(enc_wide.result(*r3))
-    low_count, high_count = len(low_shards) * 2 * slices, len(high_shards) * 2 * slices
+    others = enc_wide.result(*r3)[1:]
     plan2 = Pair(
         (
-            jnp.concatenate(low_shards + spare_part(0) + [cross_attn_w[1:3]]),
-            jnp.concatenate(high_shards + spare_part(1) + spare_part(2)),
+            jnp.concatenate(ups(others) + spare_part(0) + [cross_attn_w[1:3]]),
+            jnp.concatenate(downs(others) + spare_part(1) + spare_part(2)),
         ),
-        ([low_count, tensor_size, 2], [high_count, tensor_size, tensor_size]),
+        ([far, tensor_size, 2], [far, tensor_size, tensor_size]),
     )
     plan2.hop()
     window_s = halo(pair_s)
@@ -1300,14 +1309,15 @@
     dec_wide = Spread(join(dec_ffn_w, *r5), "tensor", wide_down)
     dec_wide.hop()
     plan2.hop(*r5)
-    (low_views, self_out_w, cross_kv), (high_views, cross_out_w, cross_query) = plan2.result()
-    enc_views = ffn_views(low_views, high_views)
+    (far_up, self_out_w, cross_kv), (far_down, cross_out_w, cross_query) = plan2.result()
+    enc_views = ffn_views((own_up, own_down), (far_up, far_down))
     active_e, slope_e, keep, send = ffn_up_down(hid_low, hid_other, enc_views, enc_first)
     came = swap(send, "tensor", 1)
     r7 = (came,)
-    low_shards, high_shards = ffn_halves(dec_wide.result(send))
+    shards = dec_wide.result(send)
     plan4 = Pair(
-        (jnp.concatenate(low_shards), jnp.concatenate(high_shards)), ([low_count], [high_count])
+        (jnp.concatenate(ups(shards)), jnp.concatenate(downs(shards))),
+        ([slices + far], [slices + far]),
     )
     plan4.hop()
 
@@ -1319,7 +1329,9 @@
     )
     enc_rows = spread(encoded, "tensor", t_down)
     plan4.hop(encoded)
-    asked = exchange(project_rows(join(decoded_low, encoded), cross_query, local, CROSS_ATT))
+    asked = exchange(
+        project_rows(join(decoded_low, *enc_rows[1:]), cross_query, local, CROSS_ATT)
+    )
     query_c = in_order(asked, t_ref)
 
     flat_c, pair_c = project(
@@ -1330,8 +1342,7 @@
     plan4.hop(*r9)
     mixed_c, mixed_t_c, totals_c = attend_fg(query_c, window_c, both)
     mixed_c = exchange(mixed_c)
-    (low_views,), (high_views,) = plan4.result()
-    dec_views = ffn_views(low_views, high_views)
+    dec_views = ffn_views([array for (array,) in plan4.result()])
     summed_c, crossed, crossed_low = out_norm(
         mixed_c, cross_out_w, decoded, table, CROSS_ATT + 2
     )
@@ -1389,7 +1400,7 @@
     given = exchange(given)
     b6 = tuple(given[1:])
     source.hop(*b6)
-    due(cross_fold.next(*b6))
+    due(cross_fold.next(*b6), lag=3)
     dq_s, below, own, above = attend_back_fg(
         query_s, window_s, fg(given), mixed_t_s, totals_s, text
     )
@@ -1423,8 +1434,8 @@
     )
     came = swap(send, "tensor", 1)
     b10 = came
-    due(target.hop(b10))
-    due(self_fold.next(b10))
+    due(target.hop(b10), lag=3)
+    due(self_fold.next(b10), lag=3)
     enc_grads = ffn_weight_grads(
         hid_low, hid_other, low_f, other_f, join(du_e, send), active_e, core, fsdp_size
     )

time: 694 us -> 676 us (0.974)
  waiting for transfers between devices: 355 us -> 331 us
  starting transfers between devices: 149 us -> 157 us
    ppermute x99, waiting for transfers between devices: 350 us -> 330 us  [swap(): lax.ppermute(value, axis, [(i, i ^ mask) for i in range(lax.axis_size(axi...]
    ppermute x99, starting transfers between devices: 124 us -> 135 us  [swap(): lax.ppermute(value, axis, [(i, i ^ mask) for i in range(lax.axis_size(axi...]
    unnamed x385 -> x398, local copies, waits for them, and re-layouts: 34.5 us -> 30.9 us
  transfers between devices with their start and end apart: 111 -> 111, of which waited for: 62 -> 63; matrix products, arithmetic and copies ran while one was open for 6% -> 6% of each run, Pallas kernels for 10% -> 12%
where the time goes in v4:
time: 676 us; the launch traced here: 668 us
  waiting for transfers between devices  331 us (49%)
  starting transfers between devices  157 us (23%)
  Pallas kernels  94.2 us (14%)
  local copies, waits for them, and re-layouts  40.9 us (6%)
  other arithmetic  40 us (6%)
    ppermute x99, waiting for transfers between devices, swap(): lax.ppermute(value, axis, [(i, i ^ mask) for i in range(lax.axis_size(axi...  330 us
    ppermute x99, starting transfers between devices, swap(): lax.ppermute(value, axis, [(i, i ^ mask) for i in range(lax.axis_size(axi...  135 us
    pallas_call x40, Pallas kernels, run(): pl.pallas_call(kernel, out_shape=[jax.ShapeDtypeStruct(shape, kind) for s...  87.2 us
    unnamed x398, local copies, waits for them, and re-layouts  30.9 us
    convert_element_type x9, other arithmetic, next(): pick(mine).astype(BF)  15.3 us
  transfers between devices with their start and end apart: 111, of which 63 were waited for; matrix products, arithmetic and copies ran while one was open for 6% of the time, Pallas kernels for 12%

profile of v4, /device:TPU:0, one launch (start us, length us, event | category | flops | bytes accessed | tf_op | source)
XLA Modules:
  0.0 667.5 jit_solution(2277859808059519670)
XLA Ops:
  25.7 6.9 %collective-permute-done.1 = bf16[2,400,256]{2,1,0:T(8,128)(2,1)S(1)} collective-permute-done((bf16[2,400,256]{2,1,0:T(8,128)(2,1)S(1)}, bf16[2,400,256]{2,1,0:T(8,128)(2,1)S(1)}, u32[]{:S(2)}, u32[]{:S(2)}) %collective-permute-start.1) | collective-permute-done | bytes 409632 | tf_op jit(solution)/shard_map/ppermute | solution.py:24
  52.9 8.8 %collective-permute-done.12 = bf16[1,128,1792]{2,1,0:T(8,128)(2,1)S(1)} collective-permute-done((bf16[1,128,1792]{2,1,0:T(8,128)(2,1)S(1)}, bf16[1,128,1792]{2,1,0:T(8,128)(2,1)S(1)}, u32[]{:S(2)}, u32[]{:S(2)}) %collective-permute-start.12) | collective-permute-done | bytes 458784 | tf_op jit(solution)/shard_map/ppermute | solution.py:24
  73.1 18.5 %collective-permute-done.13 = bf16[2,128,256]{2,1,0:T(8,128)(2,1)S(1)} collective-permute-done((bf16[2,128,256]{2,1,0:T(8,128)(2,1)S(1)}, bf16[2,128,256]{2,1,0:T(8,128)(2,1)S(1)}, u32[]{:S(2)}, u32[]{:S(2)}) %collective-permute-start.13) | collective-permute-done | bytes 131104 | tf_op jit(solution)/shard_map/ppermute | solution.py:24
  92.8 8.2 %collective-permute-done.15 = bf16[2,128,256]{2,1,0:T(8,128)(2,1)S(1)} collective-permute-done((bf16[2,128,256]{2,1,0:T(8,128)(2,1)S(1)}, bf16[2,128,256]{2,1,0:T(8,128)(2,1)S(1)}, u32[]{:S(2)}, u32[]{:S(2)}) %collective-permute-start.15) | collective-permute-done | bytes 131104 | tf_op jit(solution)/shard_map/ppermute | solution.py:24
  116.5 11.0 %collective-permute-done.19 = bf16[2,128,1024]{2,1,0:T(8,128)(2,1)S(1)} collective-permute-done((bf16[2,128,1024]{2,1,0:T(8,128)(2,1)S(1)}, bf16[2,128,1024]{2,1,0:T(8,128)(2,1)S(1)}, u32[]{:S(2)}, u32[]{:S(2)}) %collective-permute-start.19) | collective-permute-done | bytes 524320 | tf_op jit(solution)/shard_map/ppermute | solution.py:24
  142.5 8.8 %collective-permute-done.25 = bf16[2,128,256]{2,1,0:T(8,128)(2,1)S(1)} collective-permute-done((bf16[2,128,256]{2,1,0:T(8,128)(2,1)S(1)}, bf16[2,128,256]{2,1,0:T(8,128)(2,1)S(1)}, u32[]{:S(2)}, u32[]{:S(2)}) %collective-permute-start.25) | collective-permute-done | bytes 131104 | tf_op jit(solution)/shard_map/ppermute | solution.py:24
  155.2 29.8 %collective-permute-done.26 = bf16[2,10,128,256]{3,2,1,0:T(8,128)(2,1)S(1)} collective-permute-done((bf16[2,10,128,256]{3,2,1,0:T(8,128)(2,1)S(1)}, bf16[2,10,128,256]{3,2,1,0:T(8,128)(2,1)S(1)}, u32[]{:S(2)}, u32[]{:S(2)}) %collective-permute-start.26) | collective-permute-done | bytes 1310752 | tf_op jit(solution)/shard_map/ppermute | solution.py:24
  210.1 7.2 %collective-permute-done.41 = bf16[2,128,1024]{2,1,0:T(8,128)(2,1)S(1)} collective-permute-done((bf16[2,128,1024]{2,1,0:T(8,128)(2,1)S(1)}, bf16[2,128,1024]{2,1,0:T(8,128)(2,1)S(1)}, u32[]{:S(2)}, u32[]{:S(2)}) %collective-permute-start.41) | collective-permute-done | bytes 524320 | tf_op jit(solution)/shard_map/ppermute | solution.py:24
  225.6 12.3 %collective-permute-done.32.rest_2_ = bf16[128,1024]{1,0:T(8,128)(2,1)S(1)} collective-permute-done((bf16[128,1024]{1,0:T(8,128)(2,1)}, bf16[128,1024]{1,0:T(8,128)(2,1)S(1)}, u32[]{:S(2)}, u32[]{:S(2)}) %collective-permute-start.32) | collective-permute-done | bytes 262176 | tf_op jit(solution)/shard_map/ppermute | solution.py:24
  238.1 8.0 %collective-permute-done.33.rest_3_ = bf16[128,1024]{1,0:T(8,128)(2,1)S(1)} collective-permute-done((bf16[128,1024]{1,0:T(8,128)(2,1)S(1)}, bf16[128,1024]{1,0:T(8,128)(2,1)S(1)}, u32[]{:S(2)}, u32[]{:S(2)}) %collective-permute-start.33) | collective-permute-done | bytes 262176 | tf_op jit(solution)/shard_map/ppermute | solution.py:24
  273.4 21.1 %collective-permute-start.46 = (bf16[4,8,128,256]{3,2,1,0:T(8,128)(2,1)S(1)}, bf16[4,8,128,256]{3,2,1,0:T(8,128)(2,1)S(1)}, u32[]{:S(2)}, u32[]{:S(2)}) collective-permute-start(bf16[4,8,128,256]{3,2,1,0:T(8,128)(2,1)S(1)} %pad_maximum_fusion.3.refs_0_), channel_id=1, source_target_pairs={{0,4},{4,0},{8,12},{12,8},{16,20},{20,16},{24,28},{28,24},{1,5},{5... | collective-permute-start | bytes 6291464 | tf_op jit(solution)/shard_map/ppermute | solution.py:24
  307.9 6.6 collective-permute-done.48.rest_2_
  318.5 7.4 %collective-permute-done.49.other_ref.eo_ref = bf16[128,1024]{1,0:T(8,128)(2,1)S(1)} collective-permute-done((bf16[128,1024]{1,0:T(8,128)(2,1)S(1)}, bf16[128,1024]{1,0:T(8,128)(2,1)S(1)}, u32[]{:S(2)}, u32[]{:S(2)}) %collective-permute-start.49) | collective-permute-done | bytes 262176 | tf_op jit(solution)/shard_map/ppermute | solution.py:24
  350.6 7.1 %collective-permute-done.52 = bf16[2,128,256]{2,1,0:T(8,128)(2,1)S(1)} collective-permute-done((bf16[2,128,256]{2,1,0:T(8,128)(2,1)S(1)}, bf16[2,128,256]{2,1,0:T(8,128)(2,1)S(1)}, u32[]{:S(2)}, u32[]{:S(2)}) %collective-permute-start.52) | collective-permute-done | bytes 131104 | tf_op jit(solution)/shard_map/ppermute | solution.py:24
  370.5 8.3 %attend_back.3 = (bf16[512,256]{1,0:T(8,128)(2,1)S(1)}, bf16[2,512,256]{2,1,0:T(8,128)(2,1)S(1)}, f32[2,512,256]{2,1,0:T(8,128)S(1)}, bf16[2,512,256]{2,1,0:T(8,128)(2,1)S(1)}) custom-call(s32[4]{0:T(128)S(1)} %copy-done.159, s32[1]{0:T(128)} %bitcast.t_ref, s32[8,512]{1,0:T(8,128)S(1)} %copy-done.143, bf16[512,256]{1,0:T(8,128)(2,1)S(1)} %copy-done.127, ...), custom_call_target="tpu_custom_call" | custom-call | flops 30000001024 | bytes 1 | tf_op jit(solution)/shard_map/attend_back/pallas_call | solution.py:236
  388.7 7.4 %collective-permute-done.60 = bf16[2,128,256]{2,1,0:T(8,128)(2,1)} collective-permute-done((bf16[2,128,256]{2,1,0:T(8,128)(2,1)}, bf16[2,128,256]{2,1,0:T(8,128)(2,1)}, u32[]{:S(2)}, u32[]{:S(2)}) %collective-permute-start.60) | collective-permute-done | bytes 131104 | tf_op jit(solution)/shard_map/ppermute | solution.py:24
  487.5 7.2 %collective-permute-start.74 = (bf16[4,128,256]{2,1,0:T(8,128)(2,1)S(1)}, bf16[4,128,256]{2,1,0:T(8,128)(2,1)S(1)}, u32[]{:S(2)}, u32[]{:S(2)}) collective-permute-start(bf16[4,128,256]{2,1,0:T(8,128)(2,1)S(1)} %fusion.55), channel_id=1, source_target_pairs={{0,8},{4,12},{8,0},{12,4},{16,24},{20,28},{24,16},{28,20},{1,9},{5... | collective-permute-start | bytes 786440 | tf_op jit(solution)/shard_map/ppermute | solution.py:24
  519.0 11.3 %collective-permute-done.84 = bf16[1,128,1024]{2,1,0:T(8,128)(2,1)S(1)} collective-permute-done((bf16[1,128,1024]{2,1,0:T(8,128)(2,1)S(1)}, bf16[1,128,1024]{2,1,0:T(8,128)(2,1)S(1)}, u32[]{:S(2)}, u32[]{:S(2)}) %collective-permute-start.84) | collective-permute-done | bytes 262176 | tf_op jit(solution)/shard_map/ppermute | solution.py:24
  541.7 8.5 %attend_back.5 = (bf16[512,256]{1,0:T(8,128)(2,1)S(1)}, bf16[2,512,256]{2,1,0:T(8,128)(2,1)S(1)}, f32[2,512,256]{2,1,0:T(8,128)S(1)}, bf16[2,512,256]{2,1,0:T(8,128)(2,1)S(1)}) custom-call(s32[4]{0:T(128)S(1)} %copy-done.160, s32[1]{0:T(128)} %bitcast.t_ref, s32[8,512]{1,0:T(8,128)S(1)} %copy-done.144, bf16[512,256]{1,0:T(8,128)(2,1)S(1)} %copy-done.123, ...), custom_call_target="tpu_custom_call" | custom-call | flops 30000001024 | bytes 1 | tf_op jit(solution)/shard_map/attend_back/pallas_call | solution.py:236
  564.3 11.5 %collective-permute-done.88 = bf16[7,128,256]{2,1,0:T(8,128)(2,1)S(1)} collective-permute-done((bf16[7,128,256]{2,1,0:T(8,128)(2,1)S(1)}, bf16[7,128,256]{2,1,0:T(8,128)(2,1)S(1)}, u32[]{:S(2)}, u32[]{:S(2)}) %collective-permute-start.88) | collective-permute-done | bytes 458784 | tf_op jit(solution)/shard_map/ppermute | solution.py:24
  576.7 9.7 %collective-permute-done.109 = bf16[2,3,128,256]{3,2,1,0:T(8,128)(2,1)S(1)} collective-permute-done((bf16[2,3,128,256]{3,2,1,0:T(8,128)(2,1)S(1)}, bf16[2,3,128,256]{3,2,1,0:T(8,128)(2,1)S(1)}, u32[]{:S(2)}, u32[]{:S(2)}) %collective-permute-start.109) | collective-permute-done | bytes 393248 | tf_op jit(solution)/shard_map/ppermute | solution.py:24
  587.9 7.6 %collective-permute-done.87 = bf16[2,128,2048]{2,1,0:T(8,128)(2,1)S(1)} collective-permute-done((bf16[2,128,2048]{2,1,0:T(8,128)(2,1)S(1)}, bf16[2,128,2048]{2,1,0:T(8,128)(2,1)S(1)}, u32[]{:S(2)}, u32[]{:S(2)}) %collective-permute-start.87) | collective-permute-done | bytes 1048608 | tf_op jit(solution)/shard_map/ppermute | solution.py:24
  638.3 9.1 %collective-permute-done.92 = bf16[1,128,1024]{2,1,0:T(8,128)(2,1)S(1)} collective-permute-done((bf16[1,128,1024]{2,1,0:T(8,128)(2,1)S(1)}, bf16[1,128,1024]{2,1,0:T(8,128)(2,1)S(1)}, u32[]{:S(2)}, u32[]{:S(2)}) %collective-permute-start.92) | collective-permute-done | bytes 262176 | tf_op jit(solution)/shard_map/ppermute | solution.py:24
  650.2 7.4 %collective-permute-done.108 = bf16[2,128,1024]{2,1,0:T(8,128)(2,1)S(1)} collective-permute-done((bf16[2,128,1024]{2,1,0:T(8,128)(2,1)S(1)}, bf16[2,128,1024]{2,1,0:T(8,128)(2,1)S(1)}, u32[]{:S(2)}, u32[]{:S(2)}) %collective-permute-start.108) | collective-permute-done | bytes 524320 | tf_op jit(solution)/shard_map/ppermute | solution.py:24
  (793 shorter events, 413.1 us)
Async XLA Ops:
  3.1 29.9 %collective-permute-start.3 = (bf16[128,1280]{1,0:T(8,128)(2,1)S(1)}, bf16[128,1280]{1,0:T(8,128)(2,1)S(1)}, u32[]{:S(2)}, u32[]{:S(2)}) collective-permute-start(bf16[128,1280]{1,0:T(8,128)(2,1)S(1)} %pad_maximum_fusion.28.rest_0_), channel_id=1, source_target_pairs={{0,1},{1,0},{2,3},{3,2},{4,5},{5,4},{6,7},{7,6},{8,9},{9,8},{10,11... | collective-permute-start | bytes 983048 | tf_op jit(solution)/shard_map/ppermute | solution.py:24
  6.2 27.5 %collective-permute-start.4 = (bf16[128,1280]{1,0:T(8,128)(2,1)S(1)}, bf16[128,1280]{1,0:T(8,128)(2,1)S(1)}, u32[]{:S(2)}, u32[]{:S(2)}) collective-permute-start(bf16[128,1280]{1,0:T(8,128)(2,1)S(1)} %pad_maximum_fusion.28.rest_0_), channel_id=1, source_target_pairs={{0,2},{1,3},{2,0},{3,1},{4,6},{5,7},{6,4},{7,5},{8,10},{9,11},{10,... | collective-permute-start | bytes 983048 | tf_op jit(solution)/shard_map/ppermute | solution.py:24
  19.9 33.0 %collective-permute-start.6 = (bf16[1,7,128,256]{3,2,1,0:T(8,128)(2,1)}, bf16[1,7,128,256]{3,2,1,0:T(8,128)(2,1)}, u32[]{:S(2)}, u32[]{:S(2)}) collective-permute-start(bf16[1,7,128,256]{3,2,1,0:T(8,128)(2,1)} %maximum_bitcast_fusion.2), channel_id=1, source_target_pairs={{0,8},{4,12},{8,0},{12,4},{16,24},{20,28},{24,16},{28,20},{1,9},{5... | collective-permute-start | bytes 1376264 | tf_op jit(solution)/shard_map/ppermute | solution.py:24
  63.4 37.7 %collective-permute-start.10 = (bf16[2,7,128,256]{3,2,1,0:T(8,128)(2,1)S(1)}, bf16[2,7,128,256]{3,2,1,0:T(8,128)(2,1)S(1)}, u32[]{:S(2)}, u32[]{:S(2)}) collective-permute-start(bf16[2,7,128,256]{3,2,1,0:T(8,128)(2,1)S(1)} %pad_maximum_fusion.13), channel_id=1, source_target_pairs={{0,16},{4,20},{8,24},{12,28},{16,0},{20,4},{24,8},{28,12},{1,17},{... | collective-permute-start | bytes 2752520 | tf_op jit(solution)/shard_map/ppermute | solution.py:24
  65.7 35.3 %collective-permute-start.11 = (bf16[2,8,128,256]{3,2,1,0:T(8,128)(2,1)S(1)}, bf16[2,8,128,256]{3,2,1,0:T(8,128)(2,1)S(1)}, u32[]{:S(2)}, u32[]{:S(2)}) collective-permute-start(bf16[2,8,128,256]{3,2,1,0:T(8,128)(2,1)S(1)} %pad_maximum_fusion.10), channel_id=1, source_target_pairs={{0,8},{4,12},{8,0},{12,4},{16,24},{20,28},{24,16},{28,20},{1,9},{5... | collective-permute-start | bytes 3145736 | tf_op jit(solution)/shard_map/ppermute | solution.py:24
  65.9 25.7 %collective-permute-start.14 = (bf16[2,128,1792]{2,1,0:T(8,128)(2,1)S(1)}, bf16[2,128,1792]{2,1,0:T(8,128)(2,1)S(1)}, u32[]{:S(2)}, u32[]{:S(2)}) collective-permute-start(bf16[2,128,1792]{2,1,0:T(8,128)(2,1)S(1)} %pad_maximum_fusion.14), channel_id=1, source_target_pairs={{0,1},{1,0},{2,3},{3,2},{4,5},{5,4},{6,7},{7,6},{8,9},{9,8},{10,11... | collective-permute-start | bytes 2752520 | tf_op jit(solution)/shard_map/ppermute | solution.py:24
  153.9 36.5 %collective-permute-start.27 = (bf16[2,12,128,256]{3,2,1,0:T(8,128)(2,1)S(1)}, bf16[2,12,128,256]{3,2,1,0:T(8,128)(2,1)S(1)}, u32[]{:S(2)}, u32[]{:S(2)}) collective-permute-start(bf16[2,12,128,256]{3,2,1,0:T(8,128)(2,1)S(1)} %pad_maximum_fusion.6), channel_id=1, source_target_pairs={{0,8},{4,12},{8,0},{12,4},{16,24},{20,28},{24,16},{28,20},{1,9},{5... | collective-permute-start | bytes 4718600 | tf_op jit(solution)/shard_map/ppermute | solution.py:24
  154.9 30.1 %collective-permute-start.26 = (bf16[2,10,128,256]{3,2,1,0:T(8,128)(2,1)S(1)}, bf16[2,10,128,256]{3,2,1,0:T(8,128)(2,1)S(1)}, u32[]{:S(2)}, u32[]{:S(2)}) collective-permute-start(bf16[2,10,128,256]{3,2,1,0:T(8,128)(2,1)S(1)} %pad_maximum_fusion.7), channel_id=1, source_target_pairs={{0,16},{4,20},{8,24},{12,28},{16,0},{20,4},{24,8},{28,12},{1,17},{... | collective-permute-start | bytes 3932168 | tf_op jit(solution)/shard_map/ppermute | solution.py:24
  190.7 26.6 %collective-permute-start.41 = (bf16[2,128,1024]{2,1,0:T(8,128)(2,1)S(1)}, bf16[2,128,1024]{2,1,0:T(8,128)(2,1)S(1)}, u32[]{:S(2)}, u32[]{:S(2)}) collective-permute-start(bf16[2,128,1024]{2,1,0:T(8,128)(2,1)S(1)} %copy-done.181), channel_id=1, source_target_pairs={{0,2},{1,3},{2,0},{3,1},{4,6},{5,7},{6,4},{7,5},{8,10},{9,11},{10,... | collective-permute-start | bytes 1572872 | tf_op jit(solution)/shard_map/ppermute | solution.py:24
  238.0 34.6 %collective-permute-start.44 = (bf16[2,8,128,256]{3,2,1,0:T(8,128)(2,1)S(1)}, bf16[2,8,128,256]{3,2,1,0:T(8,128)(2,1)S(1)}, u32[]{:S(2)}, u32[]{:S(2)}) collective-permute-start(bf16[2,8,128,256]{3,2,1,0:T(8,128)(2,1)S(1)} %pad_maximum_fusion.11), channel_id=1, source_target_pairs={{0,16},{4,20},{8,24},{12,28},{16,0},{20,4},{24,8},{28,12},{1,17},{... | collective-permute-start | bytes 3145736 | tf_op jit(solution)/shard_map/ppermute | solution.py:24
  247.0 26.2 %collective-permute-start.45 = (bf16[2,8,128,256]{3,2,1,0:T(8,128)(2,1)S(1)}, bf16[2,8,128,256]{3,2,1,0:T(8,128)(2,1)S(1)}, u32[]{:S(2)}, u32[]{:S(2)}) collective-permute-start(bf16[2,8,128,256]{3,2,1,0:T(8,128)(2,1)S(1)} %pad_maximum_fusion.12), channel_id=1, source_target_pairs={{0,8},{4,12},{8,0},{12,4},{16,24},{20,28},{24,16},{28,20},{1,9},{5... | collective-permute-start | bytes 3145736 | tf_op jit(solution)/shard_map/ppermute | solution.py:24
  362.3 34.6 %collective-permute-start.55 = (bf16[2,128,2048]{2,1,0:T(8,128)(2,1)}, bf16[2,128,2048]{2,1,0:T(8,128)(2,1)}, u32[]{:S(2)}, u32[]{:S(2)}) collective-permute-start(bf16[2,128,2048]{2,1,0:T(8,128)(2,1)} %get-tuple-element.546), channel_id=1, source_target_pairs={{0,8},{4,12},{8,0},{12,4},{16,24},{20,28},{24,16},{28,20},{1,9},{5... | collective-permute-start | bytes 3145736 | tf_op jit(solution)/shard_map/ppermute | solution.py:24
  370.0 27.0 %collective-permute-start.56 = (bf16[2,128,2048]{2,1,0:T(8,128)(2,1)}, bf16[2,128,2048]{2,1,0:T(8,128)(2,1)}, u32[]{:S(2)}, u32[]{:S(2)}) collective-permute-start(bf16[2,128,2048]{2,1,0:T(8,128)(2,1)} %get-tuple-element.544), channel_id=1, source_target_pairs={{0,16},{4,20},{8,24},{12,28},{16,0},{20,4},{24,8},{28,12},{1,17},{... | collective-permute-start | bytes 3145736 | tf_op jit(solution)/shard_map/ppermute | solution.py:24
  446.0 55.1 %collective-permute-start.76 = (bf16[128,1024]{1,0:T(8,128)(2,1)S(1)}, bf16[128,1024]{1,0:T(8,128)(2,1)S(1)}, u32[]{:S(2)}, u32[]{:S(2)}) collective-permute-start(bf16[128,1024]{1,0:T(8,128)(2,1)S(1)} %get-tuple-element.454.own_ref.e_ref), channel_id=1, source_target_pairs={{0,1},{1,0},{2,3},{3,2},{4,5},{5,4},{6,7},{7,6},{8,9},{9,8},{10,11... | collective-permute-start | bytes 786440 | tf_op jit(solution)/shard_map/ppermute | solution.py:24
  461.7 25.8 %collective-permute-start.75 = (bf16[2,128,1024]{2,1,0:T(8,128)(2,1)S(1)}, bf16[2,128,1024]{2,1,0:T(8,128)(2,1)S(1)}, u32[]{:S(2)}, u32[]{:S(2)}) collective-permute-start(bf16[2,128,1024]{2,1,0:T(8,128)(2,1)S(1)} %fusion.7), channel_id=1, source_target_pairs={{0,2},{1,3},{2,0},{3,1},{4,6},{5,7},{6,4},{7,5},{8,10},{9,11},{10,... | collective-permute-start | bytes 1572872 | tf_op jit(solution)/shard_map/ppermute | solution.py:24
  465.0 46.5 %collective-permute-start.77 = (bf16[2,128,1024]{2,1,0:T(8,128)(2,1)}, bf16[2,128,1024]{2,1,0:T(8,128)(2,1)}, u32[]{:S(2)}, u32[]{:S(2)}) collective-permute-start(bf16[2,128,1024]{2,1,0:T(8,128)(2,1)} %pad_maximum_fusion.21), channel_id=1, source_target_pairs={{0,1},{1,0},{2,3},{3,2},{4,5},{5,4},{6,7},{7,6},{8,9},{9,8},{10,11... | collective-permute-start | bytes 1572872 | tf_op jit(solution)/shard_map/ppermute | solution.py:24
  474.0 42.2 %collective-permute-start.78 = (bf16[7,2,2,128,256]{4,3,0,2,1:T(8,128)(2,1)}, bf16[7,2,2,128,256]{4,3,0,2,1:T(8,128)(2,1)}, u32[]{:S(2)}, u32[]{:S(2)}) collective-permute-start(bf16[7,2,2,128,256]{4,3,0,2,1:T(8,128)(2,1)} %copy.49), channel_id=1, source_target_pairs={{0,4},{4,0},{8,12},{12,8},{16,20},{20,16},{24,28},{28,24},{1,5},{5... | collective-permute-start | bytes 5505032 | tf_op jit(solution)/shard_map/ppermute | solution.py:24
  510.8 29.4 %collective-permute-start.82 = (bf16[2,2,128,2048]{3,2,1,0:T(8,128)(2,1)S(1)}, bf16[2,2,128,2048]{3,2,1,0:T(8,128)(2,1)}, u32[]{:S(2)}, u32[]{:S(2)}) collective-permute-start(bf16[2,2,128,2048]{3,2,1,0:T(8,128)(2,1)S(1)} %bitcast.448), channel_id=1, source_target_pairs={{0,4},{4,0},{8,12},{12,8},{16,20},{20,16},{24,28},{28,24},{1,5},{5... | collective-permute-start | bytes 6291464 | tf_op jit(solution)/shard_map/ppermute | solution.py:24
  511.4 28.8 %collective-permute-start.83 = (bf16[2,2,128,2048]{3,2,1,0:T(8,128)(2,1)S(1)}, bf16[2,2,128,2048]{3,2,1,0:T(8,128)(2,1)S(1)}, u32[]{:S(2)}, u32[]{:S(2)}) collective-permute-start(bf16[2,2,128,2048]{3,2,1,0:T(8,128)(2,1)S(1)} %bitcast.447), channel_id=1, source_target_pairs={{0,4},{4,0},{8,12},{12,8},{16,20},{20,16},{24,28},{28,24},{1,5},{5... | collective-permute-start | bytes 6291464 | tf_op jit(solution)/shard_map/ppermute | solution.py:24
  550.2 25.7 %collective-permute-start.89 = (bf16[2,512,256]{2,1,0:T(8,128)(2,1)S(1)}, bf16[2,512,256]{2,1,0:T(8,128)(2,1)S(1)}, u32[]{:S(2)}, u32[]{:S(2)}) collective-permute-start(bf16[2,512,256]{2,1,0:T(8,128)(2,1)S(1)} %get-tuple-element.489), channel_id=1, source_target_pairs={{4,0},{8,4},{12,8},{16,12},{20,16},{24,20},{28,24},{5,1},{9,5},{13... | collective-permute-start | bytes 1572872 | tf_op jit(solution)/shard_map/ppermute | solution.py:1455
  561.7 26.2 %collective-permute-start.86 = (bf16[2,128,2048]{2,1,0:T(8,128)(2,1)S(1)}, bf16[2,128,2048]{2,1,0:T(8,128)(2,1)S(1)}, u32[]{:S(2)}, u32[]{:S(2)}) collective-permute-start(bf16[2,128,2048]{2,1,0:T(8,128)(2,1)S(1)} %get-tuple-element.542), channel_id=1, source_target_pairs={{0,8},{4,12},{8,0},{12,4},{16,24},{20,28},{24,16},{28,20},{1,9},{5... | collective-permute-start | bytes 3145736 | tf_op jit(solution)/shard_map/ppermute | solution.py:24
  562.7 32.8 %collective-permute-start.87 = (bf16[2,128,2048]{2,1,0:T(8,128)(2,1)S(1)}, bf16[2,128,2048]{2,1,0:T(8,128)(2,1)S(1)}, u32[]{:S(2)}, u32[]{:S(2)}) collective-permute-start(bf16[2,128,2048]{2,1,0:T(8,128)(2,1)S(1)} %get-tuple-element.540), channel_id=1, source_target_pairs={{0,16},{4,20},{8,24},{12,28},{16,0},{20,4},{24,8},{28,12},{1,17},{... | collective-permute-start | bytes 3145736 | tf_op jit(solution)/shard_map/ppermute | solution.py:24
  596.7 25.6 %collective-permute-start.91 = (bf16[2,128,1024]{2,1,0:T(8,128)(2,1)S(1)}, bf16[2,128,1024]{2,1,0:T(8,128)(2,1)S(1)}, u32[]{:S(2)}, u32[]{:S(2)}) collective-permute-start(bf16[2,128,1024]{2,1,0:T(8,128)(2,1)S(1)} %pad_maximum_fusion.22), channel_id=1, source_target_pairs={{0,1},{1,0},{2,3},{3,2},{4,5},{5,4},{6,7},{7,6},{8,9},{9,8},{10,11... | collective-permute-start | bytes 1572872 | tf_op jit(solution)/shard_map/ppermute | solution.py:24
  599.7 36.0 %collective-permute-start.93 = (bf16[3,2,2,128,256]{4,3,0,2,1:T(8,128)(2,1)S(1)}, bf16[3,2,2,128,256]{4,3,0,2,1:T(8,128)(2,1)S(1)}, u32[]{:S(2)}, u32[]{:S(2)}) collective-permute-start(bf16[3,2,2,128,256]{4,3,0,2,1:T(8,128)(2,1)S(1)} %copy.53), channel_id=1, source_target_pairs={{0,4},{4,0},{8,12},{12,8},{16,20},{20,16},{24,28},{28,24},{1,5},{5... | collective-permute-start | bytes 2359304 | tf_op jit(solution)/shard_map/ppermute | solution.py:24
  (281 other events, 3596.8 us)

commit v5 on v4

--- a/solution.py
+++ b/solution.py
@@ -190,6 +190,53 @@
         return self.terms
 
 
+def halve_all(folds, *gate):
+    came = join([fold.came for fold in folds], *gate)
+    index = lax.axis_index("fsdp")
+    arrays, shapes, bits = [], [], []
+    for fold, new in zip(folds, came):
+        dim, bit = fold.cut()
+        shape = fold.value.shape
+        lead = 1
+        for extent in shape[:dim]:
+            lead *= extent
+        rest = 1
+        for extent in shape[dim + 1 : -2]:
+            rest *= extent
+        flat = (lead, 2, rest) + shape[-2:]
+        arrays += [fold.value.reshape(flat), new.reshape(flat)]
+        shapes.append((shape[:dim] + shape[dim + 1 :], (lead, rest) + shape[-2:]))
+        bits.append(bit)
+    mine = jnp.stack([(index // bit) % 2 for bit in bits]).astype(jnp.int32)
+
+    def kernel(mine_ref, *refs):
+        ins, outs = refs[: len(arrays)], refs[len(arrays) :]
+        for n in range(len(folds)):
+            value, new = ins[2 * n : 2 * n + 2]
+            here = mine_ref[n]
+            lead, unused, rest = value.shape[:3]
+            for out, which in zip(outs[2 * n : 2 * n + 2], (here, 1 - here)):
+
+                @pl.loop(0, lead)
+                def _(i):
+                    for j in range(rest):
+                        out[i, j] = (
+                            value[i, which, j].astype(F32) + new[i, which, j].astype(F32)
+                        ).astype(BF)
+
+    outs = []
+    for full, flat in shapes:
+        outs += [(flat, BF)] * 2
+    done = run(kernel, [mine], arrays, outs, [], "halve", 0)
+    sent = []
+    for n, fold in enumerate(folds):
+        fold.value = done[2 * n].reshape(shapes[n][0])
+        fold.sent = done[2 * n + 1].reshape(shapes[n][0])
+        fold.bit = bits[n]
+        sent.append(fold.hop())
+    return sent
+
+
 class Fold:
     def __init__(self, keep, send, order, at):
         bits = bits_of("fsdp")
@@ -201,20 +248,14 @@
         self.came = swap(join(self.sent, *gate), "fsdp", self.bit)
         return self.came
 
-    def next(self, *gate):
+    def cut(self):
         bit = self.order.pop(0)
         dim = self.at + self.live.index(bit)
         self.live.remove(bit)
-        mine = (lax.axis_index("fsdp") // bit) % 2
-        value, came = self.value, join(self.came, *gate)
-
-        def pick(which):
-            return lax.dynamic_index_in_dim(value, which, dim, False).astype(
-                F32
-            ) + lax.dynamic_index_in_dim(came, which, dim, False).astype(F32)
-
-        self.value, self.sent, self.bit = pick(mine).astype(BF), pick(1 - mine).astype(BF), bit
-        return self.hop()
+        return dim, bit
+
+    def next(self, *gate):
+        return halve_all([self], *gate)[0]
 
     def result(self, *gate):
         while self.order:
@@ -224,6 +265,7 @@
 
 
 MIB = 2**20
+QUICK = ("halve",)
 HEAD_SCALE = HD ** (-0.5)
 
 
@@ -241,7 +283,7 @@
         scratch_shapes=scratch,
         compiler_params=pltpu.CompilerParams(vmem_limit_bytes=40 * MIB),
         cost_estimate=pl.CostEstimate(
-            flops=PACE, bytes_accessed=1, transcendentals=0
+            flops=1 if name in QUICK else PACE, bytes_accessed=1, transcendentals=0
         ),
         name=name,
         **extra,
@@ -1164,10 +1206,7 @@
             return [fold.hop(*gate) for fold in self.folds]
 
         def next(self, *gate):
-            came_ = join([fold.came for fold in self.folds], *gate)
-            for fold, value in zip(self.folds, came_):
-                fold.came = value
-            return [fold.next() for fold in self.folds]
+            return halve_all(self.folds, *gate)
 
         def result(self, *gate):
             return [fold.result(*gate) for fold in self.folds]

time: 676 us -> 669 us (0.990)
  other arithmetic: 40 us -> 18.3 us
  starting transfers between devices: 157 us -> 171 us
  waiting for transfers between devices: 331 us -> 321 us
  Pallas kernels: 94.2 us -> 101 us
    convert_element_type x18 -> x0, other arithmetic: 18.4 us -> none  [the longest x9 15.3 us: next(): pick(mine).astype(BF)]
    ppermute x99, starting transfers between devices: 135 us -> 147 us  [swap(): lax.ppermute(value, axis, [(i, i ^ mask) for i in range(lax.axis_size(axi...]
    ppermute x99, waiting for transfers between devices: 330 us -> 319 us  [swap(): lax.ppermute(value, axis, [(i, i ^ mask) for i in range(lax.axis_size(axi...]
    pallas_call x40 -> x50, Pallas kernels: 87.2 us -> 94.3 us  [run(): pl.pallas_call(kernel, out_shape=[jax.ShapeDtypeStruct(shape, kind) for s...]
    unnamed x398 -> x426, local copies, waits for them, and re-layouts: 30.9 us -> 37.7 us
  transfers between devices with their start and end apart: 111 -> 111, of which waited for: 63 -> 65; matrix products, arithmetic and copies ran while one was open for 6% -> 3% of each run, Pallas kernels for 12% -> 13%
where the time goes in v5:
time: 669 us; the launch traced here: 662 us
  waiting for transfers between devices  321 us (48%)
  starting transfers between devices  171 us (26%)
  Pallas kernels  101 us (15%)
  local copies, waits for them, and re-layouts  46.3 us (7%)
  other arithmetic  18.3 us (3%)
    ppermute x99, waiting for transfers between devices, swap(): lax.ppermute(value, axis, [(i, i ^ mask) for i in range(lax.axis_size(axi...  319 us
    ppermute x99, starting transfers between devices, swap(): lax.ppermute(value, axis, [(i, i ^ mask) for i in range(lax.axis_size(axi...  147 us
    pallas_call x50, Pallas kernels, run(): pl.pallas_call(kernel, out_shape=[jax.ShapeDtypeStruct(shape, kind) for s...  94.3 us
    unnamed x426, local copies, waits for them, and re-layouts  37.7 us
  transfers between devices with their start and end apart: 111, of which 65 were waited for; matrix products, arithmetic and copies ran while one was open for 3% of the time, Pallas kernels for 13%

profile of v5, /device:TPU:0, one launch (start us, length us, event | category | flops | bytes accessed | tf_op | source)
XLA Modules:
  0.0 661.7 jit_solution(11894323118986970942)
XLA Ops:
  25.7 6.9 %collective-permute-done.1 = bf16[2,400,256]{2,1,0:T(8,128)(2,1)S(1)} collective-permute-done((bf16[2,400,256]{2,1,0:T(8,128)(2,1)S(1)}, bf16[2,400,256]{2,1,0:T(8,128)(2,1)S(1)}, u32[]{:S(2)}, u32[]{:S(2)}) %collective-permute-start.1) | collective-permute-done | bytes 409632 | tf_op jit(solution)/shard_map/ppermute | solution.py:24
  51.9 9.8 %collective-permute-done.12 = bf16[1,128,1792]{2,1,0:T(8,128)(2,1)S(1)} collective-permute-done((bf16[1,128,1792]{2,1,0:T(8,128)(2,1)S(1)}, bf16[1,128,1792]{2,1,0:T(8,128)(2,1)S(1)}, u32[]{:S(2)}, u32[]{:S(2)}) %collective-permute-start.12) | collective-permute-done | bytes 458784 | tf_op jit(solution)/shard_map/ppermute | solution.py:24
  71.6 20.0 %collective-permute-done.13 = bf16[2,128,256]{2,1,0:T(8,128)(2,1)S(1)} collective-permute-done((bf16[2,128,256]{2,1,0:T(8,128)(2,1)S(1)}, bf16[2,128,256]{2,1,0:T(8,128)(2,1)S(1)}, u32[]{:S(2)}, u32[]{:S(2)}) %collective-permute-start.13) | collective-permute-done | bytes 131104 | tf_op jit(solution)/shard_map/ppermute | solution.py:24
  92.8 7.2 %collective-permute-done.15 = bf16[2,128,256]{2,1,0:T(8,128)(2,1)S(1)} collective-permute-done((bf16[2,128,256]{2,1,0:T(8,128)(2,1)S(1)}, bf16[2,128,256]{2,1,0:T(8,128)(2,1)S(1)}, u32[]{:S(2)}, u32[]{:S(2)}) %collective-permute-start.15) | collective-permute-done | bytes 131104 | tf_op jit(solution)/shard_map/ppermute | solution.py:24
  114.6 12.9 %collective-permute-done.19 = bf16[2,128,1024]{2,1,0:T(8,128)(2,1)S(1)} collective-permute-done((bf16[2,128,1024]{2,1,0:T(8,128)(2,1)S(1)}, bf16[2,128,1024]{2,1,0:T(8,128)(2,1)S(1)}, u32[]{:S(2)}, u32[]{:S(2)}) %collective-permute-start.19) | collective-permute-done | bytes 524320 | tf_op jit(solution)/shard_map/ppermute | solution.py:24
  140.8 7.9 %collective-permute-done.25 = bf16[2,128,256]{2,1,0:T(8,128)(2,1)S(1)} collective-permute-done((bf16[2,128,256]{2,1,0:T(8,128)(2,1)S(1)}, bf16[2,128,256]{2,1,0:T(8,128)(2,1)S(1)}, u32[]{:S(2)}, u32[]{:S(2)}) %collective-permute-start.25) | collective-permute-done | bytes 131104 | tf_op jit(solution)/shard_map/ppermute | solution.py:24
  155.1 28.9 %collective-permute-done.26 = bf16[2,10,128,256]{3,2,1,0:T(8,128)(2,1)S(1)} collective-permute-done((bf16[2,10,128,256]{3,2,1,0:T(8,128)(2,1)S(1)}, bf16[2,10,128,256]{3,2,1,0:T(8,128)(2,1)S(1)}, u32[]{:S(2)}, u32[]{:S(2)}) %collective-permute-start.26) | collective-permute-done | bytes 1310752 | tf_op jit(solution)/shard_map/ppermute | solution.py:24
  207.2 8.4 %collective-permute-done.41 = bf16[2,128,1024]{2,1,0:T(8,128)(2,1)} collective-permute-done((bf16[2,128,1024]{2,1,0:T(8,128)(2,1)}, bf16[2,128,1024]{2,1,0:T(8,128)(2,1)}, u32[]{:S(2)}, u32[]{:S(2)}) %collective-permute-start.41) | collective-permute-done | bytes 524320 | tf_op jit(solution)/shard_map/ppermute | solution.py:24
  223.6 12.4 %collective-permute-done.32.rest_2_ = bf16[128,1024]{1,0:T(8,128)(2,1)S(1)} collective-permute-done((bf16[128,1024]{1,0:T(8,128)(2,1)}, bf16[128,1024]{1,0:T(8,128)(2,1)S(1)}, u32[]{:S(2)}, u32[]{:S(2)}) %collective-permute-start.32) | collective-permute-done | bytes 262176 | tf_op jit(solution)/shard_map/ppermute | solution.py:24
  236.7 7.5 %collective-permute-done.33.rest_3_ = bf16[128,1024]{1,0:T(8,128)(2,1)S(1)} collective-permute-done((bf16[128,1024]{1,0:T(8,128)(2,1)S(1)}, bf16[128,1024]{1,0:T(8,128)(2,1)S(1)}, u32[]{:S(2)}, u32[]{:S(2)}) %collective-permute-start.33) | collective-permute-done | bytes 262176 | tf_op jit(solution)/shard_map/ppermute | solution.py:24
  271.5 20.7 %collective-permute-start.46 = (bf16[4,8,128,256]{3,2,1,0:T(8,128)(2,1)S(1)}, bf16[4,8,128,256]{3,2,1,0:T(8,128)(2,1)S(1)}, u32[]{:S(2)}, u32[]{:S(2)}) collective-permute-start(bf16[4,8,128,256]{3,2,1,0:T(8,128)(2,1)S(1)} %pad_maximum_fusion.3.refs_0_), channel_id=1, source_target_pairs={{0,4},{4,0},{8,12},{12,8},{16,20},{20,16},{24,28},{28,24},{1,5},{5... | collective-permute-start | bytes 6291464 | tf_op jit(solution)/shard_map/ppermute | solution.py:24
  315.9 7.5 %collective-permute-done.49.other_ref.eo_ref = bf16[128,1024]{1,0:T(8,128)(2,1)S(1)} collective-permute-done((bf16[128,1024]{1,0:T(8,128)(2,1)S(1)}, bf16[128,1024]{1,0:T(8,128)(2,1)S(1)}, u32[]{:S(2)}, u32[]{:S(2)}) %collective-permute-start.49) | collective-permute-done | bytes 262176 | tf_op jit(solution)/shard_map/ppermute | solution.py:24
  348.7 6.9 %collective-permute-done.52 = bf16[2,128,256]{2,1,0:T(8,128)(2,1)S(1)} collective-permute-done((bf16[2,128,256]{2,1,0:T(8,128)(2,1)S(1)}, bf16[2,128,256]{2,1,0:T(8,128)(2,1)S(1)}, u32[]{:S(2)}, u32[]{:S(2)}) %collective-permute-start.52) | collective-permute-done | bytes 131104 | tf_op jit(solution)/shard_map/ppermute | solution.py:24
  360.7 9.0 %collective-permute-start.55 = (bf16[2,128,2048]{2,1,0:T(8,128)(2,1)S(1)}, bf16[2,128,2048]{2,1,0:T(8,128)(2,1)S(1)}, u32[]{:S(2)}, u32[]{:S(2)}) collective-permute-start(bf16[2,128,2048]{2,1,0:T(8,128)(2,1)S(1)} %bitcast.415), channel_id=1, source_target_pairs={{0,8},{4,12},{8,0},{12,4},{16,24},{20,28},{24,16},{28,20},{1,9},{5... | collective-permute-start | bytes 3145736 | tf_op jit(solution)/shard_map/ppermute | solution.py:24
  384.0 7.6 %collective-permute-done.60 = bf16[2,128,256]{2,1,0:T(8,128)(2,1)S(1)} collective-permute-done((bf16[2,128,256]{2,1,0:T(8,128)(2,1)S(1)}, bf16[2,128,256]{2,1,0:T(8,128)(2,1)S(1)}, u32[]{:S(2)}, u32[]{:S(2)}) %collective-permute-start.60) | collective-permute-done | bytes 131104 | tf_op jit(solution)/shard_map/ppermute | solution.py:24
  397.4 9.3 %collective-permute-start.61 = (bf16[128,2048]{1,0:T(8,128)(2,1)S(1)}, bf16[128,2048]{1,0:T(8,128)(2,1)S(1)}, u32[]{:S(2)}, u32[]{:S(2)}) collective-permute-start(bf16[128,2048]{1,0:T(8,128)(2,1)S(1)} %bitcast.422), channel_id=1, source_target_pairs={{0,16},{4,20},{8,24},{12,28},{16,0},{20,4},{24,8},{28,12},{1,17},{... | collective-permute-start | bytes 1572872 | tf_op jit(solution)/shard_map/ppermute | solution.py:24
  409.2 9.5 %collective-permute-done.61 = bf16[128,2048]{1,0:T(8,128)(2,1)S(1)} collective-permute-done((bf16[128,2048]{1,0:T(8,128)(2,1)S(1)}, bf16[128,2048]{1,0:T(8,128)(2,1)S(1)}, u32[]{:S(2)}, u32[]{:S(2)}) %collective-permute-start.61) | collective-permute-done | bytes 524320 | tf_op jit(solution)/shard_map/ppermute | solution.py:24
  428.5 9.4 %collective-permute-done.64 = bf16[2,128,256]{2,1,0:T(8,128)(2,1)S(1)} collective-permute-done((bf16[2,128,256]{2,1,0:T(8,128)(2,1)S(1)}, bf16[2,128,256]{2,1,0:T(8,128)(2,1)S(1)}, u32[]{:S(2)}, u32[]{:S(2)}) %collective-permute-start.64) | collective-permute-done | bytes 131104 | tf_op jit(solution)/shard_map/ppermute | solution.py:24
  464.8 11.0 %collective-permute-done.72 = bf16[4,2,128,256]{3,2,1,0:T(8,128)(2,1)S(1)} collective-permute-done((bf16[4,2,128,256]{3,2,1,0:T(8,128)(2,1)S(1)}, bf16[4,2,128,256]{3,2,1,0:T(8,128)(2,1)S(1)}, u32[]{:S(2)}, u32[]{:S(2)}) %collective-permute-start.72) | collective-permute-done | bytes 524320 | tf_op jit(solution)/shard_map/ppermute | solution.py:24
  560.1 10.2 %collective-permute-done.88 = bf16[7,128,256]{2,1,0:T(8,128)(2,1)S(1)} collective-permute-done((bf16[7,128,256]{2,1,0:T(8,128)(2,1)S(1)}, bf16[7,128,256]{2,1,0:T(8,128)(2,1)S(1)}, u32[]{:S(2)}, u32[]{:S(2)}) %collective-permute-start.88) | collective-permute-done | bytes 458784 | tf_op jit(solution)/shard_map/ppermute | solution.py:24
  571.1 10.5 %collective-permute-done.109 = bf16[2,3,128,256]{3,2,1,0:T(8,128)(2,1)S(1)} collective-permute-done((bf16[2,3,128,256]{3,2,1,0:T(8,128)(2,1)S(1)}, bf16[2,3,128,256]{3,2,1,0:T(8,128)(2,1)S(1)}, u32[]{:S(2)}, u32[]{:S(2)}) %collective-permute-start.109) | collective-permute-done | bytes 393248 | tf_op jit(solution)/shard_map/ppermute | solution.py:24
  584.7 7.8 %collective-permute-done.87 = bf16[2,128,2048]{2,1,0:T(8,128)(2,1)S(1)} collective-permute-done((bf16[2,128,2048]{2,1,0:T(8,128)(2,1)S(1)}, bf16[2,128,2048]{2,1,0:T(8,128)(2,1)S(1)}, u32[]{:S(2)}, u32[]{:S(2)}) %collective-permute-start.87) | collective-permute-done | bytes 1048608 | tf_op jit(solution)/shard_map/ppermute | solution.py:24
  623.0 7.0 %collective-permute-done.107 = bf16[128,2048]{1,0:T(8,128)(2,1)S(1)} collective-permute-done((bf16[128,2048]{1,0:T(8,128)(2,1)S(1)}, bf16[128,2048]{1,0:T(8,128)(2,1)S(1)}, u32[]{:S(2)}, u32[]{:S(2)}) %collective-permute-start.107) | collective-permute-done | bytes 524320 | tf_op jit(solution)/shard_map/ppermute | solution.py:24
  645.0 6.6 collective-permute-done.108
  (806 shorter events, 402.2 us)
Async XLA Ops:
  3.1 29.9 %collective-permute-start.3 = (bf16[128,1280]{1,0:T(8,128)(2,1)S(1)}, bf16[128,1280]{1,0:T(8,128)(2,1)S(1)}, u32[]{:S(2)}, u32[]{:S(2)}) collective-permute-start(bf16[128,1280]{1,0:T(8,128)(2,1)S(1)} %pad_maximum_fusion.28.rest_0_), channel_id=1, source_target_pairs={{0,1},{1,0},{2,3},{3,2},{4,5},{5,4},{6,7},{7,6},{8,9},{9,8},{10,11... | collective-permute-start | bytes 983048 | tf_op jit(solution)/shard_map/ppermute | solution.py:24
  6.2 27.5 %collective-permute-start.4 = (bf16[128,1280]{1,0:T(8,128)(2,1)S(1)}, bf16[128,1280]{1,0:T(8,128)(2,1)S(1)}, u32[]{:S(2)}, u32[]{:S(2)}) collective-permute-start(bf16[128,1280]{1,0:T(8,128)(2,1)S(1)} %pad_maximum_fusion.28.rest_0_), channel_id=1, source_target_pairs={{0,2},{1,3},{2,0},{3,1},{4,6},{5,7},{6,4},{7,5},{8,10},{9,11},{10,... | collective-permute-start | bytes 983048 | tf_op jit(solution)/shard_map/ppermute | solution.py:24
  8.8 25.5 %collective-permute-start.5 = (bf16[128,1280]{1,0:T(8,128)(2,1)S(1)}, bf16[128,1280]{1,0:T(8,128)(2,1)S(1)}, u32[]{:S(2)}, u32[]{:S(2)}) collective-permute-start(bf16[128,1280]{1,0:T(8,128)(2,1)S(1)} %pad_maximum_fusion.28.rest_0_), channel_id=1, source_target_pairs={{0,3},{1,2},{2,1},{3,0},{4,7},{5,6},{6,5},{7,4},{8,11},{9,10},{10,... | collective-permute-start | bytes 983048 | tf_op jit(solution)/shard_map/ppermute | solution.py:24
  19.9 32.0 %collective-permute-start.6 = (bf16[1,7,128,256]{3,2,1,0:T(8,128)(2,1)}, bf16[1,7,128,256]{3,2,1,0:T(8,128)(2,1)}, u32[]{:S(2)}, u32[]{:S(2)}) collective-permute-start(bf16[1,7,128,256]{3,2,1,0:T(8,128)(2,1)} %maximum_bitcast_fusion.2), channel_id=1, source_target_pairs={{0,8},{4,12},{8,0},{12,4},{16,24},{20,28},{24,16},{28,20},{1,9},{5... | collective-permute-start | bytes 1376264 | tf_op jit(solution)/shard_map/ppermute | solution.py:24
  36.6 25.1 %collective-permute-start.7 = (bf16[1,8,128,256]{3,2,1,0:T(8,128)(2,1)}, bf16[1,8,128,256]{3,2,1,0:T(8,128)(2,1)S(1)}, u32[]{:S(2)}, u32[]{:S(2)}) collective-permute-start(bf16[1,8,128,256]{3,2,1,0:T(8,128)(2,1)} %bitcast.468), channel_id=1, source_target_pairs={{0,16},{4,20},{8,24},{12,28},{16,0},{20,4},{24,8},{28,12},{1,17},{... | collective-permute-start | bytes 1572872 | tf_op jit(solution)/shard_map/ppermute | solution.py:24
  63.4 36.6 %collective-permute-start.10 = (bf16[2,7,128,256]{3,2,1,0:T(8,128)(2,1)S(1)}, bf16[2,7,128,256]{3,2,1,0:T(8,128)(2,1)S(1)}, u32[]{:S(2)}, u32[]{:S(2)}) collective-permute-start(bf16[2,7,128,256]{3,2,1,0:T(8,128)(2,1)S(1)} %pad_maximum_fusion.13), channel_id=1, source_target_pairs={{0,16},{4,20},{8,24},{12,28},{16,0},{20,4},{24,8},{28,12},{1,17},{... | collective-permute-start | bytes 2752520 | tf_op jit(solution)/shard_map/ppermute | solution.py:24
  64.8 35.2 %collective-permute-start.11 = (bf16[2,8,128,256]{3,2,1,0:T(8,128)(2,1)S(1)}, bf16[2,8,128,256]{3,2,1,0:T(8,128)(2,1)S(1)}, u32[]{:S(2)}, u32[]{:S(2)}) collective-permute-start(bf16[2,8,128,256]{3,2,1,0:T(8,128)(2,1)S(1)} %pad_maximum_fusion.10), channel_id=1, source_target_pairs={{0,8},{4,12},{8,0},{12,4},{16,24},{20,28},{24,16},{28,20},{1,9},{5... | collective-permute-start | bytes 3145736 | tf_op jit(solution)/shard_map/ppermute | solution.py:24
  65.7 25.8 %collective-permute-start.14 = (bf16[2,128,1792]{2,1,0:T(8,128)(2,1)S(1)}, bf16[2,128,1792]{2,1,0:T(8,128)(2,1)S(1)}, u32[]{:S(2)}, u32[]{:S(2)}) collective-permute-start(bf16[2,128,1792]{2,1,0:T(8,128)(2,1)S(1)} %pad_maximum_fusion.14), channel_id=1, source_target_pairs={{0,1},{1,0},{2,3},{3,2},{4,5},{5,4},{6,7},{7,6},{8,9},{9,8},{10,11... | collective-permute-start | bytes 2752520 | tf_op jit(solution)/shard_map/ppermute | solution.py:24
  102.4 25.0 %collective-permute-start.19 = (bf16[2,128,1024]{2,1,0:T(8,128)(2,1)S(1)}, bf16[2,128,1024]{2,1,0:T(8,128)(2,1)S(1)}, u32[]{:S(2)}, u32[]{:S(2)}) collective-permute-start(bf16[2,128,1024]{2,1,0:T(8,128)(2,1)S(1)} %copy-done.195), channel_id=1, source_target_pairs={{0,2},{1,3},{2,0},{3,1},{4,6},{5,7},{6,4},{7,5},{8,10},{9,11},{10,... | collective-permute-start | bytes 1572872 | tf_op jit(solution)/shard_map/ppermute | solution.py:24
  152.8 35.5 %collective-permute-start.27 = (bf16[2,12,128,256]{3,2,1,0:T(8,128)(2,1)S(1)}, bf16[2,12,128,256]{3,2,1,0:T(8,128)(2,1)S(1)}, u32[]{:S(2)}, u32[]{:S(2)}) collective-permute-start(bf16[2,12,128,256]{3,2,1,0:T(8,128)(2,1)S(1)} %pad_maximum_fusion.6), channel_id=1, source_target_pairs={{0,8},{4,12},{8,0},{12,4},{16,24},{20,28},{24,16},{28,20},{1,9},{5... | collective-permute-start | bytes 4718600 | tf_op jit(solution)/shard_map/ppermute | solution.py:24
  154.7 29.3 %collective-permute-start.26 = (bf16[2,10,128,256]{3,2,1,0:T(8,128)(2,1)S(1)}, bf16[2,10,128,256]{3,2,1,0:T(8,128)(2,1)S(1)}, u32[]{:S(2)}, u32[]{:S(2)}) collective-permute-start(bf16[2,10,128,256]{3,2,1,0:T(8,128)(2,1)S(1)} %pad_maximum_fusion.7), channel_id=1, source_target_pairs={{0,16},{4,20},{8,24},{12,28},{16,0},{20,4},{24,8},{28,12},{1,17},{... | collective-permute-start | bytes 3932168 | tf_op jit(solution)/shard_map/ppermute | solution.py:24
  188.6 26.9 %collective-permute-start.41 = (bf16[2,128,1024]{2,1,0:T(8,128)(2,1)}, bf16[2,128,1024]{2,1,0:T(8,128)(2,1)}, u32[]{:S(2)}, u32[]{:S(2)}) collective-permute-start(bf16[2,128,1024]{2,1,0:T(8,128)(2,1)} %param.41), channel_id=1, source_target_pairs={{0,2},{1,3},{2,0},{3,1},{4,6},{5,7},{6,4},{7,5},{8,10},{9,11},{10,... | collective-permute-start | bytes 1572872 | tf_op jit(solution)/shard_map/ppermute | solution.py:24
  236.1 34.9 %collective-permute-start.44 = (bf16[2,8,128,256]{3,2,1,0:T(8,128)(2,1)S(1)}, bf16[2,8,128,256]{3,2,1,0:T(8,128)(2,1)S(1)}, u32[]{:S(2)}, u32[]{:S(2)}) collective-permute-start(bf16[2,8,128,256]{3,2,1,0:T(8,128)(2,1)S(1)} %pad_maximum_fusion.11), channel_id=1, source_target_pairs={{0,16},{4,20},{8,24},{12,28},{16,0},{20,4},{24,8},{28,12},{1,17},{... | collective-permute-start | bytes 3145736 | tf_op jit(solution)/shard_map/ppermute | solution.py:24
  245.1 26.2 %collective-permute-start.45 = (bf16[2,8,128,256]{3,2,1,0:T(8,128)(2,1)S(1)}, bf16[2,8,128,256]{3,2,1,0:T(8,128)(2,1)S(1)}, u32[]{:S(2)}, u32[]{:S(2)}) collective-permute-start(bf16[2,8,128,256]{3,2,1,0:T(8,128)(2,1)S(1)} %pad_maximum_fusion.12), channel_id=1, source_target_pairs={{0,8},{4,12},{8,0},{12,4},{16,24},{20,28},{24,16},{28,20},{1,9},{5... | collective-permute-start | bytes 3145736 | tf_op jit(solution)/shard_map/ppermute | solution.py:24
  360.7 33.1 %collective-permute-start.55 = (bf16[2,128,2048]{2,1,0:T(8,128)(2,1)S(1)}, bf16[2,128,2048]{2,1,0:T(8,128)(2,1)S(1)}, u32[]{:S(2)}, u32[]{:S(2)}) collective-permute-start(bf16[2,128,2048]{2,1,0:T(8,128)(2,1)S(1)} %bitcast.415), channel_id=1, source_target_pairs={{0,8},{4,12},{8,0},{12,4},{16,24},{20,28},{24,16},{28,20},{1,9},{5... | collective-permute-start | bytes 3145736 | tf_op jit(solution)/shard_map/ppermute | solution.py:24
  409.1 32.3 %collective-permute-start.66 = (bf16[6,2,2,128,256]{4,3,2,1,0:T(8,128)(2,1)S(1)}, bf16[6,2,2,128,256]{4,3,2,1,0:T(8,128)(2,1)S(1)}, u32[]{:S(2)}, u32[]{:S(2)}) collective-permute-start(bf16[6,2,2,128,256]{4,3,2,1,0:T(8,128)(2,1)S(1)} %bitcast.409), channel_id=1, source_target_pairs={{0,4},{4,0},{8,12},{12,8},{16,20},{20,16},{24,28},{28,24},{1,5},{5... | collective-permute-start | bytes 4718600 | tf_op jit(solution)/shard_map/ppermute | solution.py:24
  454.6 38.8 %collective-permute-start.76 = (bf16[128,1024]{1,0:T(8,128)(2,1)S(1)}, bf16[128,1024]{1,0:T(8,128)(2,1)S(1)}, u32[]{:S(2)}, u32[]{:S(2)}) collective-permute-start(bf16[128,1024]{1,0:T(8,128)(2,1)S(1)} %get-tuple-element.504.own_ref.e_ref), channel_id=1, source_target_pairs={{0,1},{1,0},{2,3},{3,2},{4,5},{5,4},{6,7},{7,6},{8,9},{9,8},{10,11... | collective-permute-start | bytes 786440 | tf_op jit(solution)/shard_map/ppermute | solution.py:24
  463.6 29.9 %collective-permute-start.75 = (bf16[2,128,1024]{2,1,0:T(8,128)(2,1)S(1)}, bf16[2,128,1024]{2,1,0:T(8,128)(2,1)S(1)}, u32[]{:S(2)}, u32[]{:S(2)}) collective-permute-start(bf16[2,128,1024]{2,1,0:T(8,128)(2,1)S(1)} %fusion.3), channel_id=1, source_target_pairs={{0,2},{1,3},{2,0},{3,1},{4,6},{5,7},{6,4},{7,5},{8,10},{9,11},{10,... | collective-permute-start | bytes 1572872 | tf_op jit(solution)/shard_map/ppermute | solution.py:24
  508.4 27.3 %collective-permute-start.82 = (bf16[2,2,128,2048]{3,2,1,0:T(8,128)(2,1)}, bf16[2,2,128,2048]{3,2,1,0:T(8,128)(2,1)}, u32[]{:S(2)}, u32[]{:S(2)}) collective-permute-start(bf16[2,2,128,2048]{3,2,1,0:T(8,128)(2,1)} %bitcast.146), channel_id=1, source_target_pairs={{0,4},{4,0},{8,12},{12,8},{16,20},{20,16},{24,28},{28,24},{1,5},{5... | collective-permute-start | bytes 6291464 | tf_op jit(solution)/shard_map/ppermute | solution.py:24
  508.4 27.3 %collective-permute-start.83 = (bf16[2,2,128,2048]{3,2,1,0:T(8,128)(2,1)}, bf16[2,2,128,2048]{3,2,1,0:T(8,128)(2,1)}, u32[]{:S(2)}, u32[]{:S(2)}) collective-permute-start(bf16[2,2,128,2048]{3,2,1,0:T(8,128)(2,1)} %bitcast.147), channel_id=1, source_target_pairs={{0,4},{4,0},{8,12},{12,8},{16,20},{20,16},{24,28},{28,24},{1,5},{5... | collective-permute-start | bytes 6291464 | tf_op jit(solution)/shard_map/ppermute | solution.py:24
  523.3 32.4 %collective-permute-start.84 = (bf16[1,128,1024]{2,1,0:T(8,128)(2,1)S(1)}, bf16[1,128,1024]{2,1,0:T(8,128)(2,1)S(1)}, u32[]{:S(2)}, u32[]{:S(2)}) collective-permute-start(bf16[1,128,1024]{2,1,0:T(8,128)(2,1)S(1)} %fusion.16), channel_id=1, source_target_pairs={{0,2},{1,3},{2,0},{3,1},{4,6},{5,7},{6,4},{7,5},{8,10},{9,11},{10,... | collective-permute-start | bytes 786440 | tf_op jit(solution)/shard_map/ppermute | solution.py:24
  541.9 28.4 %collective-permute-start.89 = (bf16[2,512,256]{2,1,0:T(8,128)(2,1)S(1)}, bf16[2,512,256]{2,1,0:T(8,128)(2,1)S(1)}, u32[]{:S(2)}, u32[]{:S(2)}) collective-permute-start(bf16[2,512,256]{2,1,0:T(8,128)(2,1)S(1)} %get-tuple-element.544), channel_id=1, source_target_pairs={{4,0},{8,4},{12,8},{16,12},{20,16},{24,20},{28,24},{5,1},{9,5},{13... | collective-permute-start | bytes 1572872 | tf_op jit(solution)/shard_map/ppermute | solution.py:1494
  543.3 26.9 %collective-permute-start.90 = (bf16[2,512,256]{2,1,0:T(8,128)(2,1)S(1)}, bf16[2,512,256]{2,1,0:T(8,128)(2,1)S(1)}, u32[]{:S(2)}, u32[]{:S(2)}) collective-permute-start(bf16[2,512,256]{2,1,0:T(8,128)(2,1)S(1)} %get-tuple-element.545), channel_id=1, source_target_pairs={{0,4},{4,8},{8,12},{12,16},{16,20},{20,24},{24,28},{1,5},{5,9},{9,... | collective-permute-start | bytes 1572872 | tf_op jit(solution)/shard_map/ppermute | solution.py:1495
  559.9 32.6 %collective-permute-start.87 = (bf16[2,128,2048]{2,1,0:T(8,128)(2,1)S(1)}, bf16[2,128,2048]{2,1,0:T(8,128)(2,1)S(1)}, u32[]{:S(2)}, u32[]{:S(2)}) collective-permute-start(bf16[2,128,2048]{2,1,0:T(8,128)(2,1)S(1)} %bitcast.411), channel_id=1, source_target_pairs={{0,16},{4,20},{8,24},{12,28},{16,0},{20,4},{24,8},{28,12},{1,17},{... | collective-permute-start | bytes 3145736 | tf_op jit(solution)/shard_map/ppermute | solution.py:24
  (295 other events, 3719.5 us)

commit v6 on v5

--- a/solution.py
+++ b/solution.py
@@ -1314,6 +1314,12 @@
     (self_qkv, own_up), (enc_out_w, own_down) = plan1.result()
     enc_wide = Spread(join(enc_ffn_w, *r2), "tensor", wide_down)
     enc_wide.hop()
+    dec_own = join(dec_ffn_w, *r2)
+    plan0 = Pair(
+        (jnp.concatenate(ups([dec_own])), jnp.concatenate(downs([dec_own]))),
+        ([slices], [slices]),
+    )
+    due(plan0.hop())
     for step in range(len(t_down) - 1):
         dec_pieces = dec_steps.send(r2)
 
@@ -1322,6 +1328,7 @@
     )
     hid_other = swap(hid_low, "tensor", 1)
     r3 = (hid_other,)
+    second_hop = plan0.hop(hid_low)
     flat_s, pair_s, query_s = project(
         fg(join(dec_pieces, hid_low)), self_qkv, local, (SELF_ATT, None, SELF_ATT + 1), t_ref
     )
@@ -1341,7 +1348,8 @@
     plan2.hop()
     window_s = halo(pair_s)
     r4 = (window_s[0], window_s[2])
-    mixed_s, mixed_t_s, totals_s = attend_fg(fg(query_s), window_s, text)
+    plan0.hop(*r4)
+    mixed_s, mixed_t_s, totals_s = attend_fg(fg(join(query_s, second_hop)), window_s, text)
     mixed_s = exchange(mixed_s)
     r5 = tuple(mixed_s[1:])
     plan2.hop(*r5)
@@ -1353,10 +1361,9 @@
     active_e, slope_e, keep, send = ffn_up_down(hid_low, hid_other, enc_views, enc_first)
     came = swap(send, "tensor", 1)
     r7 = (came,)
-    shards = dec_wide.result(send)
+    shards = dec_wide.result(send)[1:]
     plan4 = Pair(
-        (jnp.concatenate(ups(shards)), jnp.concatenate(downs(shards))),
-        ([slices + far], [slices + far]),
+        (jnp.concatenate(ups(shards)), jnp.concatenate(downs(shards))), ([far], [far])
     )
     plan4.hop()
 
@@ -1381,7 +1388,9 @@
     plan4.hop(*r9)
     mixed_c, mixed_t_c, totals_c = attend_fg(query_c, window_c, both)
     mixed_c = exchange(mixed_c)
-    dec_views = ffn_views([array for (array,) in plan4.result()])
+    dec_views = ffn_views(
+        [array for (array,) in plan0.result()], [array for (array,) in plan4.result()]
+    )
     summed_c, crossed, crossed_low = out_norm(
         mixed_c, cross_out_w, decoded, table, CROSS_ATT + 2
     )

time: 669 us -> 663 us (level)
  waiting for transfers between devices: 321 us -> 307 us
  Pallas kernels: 101 us -> 112 us
  starting transfers between devices: 171 us -> 161 us
    ppermute x99 -> x105, waiting for transfers between devices: 319 us -> 305 us  [swap(): lax.ppermute(value, axis, [(i, i ^ mask) for i in range(lax.axis_size(axi...]
    ppermute x99 -> x105, starting transfers between devices: 147 us -> 137 us  [swap(): lax.ppermute(value, axis, [(i, i ^ mask) for i in range(lax.axis_size(axi...]
    pallas_call x50, Pallas kernels: 94.3 us -> 104 us  [run(): pl.pallas_call(kernel, out_shape=[jax.ShapeDtypeStruct(shape, kind) for s...]
    unnamed x426 -> x444, local copies, waits for them, and re-layouts: 37.7 us -> 37.3 us
  transfers between devices with their start and end apart: 111 -> 117, of which waited for: 65 -> 61; matrix products, arithmetic and copies ran while one was open for 3% -> 4% of each run, Pallas kernels for 13% -> 15%
where the time goes in v6:
time: 663 us; the launch traced here: 652 us
  waiting for transfers between devices  307 us (46%)
  starting transfers between devices  161 us (24%)
  Pallas kernels  112 us (17%)
  local copies, waits for them, and re-layouts  46.2 us (7%)
  other arithmetic  20.8 us (3%)
    ppermute x105, waiting for transfers between devices, swap(): lax.ppermute(value, axis, [(i, i ^ mask) for i in range(lax.axis_size(axi...  305 us
    ppermute x105, starting transfers between devices, swap(): lax.ppermute(value, axis, [(i, i ^ mask) for i in range(lax.axis_size(axi...  137 us
    pallas_call x50, Pallas kernels, run(): pl.pallas_call(kernel, out_shape=[jax.ShapeDtypeStruct(shape, kind) for s...  104 us
    unnamed x444, local copies, waits for them, and re-layouts  37.3 us
  transfers between devices with their start and end apart: 117, of which 61 were waited for; matrix products, arithmetic and copies ran while one was open for 4% of the time, Pallas kernels for 15%

profile of v6, /device:TPU:0, one launch (start us, length us, event | category | flops | bytes accessed | tf_op | source)
XLA Modules:
  0.0 651.9 jit_solution(14931676565653314139)
XLA Ops:
  25.7 6.9 %collective-permute-done.1 = bf16[2,400,256]{2,1,0:T(8,128)(2,1)S(1)} collective-permute-done((bf16[2,400,256]{2,1,0:T(8,128)(2,1)S(1)}, bf16[2,400,256]{2,1,0:T(8,128)(2,1)S(1)}, u32[]{:S(2)}, u32[]{:S(2)}) %collective-permute-start.1) | collective-permute-done | bytes 409632 | tf_op jit(solution)/shard_map/ppermute | solution.py:24
  51.9 9.8 %collective-permute-done.12 = bf16[1,128,1792]{2,1,0:T(8,128)(2,1)S(1)} collective-permute-done((bf16[1,128,1792]{2,1,0:T(8,128)(2,1)S(1)}, bf16[1,128,1792]{2,1,0:T(8,128)(2,1)S(1)}, u32[]{:S(2)}, u32[]{:S(2)}) %collective-permute-start.12) | collective-permute-done | bytes 458784 | tf_op jit(solution)/shard_map/ppermute | solution.py:24
  72.2 19.3 %collective-permute-done.13 = bf16[2,128,256]{2,1,0:T(8,128)(2,1)S(1)} collective-permute-done((bf16[2,128,256]{2,1,0:T(8,128)(2,1)S(1)}, bf16[2,128,256]{2,1,0:T(8,128)(2,1)S(1)}, u32[]{:S(2)}, u32[]{:S(2)}) %collective-permute-start.13) | collective-permute-done | bytes 131104 | tf_op jit(solution)/shard_map/ppermute | solution.py:24
  92.8 7.2 %collective-permute-done.15 = bf16[2,128,256]{2,1,0:T(8,128)(2,1)S(1)} collective-permute-done((bf16[2,128,256]{2,1,0:T(8,128)(2,1)S(1)}, bf16[2,128,256]{2,1,0:T(8,128)(2,1)S(1)}, u32[]{:S(2)}, u32[]{:S(2)}) %collective-permute-start.15) | collective-permute-done | bytes 131104 | tf_op jit(solution)/shard_map/ppermute | solution.py:24
  169.5 23.1 %collective-permute-done.30 = bf16[2,10,128,256]{3,2,1,0:T(8,128)(2,1)S(1)} collective-permute-done((bf16[2,10,128,256]{3,2,1,0:T(8,128)(2,1)S(1)}, bf16[2,10,128,256]{3,2,1,0:T(8,128)(2,1)S(1)}, u32[]{:S(2)}, u32[]{:S(2)}) %collective-permute-start.30) | collective-permute-done | bytes 1310752 | tf_op jit(solution)/shard_map/ppermute | solution.py:24
  230.8 8.5 %collective-permute-done.36.rest_2_ = bf16[128,1024]{1,0:T(8,128)(2,1)S(1)} collective-permute-done((bf16[128,1024]{1,0:T(8,128)(2,1)}, bf16[128,1024]{1,0:T(8,128)(2,1)S(1)}, u32[]{:S(2)}, u32[]{:S(2)}) %collective-permute-start.36) | collective-permute-done | bytes 262176 | tf_op jit(solution)/shard_map/ppermute | solution.py:24
  270.6 11.5 %collective-permute-start.52 = (bf16[4,4,128,256]{3,2,1,0:T(8,128)(2,1)S(1)}, bf16[4,4,128,256]{3,2,1,0:T(8,128)(2,1)S(1)}, u32[]{:S(2)}, u32[]{:S(2)}) collective-permute-start(bf16[4,4,128,256]{3,2,1,0:T(8,128)(2,1)S(1)} %pad_maximum_fusion.11.refs_0_), channel_id=1, source_target_pairs={{0,4},{4,0},{8,12},{12,8},{16,20},{20,16},{24,28},{28,24},{1,5},{5... | collective-permute-start | bytes 3145736 | tf_op jit(solution)/shard_map/ppermute | solution.py:24
  294.2 7.3 %collective-permute-done.44.other_ref.xo_ref = bf16[128,1024]{1,0:T(8,128)(2,1)S(1)} collective-permute-done((bf16[128,1024]{1,0:T(8,128)(2,1)S(1)}, bf16[128,1024]{1,0:T(8,128)(2,1)S(1)}, u32[]{:S(2)}, u32[]{:S(2)}) %collective-permute-start.44) | collective-permute-done | bytes 262176 | tf_op jit(solution)/shard_map/ppermute | solution.py:24
  307.3 7.2 %collective-permute-done.54.rest_2_ = bf16[128,1024]{1,0:T(8,128)(2,1)S(1)} collective-permute-done((bf16[128,1024]{1,0:T(8,128)(2,1)S(1)}, bf16[128,1024]{1,0:T(8,128)(2,1)S(1)}, u32[]{:S(2)}, u32[]{:S(2)}) %collective-permute-start.54) | collective-permute-done | bytes 262176 | tf_op jit(solution)/shard_map/ppermute | solution.py:24
  318.0 6.0 collective-permute-done.55.other_ref.eo_ref
  350.9 6.6 %collective-permute-done.58 = bf16[2,128,256]{2,1,0:T(8,128)(2,1)S(1)} collective-permute-done((bf16[2,128,256]{2,1,0:T(8,128)(2,1)S(1)}, bf16[2,128,256]{2,1,0:T(8,128)(2,1)S(1)}, u32[]{:S(2)}, u32[]{:S(2)}) %collective-permute-start.58) | collective-permute-done | bytes 131104 | tf_op jit(solution)/shard_map/ppermute | solution.py:24
  364.7 7.2 %attend_back.3 = (bf16[512,256]{1,0:T(8,128)(2,1)S(1)}, bf16[2,512,256]{2,1,0:T(8,128)(2,1)S(1)}, f32[2,512,256]{2,1,0:T(8,128)S(1)}, bf16[2,512,256]{2,1,0:T(8,128)(2,1)S(1)}) custom-call(s32[4]{0:T(128)S(1)} %copy-done.193, s32[1]{0:T(128)} %bitcast.t_ref, s32[8,512]{1,0:T(8,128)S(1)} %copy-done.173, bf16[512,256]{1,0:T(8,128)(2,1)S(1)} %copy-done.152, ...), custom_call_target="tpu_custom_call" | custom-call | flops 30000001024 | bytes 1 | tf_op jit(solution)/shard_map/attend_back/pallas_call | solution.py:278
  380.2 7.5 %collective-permute-done.66 = bf16[2,128,256]{2,1,0:T(8,128)(2,1)S(1)} collective-permute-done((bf16[2,128,256]{2,1,0:T(8,128)(2,1)S(1)}, bf16[2,128,256]{2,1,0:T(8,128)(2,1)S(1)}, u32[]{:S(2)}, u32[]{:S(2)}) %collective-permute-start.66) | collective-permute-done | bytes 131104 | tf_op jit(solution)/shard_map/ppermute | solution.py:24
  392.4 9.3 %collective-permute-start.67 = (bf16[128,2048]{1,0:T(8,128)(2,1)S(1)}, bf16[128,2048]{1,0:T(8,128)(2,1)S(1)}, u32[]{:S(2)}, u32[]{:S(2)}) collective-permute-start(bf16[128,2048]{1,0:T(8,128)(2,1)S(1)} %bitcast.418), channel_id=1, source_target_pairs={{0,16},{4,20},{8,24},{12,28},{16,0},{20,4},{24,8},{28,12},{1,17},{... | collective-permute-start | bytes 1572872 | tf_op jit(solution)/shard_map/ppermute | solution.py:24
  404.2 9.6 %collective-permute-done.67 = bf16[128,2048]{1,0:T(8,128)(2,1)S(1)} collective-permute-done((bf16[128,2048]{1,0:T(8,128)(2,1)S(1)}, bf16[128,2048]{1,0:T(8,128)(2,1)S(1)}, u32[]{:S(2)}, u32[]{:S(2)}) %collective-permute-start.67) | collective-permute-done | bytes 524320 | tf_op jit(solution)/shard_map/ppermute | solution.py:24
  423.5 9.3 %collective-permute-done.70 = bf16[2,128,256]{2,1,0:T(8,128)(2,1)S(1)} collective-permute-done((bf16[2,128,256]{2,1,0:T(8,128)(2,1)S(1)}, bf16[2,128,256]{2,1,0:T(8,128)(2,1)S(1)}, u32[]{:S(2)}, u32[]{:S(2)}) %collective-permute-start.70) | collective-permute-done | bytes 131104 | tf_op jit(solution)/shard_map/ppermute | solution.py:24
  436.6 7.5 %attend_back.4 = (bf16[512,256]{1,0:T(8,128)(2,1)S(1)}, bf16[2,512,256]{2,1,0:T(8,128)(2,1)S(1)}, f32[2,512,256]{2,1,0:T(8,128)S(1)}, bf16[2,512,256]{2,1,0:T(8,128)(2,1)S(1)}) custom-call(s32[4]{0:T(128)S(1)} %copy-done.196, s32[1]{0:T(128)} %bitcast.t_ref, s32[8,512]{1,0:T(8,128)S(1)} %copy-done.176, bf16[512,256]{1,0:T(8,128)(2,1)S(1)} %copy-done.146, ...), custom_call_target="tpu_custom_call" | custom-call | flops 30000001024 | bytes 1 | tf_op jit(solution)/shard_map/attend_back/pallas_call | solution.py:278
  460.2 9.9 %collective-permute-done.78 = bf16[4,2,128,256]{3,2,1,0:T(8,128)(2,1)S(1)} collective-permute-done((bf16[4,2,128,256]{3,2,1,0:T(8,128)(2,1)S(1)}, bf16[4,2,128,256]{3,2,1,0:T(8,128)(2,1)S(1)}, u32[]{:S(2)}, u32[]{:S(2)}) %collective-permute-start.78) | collective-permute-done | bytes 524320 | tf_op jit(solution)/shard_map/ppermute | solution.py:24
  519.7 10.2 %collective-permute-done.87 = bf16[2,128,256]{2,1,0:T(8,128)(2,1)S(1)} collective-permute-done((bf16[2,128,256]{2,1,0:T(8,128)(2,1)S(1)}, bf16[2,128,256]{2,1,0:T(8,128)(2,1)S(1)}, u32[]{:S(2)}, u32[]{:S(2)}) %collective-permute-start.87) | collective-permute-done | bytes 131104 | tf_op jit(solution)/shard_map/ppermute | solution.py:24
  534.3 7.1 %attend_back.5 = (bf16[512,256]{1,0:T(8,128)(2,1)S(1)}, bf16[2,512,256]{2,1,0:T(8,128)(2,1)S(1)}, f32[2,512,256]{2,1,0:T(8,128)S(1)}, bf16[2,512,256]{2,1,0:T(8,128)(2,1)S(1)}) custom-call(s32[4]{0:T(128)S(1)} %copy-done.194, s32[1]{0:T(128)} %bitcast.t_ref, s32[8,512]{1,0:T(8,128)S(1)} %copy-done.174, bf16[512,256]{1,0:T(8,128)(2,1)S(1)} %copy-done.148, ...), custom_call_target="tpu_custom_call" | custom-call | flops 30000001024 | bytes 1 | tf_op jit(solution)/shard_map/attend_back/pallas_call | solution.py:278
  559.3 10.1 %collective-permute-done.115 = bf16[2,3,128,256]{3,2,1,0:T(8,128)(2,1)S(1)} collective-permute-done((bf16[2,3,128,256]{3,2,1,0:T(8,128)(2,1)S(1)}, bf16[2,3,128,256]{3,2,1,0:T(8,128)(2,1)S(1)}, u32[]{:S(2)}, u32[]{:S(2)}) %collective-permute-start.115) | collective-permute-done | bytes 393248 | tf_op jit(solution)/shard_map/ppermute | solution.py:24
  571.2 10.0 %collective-permute-done.92 = bf16[2,128,2048]{2,1,0:T(8,128)(2,1)S(1)} collective-permute-done((bf16[2,128,2048]{2,1,0:T(8,128)(2,1)S(1)}, bf16[2,128,2048]{2,1,0:T(8,128)(2,1)S(1)}, u32[]{:S(2)}, u32[]{:S(2)}) %collective-permute-start.92) | collective-permute-done | bytes 1048608 | tf_op jit(solution)/shard_map/ppermute | solution.py:24
  612.5 8.4 %collective-permute-done.113 = bf16[128,2048]{1,0:T(8,128)(2,1)S(1)} collective-permute-done((bf16[128,2048]{1,0:T(8,128)(2,1)S(1)}, bf16[128,2048]{1,0:T(8,128)(2,1)S(1)}, u32[]{:S(2)}, u32[]{:S(2)}) %collective-permute-start.113) | collective-permute-done | bytes 524320 | tf_op jit(solution)/shard_map/ppermute | solution.py:24
  634.7 7.6 %collective-permute-done.114 = bf16[2,128,1024]{2,1,0:T(8,128)(2,1)S(1)} collective-permute-done((bf16[2,128,1024]{2,1,0:T(8,128)(2,1)S(1)}, bf16[2,128,1024]{2,1,0:T(8,128)(2,1)S(1)}, u32[]{:S(2)}, u32[]{:S(2)}) %collective-permute-start.114) | collective-permute-done | bytes 524320 | tf_op jit(solution)/shard_map/ppermute | solution.py:24
  (840 shorter events, 420.3 us)
Async XLA Ops:
  3.1 29.9 %collective-permute-start.3 = (bf16[128,1280]{1,0:T(8,128)(2,1)S(1)}, bf16[128,1280]{1,0:T(8,128)(2,1)S(1)}, u32[]{:S(2)}, u32[]{:S(2)}) collective-permute-start(bf16[128,1280]{1,0:T(8,128)(2,1)S(1)} %pad_maximum_fusion.32.rest_0_), channel_id=1, source_target_pairs={{0,1},{1,0},{2,3},{3,2},{4,5},{5,4},{6,7},{7,6},{8,9},{9,8},{10,11... | collective-permute-start | bytes 983048 | tf_op jit(solution)/shard_map/ppermute | solution.py:24
  6.2 27.5 %collective-permute-start.4 = (bf16[128,1280]{1,0:T(8,128)(2,1)S(1)}, bf16[128,1280]{1,0:T(8,128)(2,1)S(1)}, u32[]{:S(2)}, u32[]{:S(2)}) collective-permute-start(bf16[128,1280]{1,0:T(8,128)(2,1)S(1)} %pad_maximum_fusion.32.rest_0_), channel_id=1, source_target_pairs={{0,2},{1,3},{2,0},{3,1},{4,6},{5,7},{6,4},{7,5},{8,10},{9,11},{10,... | collective-permute-start | bytes 983048 | tf_op jit(solution)/shard_map/ppermute | solution.py:24
  8.8 25.5 %collective-permute-start.5 = (bf16[128,1280]{1,0:T(8,128)(2,1)S(1)}, bf16[128,1280]{1,0:T(8,128)(2,1)S(1)}, u32[]{:S(2)}, u32[]{:S(2)}) collective-permute-start(bf16[128,1280]{1,0:T(8,128)(2,1)S(1)} %pad_maximum_fusion.32.rest_0_), channel_id=1, source_target_pairs={{0,3},{1,2},{2,1},{3,0},{4,7},{5,6},{6,5},{7,4},{8,11},{9,10},{10,... | collective-permute-start | bytes 983048 | tf_op jit(solution)/shard_map/ppermute | solution.py:24
  19.9 32.0 %collective-permute-start.6 = (bf16[1,7,128,256]{3,2,1,0:T(8,128)(2,1)}, bf16[1,7,128,256]{3,2,1,0:T(8,128)(2,1)}, u32[]{:S(2)}, u32[]{:S(2)}) collective-permute-start(bf16[1,7,128,256]{3,2,1,0:T(8,128)(2,1)} %maximum_bitcast_fusion), channel_id=1, source_target_pairs={{0,8},{4,12},{8,0},{12,4},{16,24},{20,28},{24,16},{28,20},{1,9},{5... | collective-permute-start | bytes 1376264 | tf_op jit(solution)/shard_map/ppermute | solution.py:24
  36.6 25.1 %collective-permute-start.7 = (bf16[1,8,128,256]{3,2,1,0:T(8,128)(2,1)}, bf16[1,8,128,256]{3,2,1,0:T(8,128)(2,1)S(1)}, u32[]{:S(2)}, u32[]{:S(2)}) collective-permute-start(bf16[1,8,128,256]{3,2,1,0:T(8,128)(2,1)} %bitcast.464), channel_id=1, source_target_pairs={{0,16},{4,20},{8,24},{12,28},{16,0},{20,4},{24,8},{28,12},{1,17},{... | collective-permute-start | bytes 1572872 | tf_op jit(solution)/shard_map/ppermute | solution.py:24
  63.4 36.6 %collective-permute-start.10 = (bf16[2,7,128,256]{3,2,1,0:T(8,128)(2,1)S(1)}, bf16[2,7,128,256]{3,2,1,0:T(8,128)(2,1)S(1)}, u32[]{:S(2)}, u32[]{:S(2)}) collective-permute-start(bf16[2,7,128,256]{3,2,1,0:T(8,128)(2,1)S(1)} %pad_maximum_fusion.13), channel_id=1, source_target_pairs={{0,16},{4,20},{8,24},{12,28},{16,0},{20,4},{24,8},{28,12},{1,17},{... | collective-permute-start | bytes 2752520 | tf_op jit(solution)/shard_map/ppermute | solution.py:24
  64.8 35.2 %collective-permute-start.11 = (bf16[2,8,128,256]{3,2,1,0:T(8,128)(2,1)S(1)}, bf16[2,8,128,256]{3,2,1,0:T(8,128)(2,1)S(1)}, u32[]{:S(2)}, u32[]{:S(2)}) collective-permute-start(bf16[2,8,128,256]{3,2,1,0:T(8,128)(2,1)S(1)} %pad_maximum_fusion.8), channel_id=1, source_target_pairs={{0,8},{4,12},{8,0},{12,4},{16,24},{20,28},{24,16},{28,20},{1,9},{5... | collective-permute-start | bytes 3145736 | tf_op jit(solution)/shard_map/ppermute | solution.py:24
  65.7 25.9 %collective-permute-start.14 = (bf16[2,128,1792]{2,1,0:T(8,128)(2,1)S(1)}, bf16[2,128,1792]{2,1,0:T(8,128)(2,1)S(1)}, u32[]{:S(2)}, u32[]{:S(2)}) collective-permute-start(bf16[2,128,1792]{2,1,0:T(8,128)(2,1)S(1)} %pad_maximum_fusion.14), channel_id=1, source_target_pairs={{0,1},{1,0},{2,3},{3,2},{4,5},{5,4},{6,7},{7,6},{8,9},{9,8},{10,11... | collective-permute-start | bytes 2752520 | tf_op jit(solution)/shard_map/ppermute | solution.py:24
  113.9 28.5 %collective-permute-start.26 = (bf16[2,512,256]{2,1,0:T(8,128)(2,1)S(1)}, bf16[2,512,256]{2,1,0:T(8,128)(2,1)S(1)}, u32[]{:S(2)}, u32[]{:S(2)}) collective-permute-start(bf16[2,512,256]{2,1,0:T(8,128)(2,1)S(1)} %get-tuple-element.370.w_ref), channel_id=1, source_target_pairs={{0,4},{4,8},{8,12},{12,16},{16,20},{20,24},{24,28},{1,5},{5,9},{9,... | collective-permute-start | bytes 1572872 | tf_op jit(solution)/shard_map/ppermute | solution.py:1186
  115.2 27.2 %collective-permute-start.27 = (bf16[2,512,256]{2,1,0:T(8,128)(2,1)S(1)}, bf16[2,512,256]{2,1,0:T(8,128)(2,1)S(1)}, u32[]{:S(2)}, u32[]{:S(2)}) collective-permute-start(bf16[2,512,256]{2,1,0:T(8,128)(2,1)S(1)} %get-tuple-element.370.w_ref), channel_id=1, source_target_pairs={{4,0},{8,4},{12,8},{16,12},{20,16},{24,20},{28,24},{5,1},{9,5},{13... | collective-permute-start | bytes 1572872 | tf_op jit(solution)/shard_map/ppermute | solution.py:1187
  130.8 32.4 %collective-permute-start.21 = (bf16[1,12,128,256]{3,2,1,0:T(8,128)(2,1)S(1)}, bf16[1,12,128,256]{3,2,1,0:T(8,128)(2,1)S(1)}, u32[]{:S(2)}, u32[]{:S(2)}) collective-permute-start(bf16[1,12,128,256]{3,2,1,0:T(8,128)(2,1)S(1)} %bitcast.458), channel_id=1, source_target_pairs={{0,16},{4,20},{8,24},{12,28},{16,0},{20,4},{24,8},{28,12},{1,17},{... | collective-permute-start | bytes 2359304 | tf_op jit(solution)/shard_map/ppermute | solution.py:24
  163.4 33.5 %collective-permute-start.31 = (bf16[2,12,128,256]{3,2,1,0:T(8,128)(2,1)S(1)}, bf16[2,12,128,256]{3,2,1,0:T(8,128)(2,1)S(1)}, u32[]{:S(2)}, u32[]{:S(2)}) collective-permute-start(bf16[2,12,128,256]{3,2,1,0:T(8,128)(2,1)S(1)} %pad_maximum_fusion.4), channel_id=1, source_target_pairs={{0,8},{4,12},{8,0},{12,4},{16,24},{20,28},{24,16},{28,20},{1,9},{5... | collective-permute-start | bytes 4718600 | tf_op jit(solution)/shard_map/ppermute | solution.py:24
  163.8 28.8 %collective-permute-start.30 = (bf16[2,10,128,256]{3,2,1,0:T(8,128)(2,1)S(1)}, bf16[2,10,128,256]{3,2,1,0:T(8,128)(2,1)S(1)}, u32[]{:S(2)}, u32[]{:S(2)}) collective-permute-start(bf16[2,10,128,256]{3,2,1,0:T(8,128)(2,1)S(1)} %pad_maximum_fusion.5), channel_id=1, source_target_pairs={{0,16},{4,20},{8,24},{12,28},{16,0},{20,4},{24,8},{28,12},{1,17},{... | collective-permute-start | bytes 3932168 | tf_op jit(solution)/shard_map/ppermute | solution.py:24
  165.1 33.0 %collective-permute-start.45 = (bf16[4,4,128,256]{3,2,1,0:T(8,128)(2,1)S(1)}, bf16[4,4,128,256]{3,2,1,0:T(8,128)(2,1)S(1)}, u32[]{:S(2)}, u32[]{:S(2)}) collective-permute-start(bf16[4,4,128,256]{3,2,1,0:T(8,128)(2,1)S(1)} %pad_maximum_fusion.9.refs_0_), channel_id=1, source_target_pairs={{0,4},{4,0},{8,12},{12,8},{16,20},{20,16},{24,28},{28,24},{1,5},{5... | collective-permute-start | bytes 3145736 | tf_op jit(solution)/shard_map/ppermute | solution.py:24
  166.3 73.0 %collective-permute-start.46 = (bf16[4,4,128,256]{3,2,1,0:T(8,128)(2,1)}, bf16[4,4,128,256]{3,2,1,0:T(8,128)(2,1)}, u32[]{:S(2)}, u32[]{:S(2)}) collective-permute-start(bf16[4,4,128,256]{3,2,1,0:T(8,128)(2,1)} %pad_maximum_fusion.10.refs_0_), channel_id=1, source_target_pairs={{0,4},{4,0},{8,12},{12,8},{16,20},{20,16},{24,28},{28,24},{1,5},{5... | collective-permute-start | bytes 3145736 | tf_op jit(solution)/shard_map/ppermute | solution.py:24
  166.8 51.4 %collective-permute-start.47 = (bf16[2,128,1024]{2,1,0:T(8,128)(2,1)}, bf16[2,128,1024]{2,1,0:T(8,128)(2,1)}, u32[]{:S(2)}, u32[]{:S(2)}) collective-permute-start(bf16[2,128,1024]{2,1,0:T(8,128)(2,1)} %param.41), channel_id=1, source_target_pairs={{0,2},{1,3},{2,0},{3,1},{4,6},{5,7},{6,4},{7,5},{8,10},{9,11},{10,... | collective-permute-start | bytes 1572872 | tf_op jit(solution)/shard_map/ppermute | solution.py:24
  362.5 26.2 %collective-permute-start.61 = (bf16[2,128,2048]{2,1,0:T(8,128)(2,1)S(1)}, bf16[2,128,2048]{2,1,0:T(8,128)(2,1)S(1)}, u32[]{:S(2)}, u32[]{:S(2)}) collective-permute-start(bf16[2,128,2048]{2,1,0:T(8,128)(2,1)S(1)} %bitcast.412), channel_id=1, source_target_pairs={{0,8},{4,12},{8,0},{12,4},{16,24},{20,28},{24,16},{28,20},{1,9},{5... | collective-permute-start | bytes 3145736 | tf_op jit(solution)/shard_map/ppermute | solution.py:24
  404.1 32.3 %collective-permute-start.72 = (bf16[6,2,2,128,256]{4,3,2,1,0:T(8,128)(2,1)S(1)}, bf16[6,2,2,128,256]{4,3,2,1,0:T(8,128)(2,1)S(1)}, u32[]{:S(2)}, u32[]{:S(2)}) collective-permute-start(bf16[6,2,2,128,256]{4,3,2,1,0:T(8,128)(2,1)S(1)} %bitcast.406), channel_id=1, source_target_pairs={{0,4},{4,0},{8,12},{12,8},{16,20},{20,16},{24,28},{28,24},{1,5},{5... | collective-permute-start | bytes 4718600 | tf_op jit(solution)/shard_map/ppermute | solution.py:24
  450.1 37.5 %collective-permute-start.82 = (bf16[128,1024]{1,0:T(8,128)(2,1)S(1)}, bf16[128,1024]{1,0:T(8,128)(2,1)S(1)}, u32[]{:S(2)}, u32[]{:S(2)}) collective-permute-start(bf16[128,1024]{1,0:T(8,128)(2,1)S(1)} %get-tuple-element.524.own_ref.e_ref), channel_id=1, source_target_pairs={{0,1},{1,0},{2,3},{3,2},{4,5},{5,4},{6,7},{7,6},{8,9},{9,8},{10,11... | collective-permute-start | bytes 786440 | tf_op jit(solution)/shard_map/ppermute | solution.py:24
  458.8 27.4 %collective-permute-start.81 = (bf16[2,128,1024]{2,1,0:T(8,128)(2,1)S(1)}, bf16[2,128,1024]{2,1,0:T(8,128)(2,1)S(1)}, u32[]{:S(2)}, u32[]{:S(2)}) collective-permute-start(bf16[2,128,1024]{2,1,0:T(8,128)(2,1)S(1)} %fusion.3), channel_id=1, source_target_pairs={{0,2},{1,3},{2,0},{3,1},{4,6},{5,7},{6,4},{7,5},{8,10},{9,11},{10,... | collective-permute-start | bytes 1572872 | tf_op jit(solution)/shard_map/ppermute | solution.py:24
  504.8 25.1 %collective-permute-start.88 = (bf16[2,2,128,2048]{3,2,1,0:T(8,128)(2,1)}, bf16[2,2,128,2048]{3,2,1,0:T(8,128)(2,1)}, u32[]{:S(2)}, u32[]{:S(2)}) collective-permute-start(bf16[2,2,128,2048]{3,2,1,0:T(8,128)(2,1)} %bitcast.146), channel_id=1, source_target_pairs={{0,4},{4,0},{8,12},{12,8},{16,20},{20,16},{24,28},{28,24},{1,5},{5... | collective-permute-start | bytes 6291464 | tf_op jit(solution)/shard_map/ppermute | solution.py:24
  517.9 30.4 %collective-permute-start.90 = (bf16[1,128,1024]{2,1,0:T(8,128)(2,1)S(1)}, bf16[1,128,1024]{2,1,0:T(8,128)(2,1)S(1)}, u32[]{:S(2)}, u32[]{:S(2)}) collective-permute-start(bf16[1,128,1024]{2,1,0:T(8,128)(2,1)S(1)} %fusion.16), channel_id=1, source_target_pairs={{0,2},{1,3},{2,0},{3,1},{4,6},{5,7},{6,4},{7,5},{8,10},{9,11},{10,... | collective-permute-start | bytes 786440 | tf_op jit(solution)/shard_map/ppermute | solution.py:24
  553.5 27.6 %collective-permute-start.92 = (bf16[2,128,2048]{2,1,0:T(8,128)(2,1)S(1)}, bf16[2,128,2048]{2,1,0:T(8,128)(2,1)S(1)}, u32[]{:S(2)}, u32[]{:S(2)}) collective-permute-start(bf16[2,128,2048]{2,1,0:T(8,128)(2,1)S(1)} %bitcast.409), channel_id=1, source_target_pairs={{0,8},{4,12},{8,0},{12,4},{16,24},{20,28},{24,16},{28,20},{1,9},{5... | collective-permute-start | bytes 3145736 | tf_op jit(solution)/shard_map/ppermute | solution.py:24
  557.0 25.4 %collective-permute-start.93 = (bf16[2,128,2048]{2,1,0:T(8,128)(2,1)S(1)}, bf16[2,128,2048]{2,1,0:T(8,128)(2,1)S(1)}, u32[]{:S(2)}, u32[]{:S(2)}) collective-permute-start(bf16[2,128,2048]{2,1,0:T(8,128)(2,1)S(1)} %bitcast.408), channel_id=1, source_target_pairs={{0,16},{4,20},{8,24},{12,28},{16,0},{20,4},{24,8},{28,12},{1,17},{... | collective-permute-start | bytes 3145736 | tf_op jit(solution)/shard_map/ppermute | solution.py:24
  (310 other events, 3991.9 us)
